TPU v7x, 32 devices: a whole 2x2x4 slice. The times are simulated.
32 devices in a mesh: dp: 16 (over z, y, x), mp: 2 (over core).
Axes of the slice: x: 2, y: 2, z: 4, core: 2. Of those that a mesh axis runs over, the one named last changes fastest.
Arguments:
- activations: bfloat16 [8192, 8192], P('dp', 'mp'), may hold values from -6 to 6
- out_grads: bfloat16 [8192, 8192], P('dp', 'mp'), may hold values from -0.09375 to 0.09375
- basis: bfloat16 [8192, 1024], P('mp'), may hold values from -0.0625 to 0.0625
- moment1: float32 [8192, 1024], P(('mp', 'dp')), may hold values from -1.5 to 1.5
- moment2: float32 [8192, 1024], P(('mp', 'dp')), may hold values from 0.0005 to 0.005
Outputs:
- new_first: float32 [8192, 1024], P(('mp', 'dp'))
- new_second: float32 [8192, 1024], P(('mp', 'dp'))
- update: bfloat16 [2, 4096, 8192], P(None, 'dp', 'mp')
All inputs are finite; a program needn't handle non-finite values.
Results may differ from a plain program's by a relative error of at most 0.0055.
Values may be sent and summed in bfloat16 or wider, within the bound.
No kernel may reach another device: no remote copies, remote signals or barrier semaphores. Data moves between devices by JAX's collectives and lax.ppermute only.
A program may use at most 128 MiB of HBM per device.

v0:
```python
import jax
import jax.numpy as jnp
from jax import lax
from jax.sharding import PartitionSpec as P

STEP = 100


beta_first = 0.9
beta_second = 0.999
epsilon = 1e-08


def on_device(activations, out_grads, basis, moment1, moment2):
    partial_rank = jnp.dot(activations, basis, preferred_element_type=jnp.float32)
    token_rank = lax.psum(partial_rank, "mp").astype(jnp.bfloat16)
    reduced = lax.psum_scatter(
        lax.dot_general(
            out_grads, token_rank, (((0,), (0,)), ((), ())), preferred_element_type=jnp.float32
        ),
        "dp",
        scatter_dimension=0,
        tiled=True,
    )
    new_first = beta_first * moment1 + (1.0 - beta_first) * reduced
    new_second = beta_second * moment2 + (1.0 - beta_second) * reduced * reduced
    bias_first = 1.0 - beta_first**STEP
    bias_second = 1.0 - beta_second**STEP
    normed = (new_first / bias_first / (jnp.sqrt(new_second / bias_second) + epsilon)).astype(
        jnp.bfloat16
    )
    gathered = lax.all_gather(normed[None], "mp", axis=0, tiled=True)
    groups, owned, ranks = gathered.shape
    stacked = gathered.reshape(groups * owned, ranks)
    full = lax.dot_general(
        stacked, basis, (((1,), (1,)), ((), ())), preferred_element_type=jnp.float32
    )
    update = full.astype(jnp.bfloat16).reshape(groups, owned, basis.shape[0])
    return (new_first, new_second, update)


def solution(mesh):
    return jax.shard_map(
        on_device,
        mesh=mesh,
        in_specs=(
            P("dp", "mp"),
            P("dp", "mp"),
            P("mp", None),
            P(("mp", "dp"), None),
            P(("mp", "dp"), None),
        ),
        out_specs=(P(("mp", "dp"), None), P(("mp", "dp"), None), P(None, "dp", "mp")),
        check_vma=False,
    )
```

profile of v0, /device:TPU:0, one launch (start us, length us, event | category | flops | bytes accessed | tf_op | source)
XLA Modules:
  0.0 419.0 jit_solution(8831345629814628119)
XLA Ops:
  7.2 0.0 reduce-scatter.2.cloned.1.call-start
  7.2 8.2 %fusion.3 = f32[512,1024]{1,0:T(8,128)S(1)} fusion(bf16[512,4096]{1,0:T(8,128)(2,1)} %param.5, bf16[4096,1024]{1,0:T(8,128)(2,1)} %param.7), kind=kOutput, calls=%fused_computation.7 | convolution fusion | flops 4294967296 | bytes 14680064 | tf_op jit(solution)/shard_map/dot_general | solution.py:15
  15.4 9.3 %all-reduce.1 = bf16[512,1024]{1,0:T(8,128)(2,1)S(1)} all-reduce(f32[512,1024]{1,0:T(8,128)S(1)} %fusion.3), channel_id=1, replica_groups=mesh['dp'=16,'mp'=2] {'mp'}, use_global_device_ids=true, to_apply=%region_0.0 | all-reduce | flops 524288 | bytes 3145728 | tf_op jit(solution)/shard_map/psum | solution.py:16
  24.7 10.3 %convolution_bitcast_fusion = f32[4096,1024]{0,1:T(8,128)} fusion(bf16[512,4096]{1,0:T(8,128)(2,1)} %param.6, bf16[512,1024]{1,0:T(8,128)(2,1)S(1)} %all-reduce.1), kind=kOutput, calls=%fused_computation | convolution fusion | flops 4294967296 | bytes 22020096 | tf_op jit(solution)/shard_map/dot_general | solution.py:18
  35.0 0.0 copy-start
  35.0 0.0 copy-start.1
  35.0 0.0 reduce-scatter.2.cloned.1.call-update
  35.0 0.0 all-gather.3.cloned.1.call-start
  35.1 1.1 copy-done
  36.2 0.3 copy.8
  36.6 0.0 copy-done.1
  36.6 1.3 copy.9
  37.9 346.1 %reduce-scatter.2.cloned.1.call-done = f32[256,1024]{0,1:T(8,128)} async-done(((f32[4096,1024]{0,1:T(8,128)}), f32[256,1024]{0,1:T(8,128)}) %reduce-scatter.2.cloned.1.call-update) | async-done | bytes 1048592 | tf_op jit(solution)/shard_map/reduce_scatter | solution.py:17
  384.0 3.1 divide_convert_fusion
  387.1 0.0 all-gather.3.cloned.1.call-update
  387.1 1.3 copy.10
  388.4 1.3 copy.11
  389.7 12.1 %all-gather.3.cloned.1.call-done = bf16[512,1024]{0,1:T(8,128)(2,1)} async-done(((bf16[256,1024]{0,1:T(8,128)(2,1)}), bf16[512,1024]{0,1:T(8,128)(2,1)}) %all-gather.3.cloned.1.call-update) | async-done | bytes 1048592 | tf_op jit(solution)/shard_map/all_gather | solution.py:32
  401.8 10.3 %convolution_convert_fusion = bf16[512,4096]{1,0:T(8,128)(2,1)} fusion(bf16[512,1024]{0,1:T(8,128)(2,1)} %all-gather.3.cloned.1.call-done, bf16[4096,1024]{1,0:T(8,128)(2,1)} %param.7), kind=kOutput, calls=%fused_computation.1 | convolution fusion | flops 4297064448 | bytes 13631488 | tf_op jit(solution)/shard_map/dot_general | solution.py:35
Async XLA Ops:
  7.2 376.8 %reduce-scatter.2.cloned.1.call-start = ((), (), s32[]{:S(2)}) async-start(), calls=%async_computation.1 | async-start | bytes 17825792 | tf_op jit(solution)/shard_map/reduce_scatter | solution.py:17
  35.0 1.2 copy-start
  35.0 1.6 copy-start.1
  35.0 366.8 %all-gather.3.cloned.1.call-start = ((), (), s32[]{:S(2)}) async-start(), calls=%async_computation.2 | async-start | bytes 1572864 | tf_op jit(solution)/shard_map/all_gather | solution.py:32
Sparse Core Ops, SparseCore 0:
  35.1 348.7 reduce-scatter.1
  387.2 14.5 all-gather.2
where the time goes:
time: 419 us
  waiting for transfers between devices  358 us (85%)
  matrix products  28.8 us (7%)
  between operations  14.1 us (3%)
  blocking collectives  9.29 us (2%)
  local copies, waits for them, and re-layouts  5.4 us (1%)
    reduce_scatter x1, waiting for transfers between devices, on_device(): lax.psum_scatter(lax.dot_general(out_grads, token_rank, (((0,), (0,)), ((...  346 us
    all_gather x1, waiting for transfers between devices, on_device(): gathered = lax.all_gather(normed[None], 'mp', axis=0, tiled=True)  12.1 us
    dot_general x1, matrix products, on_device(): lax.dot_general(out_grads, token_rank, (((0,), (0,)), ((), ())), preferre...  10.3 us
    dot_general x1, matrix products, on_device(): lax.dot_general(stacked, basis, (((1,), (1,)), ((), ())), preferred_eleme...  10.3 us
    psum x1, blocking collectives, on_device(): token_rank = lax.psum(partial_rank, 'mp').astype(jnp.bfloat16)  9.29 us
  transfers between devices with their start and end apart: 2, of which 2 were waited for; matrix products, arithmetic and copies ran while one was open for 1% of the time, Pallas kernels for 0%

commit v1 on v0

v1 whole, which is shorter than its diff:
```python
import jax
import jax.numpy as jnp
import numpy as np
from jax import lax
from jax.experimental import pallas as pl
from jax.experimental.pallas import tpu as pltpu
from jax.sharding import PartitionSpec as P

STEP = 100


beta_first = 0.9
beta_second = 0.999
epsilon = 1e-08

VMEM_LIMIT = 48 * 1024 * 1024


def adam(reduced, moment1, moment2):
    new_first = beta_first * moment1 + (1.0 - beta_first) * reduced
    new_second = beta_second * moment2 + (1.0 - beta_second) * reduced * reduced
    bias_first = 1.0 - beta_first**STEP
    bias_second = 1.0 - beta_second**STEP
    normed = (new_first / bias_first / (jnp.sqrt(new_second / bias_second) + epsilon)).astype(
        jnp.bfloat16
    )
    return new_first, new_second, normed


def plain(activations, out_grads, basis, moment1, moment2):
    partial_rank = jnp.dot(activations, basis, preferred_element_type=jnp.float32)
    token_rank = lax.psum(partial_rank, "mp").astype(jnp.bfloat16)
    reduced = lax.psum_scatter(
        lax.dot_general(
            out_grads, token_rank, (((0,), (0,)), ((), ())), preferred_element_type=jnp.float32
        ),
        "dp",
        scatter_dimension=0,
        tiled=True,
    )
    new_first, new_second, normed = adam(reduced, moment1, moment2)
    gathered = lax.all_gather(normed[None], "mp", axis=0, tiled=True)
    groups, owned, ranks = gathered.shape
    full = lax.dot_general(
        gathered.reshape(groups * owned, ranks),
        basis,
        (((1,), (1,)), ((), ())),
        preferred_element_type=jnp.float32,
    )
    return new_first, new_second, full.astype(jnp.bfloat16).reshape(groups, owned, basis.shape[0])


def params(**more):
    return pltpu.CompilerParams(vmem_limit_bytes=VMEM_LIMIT, **more)


def rank_half(half, activations, basis, steps=4):
    tokens, depth = activations.shape
    ranks = basis.shape[1]
    rows, tile = tokens // 2, depth // steps

    def kernel(half_ref, a_ref, b_ref, o_ref):
        part = jnp.dot(a_ref[...], b_ref[...], preferred_element_type=jnp.float32)

        @pl.when(pl.program_id(0) == 0)
        def _():
            o_ref[...] = part

        @pl.when(pl.program_id(0) > 0)
        def _():
            o_ref[...] += part

    return pl.pallas_call(
        kernel,
        out_shape=jax.ShapeDtypeStruct((rows, ranks), jnp.float32),
        grid_spec=pltpu.PrefetchScalarGridSpec(
            num_scalar_prefetch=1,
            grid=(steps,),
            in_specs=[
                pl.BlockSpec((rows, tile), lambda k, h: (h[0], k)),
                pl.BlockSpec((tile, ranks), lambda k, h: (k, 0)),
            ],
            out_specs=pl.BlockSpec((rows, ranks), lambda k, h: (0, 0)),
        ),
        compiler_params=params(),
        cost_estimate=pl.CostEstimate(
            flops=2 * rows * depth * ranks,
            bytes_accessed=2 * (rows * depth + depth * ranks) + 4 * rows * ranks,
            transcendentals=0,
        ),
        name="rank_half",
    )(half, activations, basis)


def partial_sums(place, grads, grads_got, rank_own, rank_got):
    tokens, ranks = rank_own.shape
    owned = grads_got.shape[1] // 2

    def kernel(place_ref, g_ref, got_ref, t_ref, u_ref, send_ref, keep_ref):
        dims = (((0,), (0,)), ((), ()))
        total = lax.dot_general(
            g_ref[...], t_ref[...], dims, preferred_element_type=jnp.float32
        ) + lax.dot_general(got_ref[...], u_ref[...], dims, preferred_element_type=jnp.float32)

        @pl.when(pl.program_id(0) == 0)
        def _():
            send_ref[...] = total.astype(send_ref.dtype)

        @pl.when(pl.program_id(0) == 1)
        def _():
            keep_ref[...] = total

    def side(i, p):
        return lax.rem(p[1] + 1 + i, 2)

    whole = pl.BlockSpec((tokens, ranks), lambda i, p: (0, 0))
    return pl.pallas_call(
        kernel,
        out_shape=(
            jax.ShapeDtypeStruct((owned, ranks), jnp.bfloat16),
            jax.ShapeDtypeStruct((owned, ranks), jnp.float32),
        ),
        grid_spec=pltpu.PrefetchScalarGridSpec(
            num_scalar_prefetch=1,
            grid=(2,),
            in_specs=[
                pl.BlockSpec((tokens, owned), lambda i, p: (0, p[0] + side(i, p))),
                pl.BlockSpec((tokens, owned), lambda i, p: (0, side(i, p))),
                whole,
                whole,
            ],
            out_specs=(
                pl.BlockSpec((owned, ranks), lambda i, p: (0, 0)),
                pl.BlockSpec((owned, ranks), lambda i, p: (0, 0)),
            ),
        ),
        compiler_params=params(),
        cost_estimate=pl.CostEstimate(
            flops=2 * 2 * tokens * 2 * owned * ranks,
            bytes_accessed=2 * 2 * tokens * (2 * owned + ranks) + 6 * owned * ranks,
            transcendentals=0,
        ),
        name="partial_sums",
    )(place, grads, grads_got, rank_own, rank_got)


def update_rows(group, normed, basis, groups, before=None, steps=4):
    owned, ranks = normed.shape
    width = basis.shape[0]
    tile = width // steps

    def kernel(group_ref, n_ref, b_ref, *refs):
        refs[-1][0] = lax.dot_general(
            n_ref[...], b_ref[...], (((1,), (1,)), ((), ())), preferred_element_type=jnp.float32
        ).astype(jnp.bfloat16)

    more = () if before is None else (before,)
    return pl.pallas_call(
        kernel,
        out_shape=jax.ShapeDtypeStruct((groups, owned, width), jnp.bfloat16),
        grid_spec=pltpu.PrefetchScalarGridSpec(
            num_scalar_prefetch=1,
            grid=(steps,),
            in_specs=[
                pl.BlockSpec((owned, ranks), lambda n, g: (0, 0)),
                pl.BlockSpec((tile, ranks), lambda n, g: (n, 0)),
            ]
            + [pl.BlockSpec(memory_space=pl.ANY) for _ in more],
            out_specs=pl.BlockSpec((1, owned, tile), lambda n, g: (g[0], 0, n)),
        ),
        input_output_aliases={3: 0} if more else {},
        compiler_params=params(),
        cost_estimate=pl.CostEstimate(
            flops=2 * owned * ranks * width,
            bytes_accessed=2 * (owned * ranks + width * ranks + owned * width),
            transcendentals=0,
        ),
        name="update_rows",
    )(group, normed, basis, *more)


def staged(activations, out_grads, basis, moment1, moment2):
    shards = lax.axis_size("dp")
    planes = shards // 4
    owned = moment1.shape[0]
    me, core = lax.axis_index("dp"), lax.axis_index("mp")
    z, y, x = me // 4, me // 2 % 2, me % 2

    along_y = [(i, i ^ 2) for i in range(shards)]
    along_x = [(i, i ^ 1) for i in range(shards)]
    last = planes - 1
    outer = [(0, 1), (last, last - 1)]
    inner = [(1, 2), (2, 1)]
    to_end = [(1, 0), (2, last)]
    outer, inner, to_end = (
        [(4 * a + k, 4 * b + k) for a, b in hops for k in range(4)] for hops in (outer, inner, to_end)
    )
    cores = [(0, 1), (1, 0)]

    order = np.array(
        [
            sorted(
                range(planes),
                key=lambda d, p=p: (d == p, -abs(d - p), (d < p) == (p < planes // 2)),
            )
            for p in range(planes)
        ],
        np.int32,
    )
    blocks = jnp.asarray(order)[z]

    wide = 2 * owned
    got = []
    for c in range(planes):
        mine = lax.dynamic_slice_in_dim(out_grads, (blocks[c] * 4 + (1 - y) * 2) * owned, wide, 1)
        got.append(lax.ppermute(mine, "dp", along_y))

    other = rank_half((1 - core)[None].astype(jnp.int32), activations, basis)
    arrived = lax.ppermute(other, "mp", cores)
    own = rank_half(core[None].astype(jnp.int32), activations, basis)
    half = (own + arrived).astype(jnp.bfloat16)
    half_far = lax.ppermute(half, "dp", along_y)
    half_other = lax.ppermute(half, "mp", cores)
    half_far_other = lax.ppermute(half_far, "mp", cores)

    def joined(a, b):
        first = core == 0
        return jnp.concatenate([jnp.where(first, a, b), jnp.where(first, b, a)])

    rank_own, rank_got = joined(half, half_other), joined(half_far, half_far_other)

    sums = []
    for c in range(planes):
        place = jnp.stack([blocks[c] * 4 + y * 2, x]).astype(jnp.int32)
        send, keep = partial_sums(place, out_grads, got[c], rank_own, rank_got)
        sums.append(keep + lax.ppermute(send, "dp", along_x).astype(jnp.float32))

    def hop(value, pairs):
        return lax.ppermute(value.astype(jnp.bfloat16), "dp", pairs).astype(jnp.float32)

    first, second, third, final = sums
    out1 = hop(first, outer)
    out2 = hop(second, outer)
    in2 = hop(first + out1, inner)
    out3 = hop(third, outer)
    in3 = hop(second + out2, inner)
    end3 = hop(third + in2, to_end)
    reduced = final + out3 + in3 + end3

    new_first, new_second, normed = adam(reduced, moment1, moment2)
    normed_other = lax.ppermute(normed, "mp", cores)
    update = update_rows(core[None].astype(jnp.int32), normed, basis, 2)
    update = update_rows((1 - core)[None].astype(jnp.int32), normed_other, basis, 2, update)
    return new_first, new_second, update


def solution(mesh):
    fits = mesh.shape["mp"] == 2 and mesh.shape["dp"] == 16
    return jax.shard_map(
        staged if fits else plain,
        mesh=mesh,
        in_specs=(
            P("dp", "mp"),
            P("dp", "mp"),
            P("mp", None),
            P(("mp", "dp"), None),
            P(("mp", "dp"), None),
        ),
        out_specs=(P(("mp", "dp"), None), P(("mp", "dp"), None), P(None, "dp", "mp")),
        check_vma=False,
    )
```

time: 419 us -> 146 us (0.35)
  waiting for transfers between devices: 358 us -> 52.3 us
  Pallas kernels: 0 us -> 40.1 us
  matrix products: 28.8 us -> 0 us
  starting transfers between devices: 0.08 us -> 27.3 us
  between operations: 14.1 us -> 3.33 us
  other arithmetic: 3.08 us -> 12.6 us
  blocking collectives: 9.29 us -> 0 us
    reduce_scatter x1 -> x0, waiting for transfers between devices: 346 us -> none  [on_device(): lax.psum_scatter(lax.dot_general(out_grads, token_rank, (((0,), (0,)), ((...]
    ppermute x0 -> x19, waiting for transfers between devices: none -> 52.3 us  [the longest x4 23.3 us: staged(): got.append(lax.ppermute(mine, 'dp', along_y))]
    pallas_call x0 -> x8, Pallas kernels: none -> 40.1 us  [the longest x4 15.1 us: partial_sums(): pl.pallas_call(kernel, out_shape=(jax.ShapeDtypeStruct((owned, ranks), jn...]
    dot_general x3 -> x0, matrix products: 28.8 us -> none  [the longest x1 10.3 us: on_device(): lax.dot_general(out_grads, token_rank, (((0,), (0,)), ((), ())), preferre...]
    ppermute x0 -> x19, starting transfers between devices: none -> 27.3 us  [the longest x6 14.5 us: hop(): lax.ppermute(value.astype(jnp.bfloat16), 'dp', pairs).astype(jnp.float32)]
    all_gather x1 -> x0, waiting for transfers between devices: 12.1 us -> none  [on_device(): gathered = lax.all_gather(normed[None], 'mp', axis=0, tiled=True)]
    psum x1 -> x0, blocking collectives: 9.29 us -> none  [on_device(): token_rank = lax.psum(partial_rank, 'mp').astype(jnp.bfloat16)]
    convert_element_type x1 -> x7, other arithmetic: 3.08 us -> 12 us  [the longest x5 9.52 us: hop(): value.astype(jnp.bfloat16)]
  transfers between devices with their start and end apart: 2 -> 19, of which waited for: 2 -> 8; matrix products, arithmetic and copies ran while one was open for 1% -> 10% of each run, Pallas kernels for 0% -> 19%
where the time goes in v1:
time: 146 us; the launch traced here: 145 us
  waiting for transfers between devices  52.3 us (36%)
  Pallas kernels  40.1 us (27%)
  starting transfers between devices  27.3 us (19%)
  other arithmetic  12.6 us (9%)
  local copies, waits for them, and re-layouts  9.17 us (6%)
  between operations  3.33 us (2%)
    ppermute x4, waiting for transfers between devices, staged(): got.append(lax.ppermute(mine, 'dp', along_y))  23.3 us
    pallas_call x4, Pallas kernels, partial_sums(): pl.pallas_call(kernel, out_shape=(jax.ShapeDtypeStruct((owned, ranks), jn...  15.1 us
    ppermute x6, starting transfers between devices, hop(): lax.ppermute(value.astype(jnp.bfloat16), 'dp', pairs).astype(jnp.float32)  14.5 us
    pallas_call x2, Pallas kernels, update_rows(): pl.pallas_call(kernel, out_shape=jax.ShapeDtypeStruct((groups, owned, wid...  13.2 us
    pallas_call x2, Pallas kernels, rank_half(): pl.pallas_call(kernel, out_shape=jax.ShapeDtypeStruct((rows, ranks), jnp....  11.9 us
    ppermute x4, waiting for transfers between devices, staged(): sums.append(keep + lax.ppermute(send, 'dp', along_x).astype(jnp.float32))  10.2 us
    ppermute x6, waiting for transfers between devices, hop(): lax.ppermute(value.astype(jnp.bfloat16), 'dp', pairs).astype(jnp.float32)  10.2 us
    convert_element_type x5, other arithmetic, hop(): value.astype(jnp.bfloat16)  9.52 us
  transfers between devices with their start and end apart: 19, of which 8 were waited for; matrix products, arithmetic and copies ran while one was open for 10% of the time, Pallas kernels for 19%

profile of v1, /device:TPU:0, one launch (start us, length us, event | category | flops | bytes accessed | tf_op | source)
XLA Modules:
  0.0 144.8 jit_solution(15835004205411473477)
XLA Ops:
  0.6 2.2 %copy-done = bf16[512,4096]{1,0:T(8,128)(2,1)S(1)} copy-done((bf16[512,4096]{1,0:T(8,128)(2,1)S(1)}, bf16[512,4096]{1,0:T(8,128)(2,1)}, u32[]{:S(2)}) %copy-start) | copy-done | bytes 4194328
  2.8 6.0 %rank_half.3 = f32[256,1024]{1,0:T(8,128)S(1)} custom-call(s32[1]{0:T(128)} %bitcast.4.half_ref.group_ref, bf16[512,4096]{1,0:T(8,128)(2,1)S(1)} %copy-done, bf16[4096,1024]{1,0:T(8,128)(2,1)} %b_ref.7), custom_call_target="tpu_custom_call" | custom-call | flops 2147483648 | bytes 11534336 | tf_op jit(solution)/shard_map/rank_half/pallas_call | solution.py:73
  9.4 5.9 %rank_half.2 = f32[256,1024]{1,0:T(8,128)S(1)} custom-call(s32[1]{0:T(128)} %bitcast.3.half_ref.group_ref, bf16[512,4096]{1,0:T(8,128)(2,1)S(1)} %copy-done.1, bf16[4096,1024]{1,0:T(8,128)(2,1)} %b_ref.7), custom_call_target="tpu_custom_call" | custom-call | flops 2147483648 | bytes 11534336 | tf_op jit(solution)/shard_map/rank_half/pallas_call | solution.py:73
  15.4 2.6 %collective-permute-start.3 = (bf16[256,1024]{1,0:T(8,128)(2,1)S(1)}, bf16[256,1024]{1,0:T(8,128)(2,1)S(1)}, u32[]{:S(2)}, u32[]{:S(2)}) collective-permute-start(bf16[256,1024]{1,0:T(8,128)(2,1)S(1)} %add_convert_fusion.3), channel_id=1, source_target_pairs={{0,4},{2,6},{4,0},{6,2},{8,12},{10,14},{12,8},{14,10},{16,20},{18,... | collective-permute-start | bytes 1572872 | tf_op jit(solution)/shard_map/ppermute | solution.py:222
  22.1 8.6 %collective-permute-done.3 = bf16[256,1024]{1,0:T(8,128)(2,1)S(1)} collective-permute-done((bf16[256,1024]{1,0:T(8,128)(2,1)S(1)}, bf16[256,1024]{1,0:T(8,128)(2,1)S(1)}, u32[]{:S(2)}, u32[]{:S(2)}) %collective-permute-start.3) | collective-permute-done | bytes 524320 | tf_op jit(solution)/shard_map/ppermute | solution.py:222
  30.6 2.9 %constant_dynamic-slice_fusion.3 = (bf16[512,512]{1,0:T(8,128)(2,1)}, bf16[512,512]{1,0:T(8,128)(2,1)}, bf16[512,512]{1,0:T(8,128)(2,1)}, bf16[512,512]{1,0:T(8,128)(2,1)}) fusion(bf16[512,4096]{1,0:T(8,128)(2,1)} %g_ref.7, s32[]{:T(128)S(6)} %select_n.58, s32[]{:T(128)S(6)} %select_n.65, s32[]{:T(128)S(6)} %select_n.64, s32[]{:T(128)S(6)} %select_n.66), kind=kLoop, calls=%fused_computation.24 | loop fusion | bytes 4194320 | tf_op jit(solution)/shard_map/dynamic_slice | solution.py:215
  35.9 23.3 %collective-permute-done.13.got_ref = bf16[512,512]{1,0:T(8,128)(2,1)S(1)} collective-permute-done((bf16[512,512]{1,0:T(8,128)(2,1)}, bf16[512,512]{1,0:T(8,128)(2,1)S(1)}, u32[]{:S(2)}, u32[]{:S(2)}) %collective-permute-start.13) | collective-permute-done | bytes 524320 | tf_op jit(solution)/shard_map/ppermute | solution.py:216
  59.3 3.9 %partial_sums.7 = (bf16[256,1024]{1,0:T(8,128)(2,1)}, f32[256,1024]{1,0:T(8,128)S(1)}) custom-call(s32[2]{0:T(128)S(1)} %pad_add_fusion.3.place_ref, bf16[512,4096]{1,0:T(8,128)(2,1)} %g_ref.7, bf16[512,512]{1,0:T(8,128)(2,1)S(1)} %collective-permute-done.13.got_ref, bf16[512,1024]{1,0:T(8,128)(2,1)S(1)} %get-tuple-element.36.t_ref, ...), custom_call_target="tpu_custom_call" | custom-call | flops 1073741824 | bytes 4718592 | tf_op jit(solution)/shard_map/partial_sums/pallas_call | solution.py:117
  69.3 3.9 %partial_sums.6 = (bf16[256,1024]{1,0:T(8,128)(2,1)}, f32[256,1024]{1,0:T(8,128)S(1)}) custom-call(s32[2]{0:T(128)S(1)} %pad_add_fusion.2.place_ref, bf16[512,4096]{1,0:T(8,128)(2,1)} %g_ref.7, bf16[512,512]{1,0:T(8,128)(2,1)S(1)} %copy-done.8, bf16[512,1024]{1,0:T(8,128)(2,1)S(1)} %get-tuple-element.36.t_ref, bf16[512,1024]{1,0:T(8,128)(2,1)S(1)} %get-tuple-element.37.u_ref), custom_call_target="tpu_custom_call" | custom-call | flops 1073741824 | bytes 4718592 | tf_op jit(solution)/shard_map/partial_sums/pallas_call | solution.py:117
  73.8 5.5 %collective-permute-done.14 = bf16[256,1024]{1,0:T(8,128)(2,1)} collective-permute-done((bf16[256,1024]{1,0:T(8,128)(2,1)}, bf16[256,1024]{1,0:T(8,128)(2,1)}, u32[]{:S(2)}, u32[]{:S(2)}) %collective-permute-start.14) | collective-permute-done | bytes 524320 | tf_op jit(solution)/shard_map/ppermute | solution.py:236
  79.3 2.0 %fusion.3 = bf16[256,1024]{1,0:T(8,128)(2,1)} fusion(f32[256,1024]{1,0:T(8,128)S(1)} %copy-done.3, bf16[256,1024]{1,0:T(8,128)(2,1)} %collective-permute-done.14), kind=kLoop, calls=%fused_computation.16 | loop fusion | flops 786432 | bytes 2097152 | tf_op jit(solution)/shard_map/convert_element_type | solution.py:239
  81.3 4.5 %collective-permute-start.15 = (bf16[256,1024]{1,0:T(8,128)(2,1)}, bf16[256,1024]{1,0:T(8,128)(2,1)}, u32[]{:S(2)}, u32[]{:S(2)}) collective-permute-start(bf16[256,1024]{1,0:T(8,128)(2,1)} %fusion.3), channel_id=1, source_target_pairs={{0,8},{2,10},{4,12},{6,14},{24,16},{26,18},{28,20},{30,22},{1,9},{... | collective-permute-start | bytes 1572872 | tf_op jit(solution)/shard_map/ppermute | solution.py:239
  87.4 4.0 %partial_sums.5 = (bf16[256,1024]{1,0:T(8,128)(2,1)}, f32[256,1024]{1,0:T(8,128)S(1)}) custom-call(s32[2]{0:T(128)S(1)} %pad_add_fusion.1.place_ref, bf16[512,4096]{1,0:T(8,128)(2,1)} %g_ref.7, bf16[512,512]{1,0:T(8,128)(2,1)} %collective-permute-done.6.got_ref, bf16[512,1024]{1,0:T(8,128)(2,1)S(1)} %get-tuple-element.36.t_ref, ...), custom_call_target="tpu_custom_call" | custom-call | flops 1073741824 | bytes 4718592 | tf_op jit(solution)/shard_map/partial_sums/pallas_call | solution.py:117
  91.4 2.4 %fusion.2 = bf16[256,1024]{1,0:T(8,128)(2,1)} fusion(f32[256,1024]{1,0:T(8,128)S(1)} %get-tuple-element.15, bf16[256,1024]{1,0:T(8,128)(2,1)} %collective-permute-done.10), kind=kLoop, calls=%fused_computation.15 | loop fusion | flops 786432 | bytes 2097152 | tf_op jit(solution)/shard_map/convert_element_type | solution.py:239
  93.8 2.1 %collective-permute-start.11 = (bf16[256,1024]{1,0:T(8,128)(2,1)}, bf16[256,1024]{1,0:T(8,128)(2,1)}, u32[]{:S(2)}, u32[]{:S(2)}) collective-permute-start(bf16[256,1024]{1,0:T(8,128)(2,1)} %fusion.2), channel_id=1, source_target_pairs={{0,8},{2,10},{4,12},{6,14},{24,16},{26,18},{28,20},{30,22},{1,9},{... | collective-permute-start | bytes 1572872 | tf_op jit(solution)/shard_map/ppermute | solution.py:239
  97.3 2.2 %add_convert_fusion.1 = bf16[256,1024]{1,0:T(8,128)(2,1)} fusion(bf16[256,1024]{1,0:T(8,128)(2,1)} %collective-permute-done.15, f32[256,1024]{1,0:T(8,128)S(1)} %copy-done.4, bf16[256,1024]{1,0:T(8,128)(2,1)} %collective-permute-done.14), kind=kLoop, calls=%fused_computation.8 | loop fusion | flops 1310720 | bytes 2621440 | tf_op jit(solution)/shard_map/convert_element_type | solution.py:239
  101.1 3.2 %partial_sums.4 = (bf16[256,1024]{1,0:T(8,128)(2,1)S(1)}, f32[256,1024]{1,0:T(8,128)S(1)}) custom-call(s32[2]{0:T(128)S(1)} %pad_add_fusion.place_ref, bf16[512,4096]{1,0:T(8,128)(2,1)} %g_ref.7, bf16[512,512]{1,0:T(8,128)(2,1)} %collective-permute-done.got_ref, bf16[512,1024]{1,0:T(8,128)(2,1)S(1)} %get-tuple-element.36.t_ref, ...), custom_call_target="tpu_custom_call" | custom-call | flops 1073741824 | bytes 4718592 | tf_op jit(solution)/shard_map/partial_sums/pallas_call | solution.py:117
  107.6 3.4 %collective-permute-done.7 = bf16[256,1024]{1,0:T(8,128)(2,1)} collective-permute-done((bf16[256,1024]{1,0:T(8,128)(2,1)}, bf16[256,1024]{1,0:T(8,128)(2,1)}, u32[]{:S(2)}, u32[]{:S(2)}) %collective-permute-start.7) | collective-permute-done | bytes 524320 | tf_op jit(solution)/shard_map/ppermute | solution.py:236
  112.5 4.5 %collective-permute-start.8 = (bf16[256,1024]{1,0:T(8,128)(2,1)S(1)}, bf16[256,1024]{1,0:T(8,128)(2,1)S(1)}, u32[]{:S(2)}, u32[]{:S(2)}) collective-permute-start(bf16[256,1024]{1,0:T(8,128)(2,1)S(1)} %get-tuple-element.26), channel_id=1, source_target_pairs={{0,8},{2,10},{4,12},{6,14},{24,16},{26,18},{28,20},{30,22},{1,9},{... | collective-permute-start | bytes 1572872 | tf_op jit(solution)/shard_map/ppermute | solution.py:239
  119.6 5.6 %collective-permute-done.8 = bf16[256,1024]{1,0:T(8,128)(2,1)S(1)} collective-permute-done((bf16[256,1024]{1,0:T(8,128)(2,1)S(1)}, bf16[256,1024]{1,0:T(8,128)(2,1)S(1)}, u32[]{:S(2)}, u32[]{:S(2)}) %collective-permute-start.8) | collective-permute-done | bytes 524320 | tf_op jit(solution)/shard_map/ppermute | solution.py:239
  125.2 4.1 %collective-permute-done.17 = bf16[256,1024]{1,0:T(8,128)(2,1)S(1)} collective-permute-done((bf16[256,1024]{1,0:T(8,128)(2,1)S(1)}, bf16[256,1024]{1,0:T(8,128)(2,1)S(1)}, u32[]{:S(2)}, u32[]{:S(2)}) %collective-permute-start.17) | collective-permute-done | bytes 524320 | tf_op jit(solution)/shard_map/ppermute | solution.py:239
  129.3 2.3 %divide_convert_fusion = (bf16[256,1024]{1,0:T(8,128)(2,1)S(1)}, f32[256,1024]{1,0:T(8,128)}, f32[256,1024]{1,0:T(8,128)}) fusion(bf16[256,1024]{1,0:T(8,128)(2,1)S(1)} %collective-permute-done.17, bf16[256,1024]{1,0:T(8,128)(2,1)S(1)} %collective-permute-done.12, bf16[256,1024]{1,0:T(8,128)(2,1)S(1)} %collective-permute-done.8, ...), kind=kLoop, calls=%fused_computation.4 | loop fusion | flops 5242880 | bytes 7864320 | tf_op jit(solution)/shard_map/convert_element_type | solution.py:24
  131.6 6.6 %update_rows.2.refs_0_ = bf16[2,256,4096]{2,1,0:T(8,128)(2,1)} custom-call(s32[1]{0:T(128)} %bitcast.3.half_ref.group_ref, bf16[256,1024]{1,0:T(8,128)(2,1)S(1)} %get-tuple-element.19.n_ref, bf16[4096,1024]{1,0:T(8,128)(2,1)} %b_ref.7), custom_call_target="tpu_custom_call" | custom-call | flops 2147483648 | bytes 11010048 | tf_op jit(solution)/shard_map/update_rows/pallas_call | solution.py:158
  138.2 6.6 %update_rows.3 = bf16[2,256,4096]{2,1,0:T(8,128)(2,1)} custom-call(s32[1]{0:T(128)} %bitcast.4.half_ref.group_ref, bf16[256,1024]{1,0:T(8,128)(2,1)S(1)} %collective-permute-done.18.n_ref, bf16[4096,1024]{1,0:T(8,128)(2,1)} %b_ref.7, bf16[2,256,4096]{2,1,0:T(8,128)(2,1)} %update_rows.2.refs_0_), custom_call_target="tpu_custom_call", output_to_operand_aliasing={{}: (3, {})} | custom-call | flops 2147483648 | bytes 11010048 | tf_op jit(solution)/shard_map/update_rows/pallas_call | solution.py:158
  (61 shorter events, 23.2 us)
Async XLA Ops:
  8.8 6.4 %collective-permute-start.1 = (f32[256,1024]{1,0:T(8,128)S(1)}, f32[256,1024]{1,0:T(8,128)S(1)}, u32[]{:S(2)}, u32[]{:S(2)}) collective-permute-start(f32[256,1024]{1,0:T(8,128)S(1)} %rank_half.3), channel_id=1, source_target_pairs={{0,1},{1,0},{2,3},{3,2},{4,5},{5,4},{6,7},{7,6},{8,9},{9,8},{10,11... | collective-permute-start | bytes 3145736 | tf_op jit(solution)/shard_map/ppermute | solution.py:219
  15.4 15.2 %collective-permute-start.3 = (bf16[256,1024]{1,0:T(8,128)(2,1)S(1)}, bf16[256,1024]{1,0:T(8,128)(2,1)S(1)}, u32[]{:S(2)}, u32[]{:S(2)}) collective-permute-start(bf16[256,1024]{1,0:T(8,128)(2,1)S(1)} %add_convert_fusion.3), channel_id=1, source_target_pairs={{0,4},{2,6},{4,0},{6,2},{8,12},{10,14},{12,8},{14,10},{16,20},{18,... | collective-permute-start | bytes 1572872 | tf_op jit(solution)/shard_map/ppermute | solution.py:222
  18.0 17.5 %collective-permute-start.2 = (bf16[256,1024]{1,0:T(8,128)(2,1)S(1)}, bf16[256,1024]{1,0:T(8,128)(2,1)S(1)}, u32[]{:S(2)}, u32[]{:S(2)}) collective-permute-start(bf16[256,1024]{1,0:T(8,128)(2,1)S(1)} %add_convert_fusion.3), channel_id=1, source_target_pairs={{0,1},{1,0},{2,3},{3,2},{4,5},{5,4},{6,7},{7,6},{8,9},{9,8},{10,11... | collective-permute-start | bytes 1572872 | tf_op jit(solution)/shard_map/ppermute | solution.py:223
  30.6 5.1 %collective-permute-start.4 = (bf16[256,1024]{1,0:T(8,128)(2,1)S(1)}, bf16[256,1024]{1,0:T(8,128)(2,1)S(1)}, u32[]{:S(2)}, u32[]{:S(2)}) collective-permute-start(bf16[256,1024]{1,0:T(8,128)(2,1)S(1)} %collective-permute-done.3), channel_id=1, source_target_pairs={{0,1},{1,0},{2,3},{3,2},{4,5},{5,4},{6,7},{7,6},{8,9},{9,8},{10,11... | collective-permute-start | bytes 1572872 | tf_op jit(solution)/shard_map/ppermute | solution.py:224
  33.5 34.0 %collective-permute-start.9 = (bf16[512,512]{1,0:T(8,128)(2,1)}, bf16[512,512]{1,0:T(8,128)(2,1)S(1)}, u32[]{:S(2)}, u32[]{:S(2)}) collective-permute-start(bf16[512,512]{1,0:T(8,128)(2,1)} %get-tuple-element.23), channel_id=1, source_target_pairs={{0,4},{2,6},{4,0},{6,2},{8,12},{10,14},{12,8},{14,10},{16,20},{18,... | collective-permute-start | bytes 1572872 | tf_op jit(solution)/shard_map/ppermute | solution.py:216
  35.2 24.0 %collective-permute-start.13 = (bf16[512,512]{1,0:T(8,128)(2,1)}, bf16[512,512]{1,0:T(8,128)(2,1)S(1)}, u32[]{:S(2)}, u32[]{:S(2)}) collective-permute-start(bf16[512,512]{1,0:T(8,128)(2,1)} %get-tuple-element.25), channel_id=1, source_target_pairs={{0,4},{2,6},{4,0},{6,2},{8,12},{10,14},{12,8},{14,10},{16,20},{18,... | collective-permute-start | bytes 1572872 | tf_op jit(solution)/shard_map/ppermute | solution.py:216
  64.2 15.1 %collective-permute-start.14 = (bf16[256,1024]{1,0:T(8,128)(2,1)}, bf16[256,1024]{1,0:T(8,128)(2,1)}, u32[]{:S(2)}, u32[]{:S(2)}) collective-permute-start(bf16[256,1024]{1,0:T(8,128)(2,1)} %get-tuple-element.18), channel_id=1, source_target_pairs={{0,2},{2,0},{4,6},{6,4},{8,10},{10,8},{12,14},{14,12},{16,18},{18,... | collective-permute-start | bytes 1572872 | tf_op jit(solution)/shard_map/ppermute | solution.py:236
  65.9 21.5 %collective-permute-start.6 = (bf16[512,512]{1,0:T(8,128)(2,1)}, bf16[512,512]{1,0:T(8,128)(2,1)}, u32[]{:S(2)}, u32[]{:S(2)}) collective-permute-start(bf16[512,512]{1,0:T(8,128)(2,1)} %get-tuple-element.24), channel_id=1, source_target_pairs={{0,4},{2,6},{4,0},{6,2},{8,12},{10,14},{12,8},{14,10},{16,20},{18,... | collective-permute-start | bytes 1572872 | tf_op jit(solution)/shard_map/ppermute | solution.py:216
  67.4 11.9 %copy-start.3 = (f32[256,1024]{1,0:T(8,128)S(1)}, f32[256,1024]{1,0:T(8,128)}, u32[]{:S(2)}) copy-start(f32[256,1024]{1,0:T(8,128)} %copy-done.2) | copy-start | bytes 3145732
  73.2 18.1 %collective-permute-start.10 = (bf16[256,1024]{1,0:T(8,128)(2,1)}, bf16[256,1024]{1,0:T(8,128)(2,1)}, u32[]{:S(2)}, u32[]{:S(2)}) collective-permute-start(bf16[256,1024]{1,0:T(8,128)(2,1)} %get-tuple-element.16), channel_id=1, source_target_pairs={{0,2},{2,0},{4,6},{6,4},{8,10},{10,8},{12,14},{14,12},{16,18},{18,... | collective-permute-start | bytes 1572872 | tf_op jit(solution)/shard_map/ppermute | solution.py:236
  81.3 16.0 %collective-permute-start.15 = (bf16[256,1024]{1,0:T(8,128)(2,1)}, bf16[256,1024]{1,0:T(8,128)(2,1)}, u32[]{:S(2)}, u32[]{:S(2)}) collective-permute-start(bf16[256,1024]{1,0:T(8,128)(2,1)} %fusion.3), channel_id=1, source_target_pairs={{0,8},{2,10},{4,12},{6,14},{24,16},{26,18},{28,20},{30,22},{1,9},{... | collective-permute-start | bytes 1572872 | tf_op jit(solution)/shard_map/ppermute | solution.py:239
  85.8 15.3 %collective-permute-start = (bf16[512,512]{1,0:T(8,128)(2,1)}, bf16[512,512]{1,0:T(8,128)(2,1)}, u32[]{:S(2)}, u32[]{:S(2)}) collective-permute-start(bf16[512,512]{1,0:T(8,128)(2,1)} %get-tuple-element.22), channel_id=1, source_target_pairs={{0,4},{2,6},{4,0},{6,2},{8,12},{10,14},{12,8},{14,10},{16,20},{18,... | collective-permute-start | bytes 1572872 | tf_op jit(solution)/shard_map/ppermute | solution.py:216
  87.4 10.0 %copy-start.4 = (f32[256,1024]{1,0:T(8,128)S(1)}, f32[256,1024]{1,0:T(8,128)}, u32[]{:S(2)}) copy-start(f32[256,1024]{1,0:T(8,128)} %copy-done.2) | copy-start | bytes 3145732
  93.8 11.7 %collective-permute-start.11 = (bf16[256,1024]{1,0:T(8,128)(2,1)}, bf16[256,1024]{1,0:T(8,128)(2,1)}, u32[]{:S(2)}, u32[]{:S(2)}) collective-permute-start(bf16[256,1024]{1,0:T(8,128)(2,1)} %fusion.2), channel_id=1, source_target_pairs={{0,8},{2,10},{4,12},{6,14},{24,16},{26,18},{28,20},{30,22},{1,9},{... | collective-permute-start | bytes 1572872 | tf_op jit(solution)/shard_map/ppermute | solution.py:239
  95.8 15.2 %collective-permute-start.7 = (bf16[256,1024]{1,0:T(8,128)(2,1)}, bf16[256,1024]{1,0:T(8,128)(2,1)}, u32[]{:S(2)}, u32[]{:S(2)}) collective-permute-start(bf16[256,1024]{1,0:T(8,128)(2,1)} %get-tuple-element.14), channel_id=1, source_target_pairs={{0,2},{2,0},{4,6},{6,4},{8,10},{10,8},{12,14},{14,12},{16,18},{18,... | collective-permute-start | bytes 1572872 | tf_op jit(solution)/shard_map/ppermute | solution.py:236
  99.6 11.4 %collective-permute-start.16 = (bf16[256,1024]{1,0:T(8,128)(2,1)}, bf16[256,1024]{1,0:T(8,128)(2,1)}, u32[]{:S(2)}, u32[]{:S(2)}) collective-permute-start(bf16[256,1024]{1,0:T(8,128)(2,1)} %add_convert_fusion.1), channel_id=1, source_target_pairs={{8,16},{10,18},{12,20},{14,22},{16,8},{18,10},{20,12},{22,14},{9,1... | collective-permute-start | bytes 1572872 | tf_op jit(solution)/shard_map/ppermute | solution.py:239
  101.1 9.9 %copy-start.6 = (f32[256,1024]{1,0:T(8,128)S(1)}, f32[256,1024]{1,0:T(8,128)}, u32[]{:S(2)}) copy-start(f32[256,1024]{1,0:T(8,128)} %copy-done.5) | copy-start | bytes 3145732
  104.4 25.0 %copy-start.9 = (f32[256,1024]{1,0:T(8,128)S(1)}, f32[256,1024]{1,0:T(8,128)}, u32[]{:S(2)}) copy-start(f32[256,1024]{1,0:T(8,128)} %param.10) | copy-start | bytes 3145732
  104.4 25.0 %copy-start.10 = (f32[256,1024]{1,0:T(8,128)S(1)}, f32[256,1024]{1,0:T(8,128)}, u32[]{:S(2)}) copy-start(f32[256,1024]{1,0:T(8,128)} %param.9) | copy-start | bytes 3145732
  104.4 15.2 %collective-permute-start.5 = (bf16[256,1024]{1,0:T(8,128)(2,1)S(1)}, bf16[256,1024]{1,0:T(8,128)(2,1)S(1)}, u32[]{:S(2)}, u32[]{:S(2)}) collective-permute-start(bf16[256,1024]{1,0:T(8,128)(2,1)S(1)} %get-tuple-element.12), channel_id=1, source_target_pairs={{0,2},{2,0},{4,6},{6,4},{8,10},{10,8},{12,14},{14,12},{16,18},{18,... | collective-permute-start | bytes 1572872 | tf_op jit(solution)/shard_map/ppermute | solution.py:236
  106.9 12.7 %collective-permute-start.12 = (bf16[256,1024]{1,0:T(8,128)(2,1)S(1)}, bf16[256,1024]{1,0:T(8,128)(2,1)S(1)}, u32[]{:S(2)}, u32[]{:S(2)}) collective-permute-start(bf16[256,1024]{1,0:T(8,128)(2,1)S(1)} %add_convert_fusion.2), channel_id=1, source_target_pairs={{8,16},{10,18},{12,20},{14,22},{16,8},{18,10},{20,12},{22,14},{9,1... | collective-permute-start | bytes 1572872 | tf_op jit(solution)/shard_map/ppermute | solution.py:239
  112.5 12.7 %collective-permute-start.8 = (bf16[256,1024]{1,0:T(8,128)(2,1)S(1)}, bf16[256,1024]{1,0:T(8,128)(2,1)S(1)}, u32[]{:S(2)}, u32[]{:S(2)}) collective-permute-start(bf16[256,1024]{1,0:T(8,128)(2,1)S(1)} %get-tuple-element.26), channel_id=1, source_target_pairs={{0,8},{2,10},{4,12},{6,14},{24,16},{26,18},{28,20},{30,22},{1,9},{... | collective-permute-start | bytes 1572872 | tf_op jit(solution)/shard_map/ppermute | solution.py:239
  117.0 12.3 %collective-permute-start.17 = (bf16[256,1024]{1,0:T(8,128)(2,1)S(1)}, bf16[256,1024]{1,0:T(8,128)(2,1)S(1)}, u32[]{:S(2)}, u32[]{:S(2)}) collective-permute-start(bf16[256,1024]{1,0:T(8,128)(2,1)S(1)} %get-tuple-element.27), channel_id=1, source_target_pairs={{8,0},{10,2},{12,4},{14,6},{16,24},{18,26},{20,28},{22,30},{9,1},{... | collective-permute-start | bytes 1572872 | tf_op jit(solution)/shard_map/ppermute | solution.py:239
  131.6 6.6 %collective-permute-start.18 = (bf16[256,1024]{1,0:T(8,128)(2,1)S(1)}, bf16[256,1024]{1,0:T(8,128)(2,1)S(1)}, u32[]{:S(2)}, u32[]{:S(2)}) collective-permute-start(bf16[256,1024]{1,0:T(8,128)(2,1)S(1)} %get-tuple-element.19.n_ref), channel_id=1, source_target_pairs={{0,1},{1,0},{2,3},{3,2},{4,5},{5,4},{6,7},{7,6},{8,9},{9,8},{10,11... | collective-permute-start | bytes 1572872 | tf_op jit(solution)/shard_map/ppermute | solution.py:251
  (6 other events, 19.7 us)

commit v2 on v0

v2 whole, which is shorter than its diff:
```python
import jax
import jax.numpy as jnp
from jax import lax
from jax.experimental import pallas as pl
from jax.experimental.pallas import tpu as pltpu
from jax.sharding import PartitionSpec as P

STEP = 100


beta_first = 0.9
beta_second = 0.999
epsilon = 1e-08


def adam(reduced, moment1, moment2):
    new_first = beta_first * moment1 + (1.0 - beta_first) * reduced
    new_second = beta_second * moment2 + (1.0 - beta_second) * reduced * reduced
    bias_first = 1.0 - beta_first**STEP
    bias_second = 1.0 - beta_second**STEP
    normed = (new_first / bias_first / (jnp.sqrt(new_second / bias_second) + epsilon)).astype(
        jnp.bfloat16
    )
    return new_first, new_second, normed


def plain(activations, out_grads, basis, moment1, moment2):
    partial_rank = jnp.dot(activations, basis, preferred_element_type=jnp.float32)
    token_rank = lax.psum(partial_rank, "mp").astype(jnp.bfloat16)
    reduced = lax.psum_scatter(
        lax.dot_general(
            out_grads, token_rank, (((0,), (0,)), ((), ())), preferred_element_type=jnp.float32
        ),
        "dp",
        scatter_dimension=0,
        tiled=True,
    )
    new_first, new_second, normed = adam(reduced, moment1, moment2)
    gathered = lax.all_gather(normed[None], "mp", axis=0, tiled=True)
    groups, owned, ranks = gathered.shape
    full = lax.dot_general(
        gathered.reshape(groups * owned, ranks),
        basis,
        (((1,), (1,)), ((), ())),
        preferred_element_type=jnp.float32,
    )
    return new_first, new_second, full.astype(jnp.bfloat16).reshape(groups, owned, basis.shape[0])


def whole(rows, columns):
    return pl.BlockSpec((rows, columns), lambda *_: (0, 0))


def call(kernel, name, outs, specs, mib, flops, moved, out_specs=None, grid=(1,), scratch=()):
    return pl.pallas_call(
        kernel,
        out_shape=outs,
        grid_spec=pltpu.PrefetchScalarGridSpec(
            num_scalar_prefetch=1,
            grid=grid,
            in_specs=specs,
            out_specs=[whole(*o.shape) for o in outs] if out_specs is None else out_specs,
            scratch_shapes=scratch,
        ),
        compiler_params=pltpu.CompilerParams(vmem_limit_bytes=mib * 1024 * 1024),
        cost_estimate=pl.CostEstimate(flops=flops, bytes_accessed=moved, transcendentals=0),
        name=name,
    )


def shape(rows, columns, dtype):
    return jax.ShapeDtypeStruct((rows, columns), dtype)


def take(place, grads, pieces, wide):
    def kernel(place_ref, g_ref, *refs):
        outs, sems = refs[:-1], refs[-1]
        copies = []
        for k, ((entry, first, rows), out) in enumerate(zip(pieces, outs)):
            columns = pl.ds(pl.multiple_of(place_ref[entry] * wide, wide), wide)
            copies.append(
                pltpu.make_async_copy(g_ref.at[pl.ds(first, rows), columns], out, sems.at[k])
            )
        for copy in copies:
            copy.start()
        for copy in copies:
            copy.wait()

    outs = [shape(rows, wide, grads.dtype) for _, _, rows in pieces]
    return call(
        kernel,
        "take",
        outs,
        [pl.BlockSpec(memory_space=pl.ANY)],
        8,
        0,
        4 * wide * sum(rows for _, _, rows in pieces),
        scratch=[pltpu.SemaphoreType.DMA((len(pieces),))],
    )(place, grads)


def rank_halves(place, activations, basis, core_at, steps=4):
    tokens, depth = activations.shape
    ranks = basis.shape[1] // 2
    tile = depth // steps

    def kernel(place_ref, a_ref, b_ref, other_ref, own_ref):
        core = place_ref[core_at]
        for o_ref, half in ((other_ref, 1 - core), (own_ref, core)):
            columns = pl.ds(pl.multiple_of(half * ranks, ranks), ranks)
            part = jnp.dot(a_ref[...], b_ref[:, columns], preferred_element_type=jnp.float32)

            @pl.when(pl.program_id(0) == 0)
            def _():
                o_ref[...] = part

            @pl.when(pl.program_id(0) > 0)
            def _():
                o_ref[...] += part

    half = shape(tokens, ranks, jnp.float32)
    return call(
        kernel,
        "rank_halves",
        [half, half],
        [
            pl.BlockSpec((tokens, tile), lambda k, p: (0, k)),
            pl.BlockSpec((tile, 2 * ranks), lambda k, p: (k, 0)),
        ],
        16,
        4 * tokens * depth * ranks,
        2 * (tokens + 2 * ranks) * depth + 8 * tokens * ranks,
        grid=(steps,),
    )(place, activations, basis)


def added(place, terms, dtype, masked=(), mask_at=None):
    rows, columns = terms[0].shape
    count = len(terms)

    def kernel(place_ref, *refs):
        total = refs[0][...].astype(jnp.float32)
        for ref in refs[1:count]:
            total += ref[...].astype(jnp.float32)
        for ref in refs[count:-1]:
            total += jnp.where(place_ref[mask_at] == 1, ref[...].astype(jnp.float32), 0.0)
        refs[-1][...] = total.astype(dtype)

    operands = [*terms, *masked]
    return call(
        kernel,
        "added",
        [shape(rows, columns, dtype)],
        [whole(rows, columns)] * len(operands),
        12,
        rows * columns * len(operands),
        4 * rows * columns * len(operands),
    )(place, *operands)[0]


def partial_sums(place, grads, got, rank_own, rank_got, block_at, x_at):
    tokens, ranks = rank_own[0].shape
    wide = got[0].shape[1]
    owned = wide // 2
    pieces = len(got)

    def kernel(place_ref, g_ref, *refs):
        got_refs, (t0_ref, t1_ref, u0_ref, u1_ref, send_ref, keep_ref) = refs[:pieces], refs[pieces:]
        x = place_ref[x_at]
        theirs = pl.ds(pl.multiple_of((1 - x) * owned, owned), owned)
        ours = pl.ds(pl.multiple_of(x * owned, owned), owned)
        mine = jnp.concatenate([g_ref[:, theirs], g_ref[:, ours]], axis=1)
        far = jnp.concatenate(
            [jnp.concatenate([r[:, theirs], r[:, ours]], axis=1) for r in got_refs], axis=0
        )
        dims = (((0,), (0,)), ((), ()))
        for side, (t_ref, u_ref) in enumerate(((t0_ref, u0_ref), (t1_ref, u1_ref))):
            total = lax.dot_general(
                mine, t_ref[...], dims, preferred_element_type=jnp.float32
            ) + lax.dot_general(far, u_ref[...], dims, preferred_element_type=jnp.float32)
            columns = slice(side * ranks, (side + 1) * ranks)
            send_ref[:, columns] = total[:owned].astype(send_ref.dtype)
            keep_ref[:, columns] = total[owned:]

    return call(
        kernel,
        "partial_sums",
        [shape(owned, 2 * ranks, jnp.bfloat16), shape(owned, 2 * ranks, jnp.float32)],
        [pl.BlockSpec((tokens, wide), lambda i, p: (0, p[block_at]))]
        + [whole(*g.shape) for g in got]
        + [whole(tokens, ranks)] * 4,
        20,
        8 * tokens * wide * ranks,
        4 * tokens * (wide + 2 * ranks) + 12 * owned * ranks,
    )(place, grads, *got, *rank_own, *rank_got)


def moments(place, terms, masked, moment1, moment2, mask_at, core_at, steps=4):
    owned, ranks = moment1.shape
    rows = owned // steps
    count = len(terms)

    def kernel(place_ref, *refs):
        total = refs[0][...].astype(jnp.float32)
        for ref in refs[1:count]:
            total += ref[...].astype(jnp.float32)
        total += jnp.where(place_ref[mask_at] == 1, refs[count][...].astype(jnp.float32), 0.0)
        here, there = total[:, : ranks // 2], total[:, ranks // 2 :]
        first = place_ref[core_at] == 0
        reduced = jnp.concatenate(
            [jnp.where(first, here, there), jnp.where(first, there, here)], axis=1
        )
        m1_ref, m2_ref, first_ref, second_ref, normed_ref = refs[count + 1 :]
        first_ref[...], second_ref[...], normed_ref[...] = adam(reduced, m1_ref[...], m2_ref[...])

    block = pl.BlockSpec((rows, ranks), lambda i, p: (i, 0))
    wide = shape(owned, ranks, jnp.float32)
    return call(
        kernel,
        "moments",
        [wide, wide, shape(owned, ranks, jnp.bfloat16)],
        [block] * (count + 3),
        12,
        20 * owned * ranks,
        28 * owned * ranks,
        out_specs=[block] * 3,
        grid=(steps,),
    )(place, *terms, masked, moment1, moment2)


def update_rows(place, normed, normed_other, basis, core_at, steps=8):
    owned, ranks = normed.shape
    width = basis.shape[0]
    tile = width // steps

    def kernel(place_ref, n_ref, m_ref, b_ref, o_ref):
        core = place_ref[core_at]
        rows = jnp.concatenate([n_ref[...], m_ref[...]])
        here = pl.ds(pl.multiple_of(pl.program_id(0) * tile, tile), tile)
        full = lax.dot_general(
            rows, b_ref[here, :], (((1,), (1,)), ((), ())), preferred_element_type=jnp.float32
        ).astype(jnp.bfloat16)
        o_ref[core] = full[:owned]
        o_ref[1 - core] = full[owned:]

    return call(
        kernel,
        "update_rows",
        [jax.ShapeDtypeStruct((2, owned, width), jnp.bfloat16)],
        [whole(owned, ranks), whole(owned, ranks), pl.BlockSpec(memory_space=pltpu.VMEM)],
        16,
        4 * owned * ranks * width,
        2 * (2 * owned * ranks + width * ranks + 2 * owned * width),
        out_specs=[pl.BlockSpec((2, owned, tile), lambda n, p: (0, 0, n))],
        grid=(steps,),
    )(place, normed, normed_other, basis)[0]


def staged(activations, out_grads, basis, moment1, moment2):
    shards = lax.axis_size("dp")
    planes = shards // 4
    owned = moment1.shape[0]
    tokens = activations.shape[0]
    me, core = lax.axis_index("dp"), lax.axis_index("mp")
    z, y, x = me // 4, me // 2 % 2, me % 2
    mid = (z > 0) & (z < planes - 1)

    along_y = [(i, i ^ 2) for i in range(shards)]
    along_x = [(i, i ^ 1) for i in range(shards)]
    outer = [(i, i ^ 4) for i in range(shards)]
    inner = [(i, i ^ 12 if 4 <= i < shards - 4 else i) for i in range(shards)]
    cores = [(0, 1), (1, 0)]

    order = [
        sorted(
            range(planes),
            key=lambda d, p=p: (d == p, -abs(d - p), (d < p) == (p < planes // 2)),
        )
        for p in range(planes)
    ]
    blocks = [
        sum(jnp.where(z == p, order[p][c], 0) for p in range(planes)) for c in range(planes)
    ]
    place = jnp.stack(
        [b * 2 + 1 - y for b in blocks] + [b * 2 + y for b in blocks] + [x, core, mid]
    ).astype(jnp.int32)
    x_at, core_at, mid_at = range(2 * planes, 2 * planes + 3)

    wide = 2 * owned
    split = tokens * 3 // 4
    grads, basis_hbm = (pltpu.with_memory_space_constraint(a, pltpu.HBM) for a in (out_grads, basis))
    early, late = take(place, grads, [(0, 0, split), (0, split, tokens - split)], wide)
    activations, early, late = lax.optimization_barrier((activations, early, late))
    early = lax.ppermute(early, "dp", along_y)
    late = lax.ppermute(late, "dp", along_y)

    activations = pltpu.with_memory_space_constraint(activations, pltpu.HBM)
    other, own = rank_halves(place, activations, basis_hbm, core_at)
    other, own, early = lax.optimization_barrier((other, own, early))
    arrived = lax.ppermute(other, "mp", cores)
    own, late = lax.optimization_barrier((own, late))
    half = added(place, [own, arrived], jnp.bfloat16)
    half_far = lax.ppermute(half, "dp", along_y)
    half_other = lax.ppermute(half, "mp", cores)
    place_later, _ = lax.optimization_barrier((place, half))
    rest = take(place_later, grads, [(c, 0, tokens) for c in range(1, planes)], wide)
    half_far, *rest = lax.optimization_barrier((half_far, *rest))
    half_far_other = lax.ppermute(half_far, "mp", cores)
    rank_own, rank_got = (half, half_other), (half_far, half_far_other)
    got = [[early, late]] + [[lax.ppermute(mine, "dp", along_y)] for mine in rest]

    sums = []
    for c in range(planes):
        send, keep = partial_sums(
            place, grads, got[c], rank_own, rank_got, planes + c, x_at
        )
        sums.append([keep, lax.ppermute(send, "dp", along_x)])

    def hop(terms, pairs, *masked):
        return lax.ppermute(added(place, terms, jnp.bfloat16, masked, mid_at), "dp", pairs)

    first, second, third, final = sums
    out1 = hop(first, outer)
    out2 = hop(second, outer)
    in2 = hop([*first, out1], inner)
    out3 = hop(third, outer, in2)
    in3 = hop([*second, out2], inner)

    new_first, new_second, normed = moments(
        place, [*final, out3], in3, moment1, moment2, mid_at, core_at
    )
    normed_other = lax.ppermute(normed, "mp", cores)
    update = update_rows(place, normed, normed_other, basis, core_at)
    return new_first, new_second, update


def solution(mesh):
    fits = mesh.shape["mp"] == 2 and mesh.shape["dp"] == 16
    return jax.shard_map(
        staged if fits else plain,
        mesh=mesh,
        in_specs=(
            P("dp", "mp"),
            P("dp", "mp"),
            P("mp", None),
            P(("mp", "dp"), None),
            P(("mp", "dp"), None),
        ),
        out_specs=(P(("mp", "dp"), None), P(("mp", "dp"), None), P(None, "dp", "mp")),
        check_vma=False,
    )
```

time: 419 us -> 108 us (0.26)
  waiting for transfers between devices: 358 us -> 41.9 us
  Pallas kernels: 0 us -> 38.4 us
  matrix products: 28.8 us -> 0 us
  starting transfers between devices: 0.08 us -> 26.2 us
  between operations: 14.1 us -> 0.88 us
  blocking collectives: 9.29 us -> 0 us
  local copies, waits for them, and re-layouts: 5.4 us -> 0.11 us
    reduce_scatter x1 -> x0, waiting for transfers between devices: 346 us -> none  [on_device(): lax.psum_scatter(lax.dot_general(out_grads, token_rank, (((0,), (0,)), ((...]
    ppermute x0 -> x19, waiting for transfers between devices: none -> 41.9 us  [the longest x3 10.4 us: staged(): lax.ppermute(mine, 'dp', along_y)]
    pallas_call x0 -> x15, Pallas kernels: none -> 38.4 us  [the longest x4 11.5 us: partial_sums(): call(kernel, 'partial_sums', [shape(owned, 2 * ranks, jnp.bfloat16), shap...]
    dot_general x3 -> x0, matrix products: 28.8 us -> none  [the longest x1 10.3 us: on_device(): lax.dot_general(out_grads, token_rank, (((0,), (0,)), ((), ())), preferre...]
    ppermute x0 -> x19, starting transfers between devices: none -> 26.2 us  [the longest x5 9.2 us: hop(): lax.ppermute(added(place, terms, jnp.bfloat16, masked, mid_at), 'dp', pairs)]
    all_gather x1 -> x0, waiting for transfers between devices: 12.1 us -> none  [on_device(): gathered = lax.all_gather(normed[None], 'mp', axis=0, tiled=True)]
    psum x1 -> x0, blocking collectives: 9.29 us -> none  [on_device(): token_rank = lax.psum(partial_rank, 'mp').astype(jnp.bfloat16)]
    unnamed x8, local copies, waits for them, and re-layouts: 5.4 us -> 0.02 us
  transfers between devices with their start and end apart: 2 -> 19, of which waited for: 2 -> 12; matrix products, arithmetic and copies ran while one was open for 1% -> 0% of each run, Pallas kernels for 0% -> 24%
where the time goes in v2:
time: 108 us; the launch traced here: 107 us
  waiting for transfers between devices  41.9 us (39%)
  Pallas kernels  38.4 us (36%)
  starting transfers between devices  26.2 us (24%)
    pallas_call x4, Pallas kernels, partial_sums(): call(kernel, 'partial_sums', [shape(owned, 2 * ranks, jnp.bfloat16), shap...  11.5 us
    ppermute x3, waiting for transfers between devices, staged(): lax.ppermute(mine, 'dp', along_y)  10.4 us
    ppermute x1, waiting for transfers between devices, staged(): half_far = lax.ppermute(half, 'dp', along_y)  10 us
    pallas_call x1, Pallas kernels, rank_halves(): call(kernel, 'rank_halves', [half, half], [pl.BlockSpec((tokens, tile), l...  9.25 us
    ppermute x5, starting transfers between devices, hop(): lax.ppermute(added(place, terms, jnp.bfloat16, masked, mid_at), 'dp', pairs)  9.2 us
    ppermute x4, waiting for transfers between devices, staged(): sums.append([keep, lax.ppermute(send, 'dp', along_x)])  7.79 us
    pallas_call x1, Pallas kernels, update_rows(): call(kernel, 'update_rows', [jax.ShapeDtypeStruct((2, owned, width), jnp....  7.47 us
    ppermute x5, waiting for transfers between devices, hop(): lax.ppermute(added(place, terms, jnp.bfloat16, masked, mid_at), 'dp', pairs)  6.94 us
  transfers between devices with their start and end apart: 19, of which 12 were waited for; matrix products, arithmetic and copies ran while one was open for 0% of the time, Pallas kernels for 24%

profile of v2, /device:TPU:0, one launch (start us, length us, event | category | flops | bytes accessed | tf_op | source)
XLA Modules:
  0.0 107.5 jit_solution(9023624604603964863)
XLA Ops:
  0.8 1.6 %take.2 = (bf16[384,512]{1,0:T(8,128)(2,1)S(1)}, bf16[128,512]{1,0:T(8,128)(2,1)S(1)}) custom-call(s32[11]{0:T(128)S(1)} %stack.51.place_ref, bf16[512,4096]{1,0:T(8,128)(2,1)} %g_ref.11), custom_call_target="tpu_custom_call" | custom-call | bytes 1048576 | tf_op jit(solution)/shard_map/take/pallas_call | solution.py:90
  2.4 3.0 %collective-permute-start = (bf16[384,512]{1,0:T(8,128)(2,1)S(1)}, bf16[384,512]{1,0:T(8,128)(2,1)S(1)}, u32[]{:S(2)}, u32[]{:S(2)}) collective-permute-start(bf16[384,512]{1,0:T(8,128)(2,1)S(1)} %get-tuple-element.39), channel_id=1, source_target_pairs={{0,4},{2,6},{4,0},{6,2},{8,12},{10,14},{12,8},{14,10},{16,20},{18,... | collective-permute-start | bytes 1179656 | tf_op jit(solution)/shard_map/ppermute | solution.py:294
  5.4 9.3 %rank_halves.1 = (f32[512,512]{1,0:T(8,128)S(1)}, f32[512,512]{1,0:T(8,128)S(1)}) custom-call(s32[11]{0:T(128)S(1)} %stack.51.place_ref, bf16[512,4096]{1,0:T(8,128)(2,1)} %a_ref, bf16[4096,1024]{1,0:T(8,128)(2,1)} %b_ref.3), custom_call_target="tpu_custom_call" | custom-call | flops 4294967296 | bytes 14680064 | tf_op jit(solution)/shard_map/rank_halves/pallas_call | solution.py:122
  16.3 4.4 %collective-permute-done.1.refs_1_ = bf16[128,512]{1,0:T(8,128)(2,1)S(1)} collective-permute-done((bf16[128,512]{1,0:T(8,128)(2,1)S(1)}, bf16[128,512]{1,0:T(8,128)(2,1)S(1)}, u32[]{:S(2)}, u32[]{:S(2)}) %collective-permute-start.1) | collective-permute-done | bytes 131104 | tf_op jit(solution)/shard_map/ppermute | solution.py:295
  22.9 1.9 %take.3 = (bf16[512,512]{1,0:T(8,128)(2,1)S(1)}, bf16[512,512]{1,0:T(8,128)(2,1)S(1)}, bf16[512,512]{1,0:T(8,128)(2,1)S(1)}) custom-call(s32[11]{0:T(128)S(1)} %stack.51.place_ref, bf16[512,4096]{1,0:T(8,128)(2,1)} %g_ref.11), custom_call_target="tpu_custom_call" | custom-call | bytes 3145728 | tf_op jit(solution)/shard_map/take/pallas_call | solution.py:90
  24.9 10.0 %collective-permute-done.3.refs_3_.refs_4_ = bf16[512,512]{1,0:T(8,128)(2,1)S(1)} collective-permute-done((bf16[512,512]{1,0:T(8,128)(2,1)S(1)}, bf16[512,512]{1,0:T(8,128)(2,1)S(1)}, u32[]{:S(2)}, u32[]{:S(2)}) %collective-permute-start.3) | collective-permute-done | bytes 524320 | tf_op jit(solution)/shard_map/ppermute | solution.py:303
  36.8 2.9 %partial_sums.6 = (bf16[256,1024]{1,0:T(8,128)(2,1)S(1)}, f32[256,1024]{1,0:T(8,128)S(1)}) custom-call(s32[11]{0:T(128)S(1)} %stack.51.place_ref, bf16[512,4096]{1,0:T(8,128)(2,1)} %g_ref.11, bf16[384,512]{1,0:T(8,128)(2,1)S(1)} %collective-permute-done.refs_0_, bf16[128,512]{1,0:T(8,128)(2,1)S(1)} %collective-permute-done.1.refs_1_, ...), custom_call_target="tpu_custom_call" | custom-call | flops 1073741824 | bytes 4718592 | tf_op jit(solution)/shard_map/partial_sums/pallas_call | solution.py:185
  41.2 1.6 %collective-permute-start.8 = (bf16[512,512]{1,0:T(8,128)(2,1)S(1)}, bf16[512,512]{1,0:T(8,128)(2,1)S(1)}, u32[]{:S(2)}, u32[]{:S(2)}) collective-permute-start(bf16[512,512]{1,0:T(8,128)(2,1)S(1)} %get-tuple-element.52), channel_id=1, source_target_pairs={{0,4},{2,6},{4,0},{6,2},{8,12},{10,14},{12,8},{14,10},{16,20},{18,... | collective-permute-start | bytes 1572872 | tf_op jit(solution)/shard_map/ppermute | solution.py:310
  42.8 6.8 %collective-permute-done.14.refs_0_ = bf16[512,512]{1,0:T(8,128)(2,1)S(1)} collective-permute-done((bf16[512,512]{1,0:T(8,128)(2,1)S(1)}, bf16[512,512]{1,0:T(8,128)(2,1)S(1)}, u32[]{:S(2)}, u32[]{:S(2)}) %collective-permute-start.14) | collective-permute-done | bytes 524320 | tf_op jit(solution)/shard_map/ppermute | solution.py:310
  49.6 2.9 %partial_sums.7 = (bf16[256,1024]{1,0:T(8,128)(2,1)S(1)}, f32[256,1024]{1,0:T(8,128)S(1)}) custom-call(s32[11]{0:T(128)S(1)} %stack.51.place_ref, bf16[512,4096]{1,0:T(8,128)(2,1)} %g_ref.11, bf16[512,512]{1,0:T(8,128)(2,1)S(1)} %collective-permute-done.14.refs_0_, bf16[512,512]{1,0:T(8,128)(2,1)S(1)} %added.6.refs_1_.refs_2_, ...), custom_call_target="tpu_custom_call" | custom-call | flops 1073741824 | bytes 4718592 | tf_op jit(solution)/shard_map/partial_sums/pallas_call | solution.py:185
  54.7 1.7 %collective-permute-start.11 = (bf16[256,1024]{1,0:T(8,128)(2,1)S(1)}, bf16[256,1024]{1,0:T(8,128)(2,1)S(1)}, u32[]{:S(2)}, u32[]{:S(2)}) collective-permute-start(bf16[256,1024]{1,0:T(8,128)(2,1)S(1)} %added.7), channel_id=1, source_target_pairs={{0,8},{2,10},{4,12},{6,14},{8,0},{10,2},{12,4},{14,6},{16,24},{18,... | collective-permute-start | bytes 1572872 | tf_op jit(solution)/shard_map/ppermute | solution.py:320
  57.9 3.0 %collective-permute-done.8.refs_0_ = bf16[512,512]{1,0:T(8,128)(2,1)S(1)} collective-permute-done((bf16[512,512]{1,0:T(8,128)(2,1)S(1)}, bf16[512,512]{1,0:T(8,128)(2,1)S(1)}, u32[]{:S(2)}, u32[]{:S(2)}) %collective-permute-start.8) | collective-permute-done | bytes 524320 | tf_op jit(solution)/shard_map/ppermute | solution.py:310
  60.9 2.9 %partial_sums.5 = (bf16[256,1024]{1,0:T(8,128)(2,1)S(1)}, f32[256,1024]{1,0:T(8,128)S(1)}) custom-call(s32[11]{0:T(128)S(1)} %stack.51.place_ref, bf16[512,4096]{1,0:T(8,128)(2,1)} %g_ref.11, bf16[512,512]{1,0:T(8,128)(2,1)S(1)} %collective-permute-done.8.refs_0_, bf16[512,512]{1,0:T(8,128)(2,1)S(1)} %added.6.refs_1_.refs_2_, ...), custom_call_target="tpu_custom_call" | custom-call | flops 1073741824 | bytes 4718592 | tf_op jit(solution)/shard_map/partial_sums/pallas_call | solution.py:185
  63.7 2.0 %collective-permute-done.15.refs_1_ = bf16[256,1024]{1,0:T(8,128)(2,1)S(1)} collective-permute-done((bf16[256,1024]{1,0:T(8,128)(2,1)S(1)}, bf16[256,1024]{1,0:T(8,128)(2,1)S(1)}, u32[]{:S(2)}, u32[]{:S(2)}) %collective-permute-start.15) | collective-permute-done | bytes 524320 | tf_op jit(solution)/shard_map/ppermute | solution.py:317
  66.4 1.6 %collective-permute-start.16 = (bf16[256,1024]{1,0:T(8,128)(2,1)S(1)}, bf16[256,1024]{1,0:T(8,128)(2,1)S(1)}, u32[]{:S(2)}, u32[]{:S(2)}) collective-permute-start(bf16[256,1024]{1,0:T(8,128)(2,1)S(1)} %added.10), channel_id=1, source_target_pairs={{0,8},{2,10},{4,12},{6,14},{8,0},{10,2},{12,4},{14,6},{16,24},{18,... | collective-permute-start | bytes 1572872 | tf_op jit(solution)/shard_map/ppermute | solution.py:320
  71.7 2.9 %partial_sums.4 = (bf16[256,1024]{1,0:T(8,128)(2,1)S(1)}, f32[256,1024]{1,0:T(8,128)S(1)}) custom-call(s32[11]{0:T(128)S(1)} %stack.51.place_ref, bf16[512,4096]{1,0:T(8,128)(2,1)} %g_ref.11, bf16[512,512]{1,0:T(8,128)(2,1)S(1)} %collective-permute-done.4.refs_0_, bf16[512,512]{1,0:T(8,128)(2,1)S(1)} %added.6.refs_1_.refs_2_, ...), custom_call_target="tpu_custom_call" | custom-call | flops 1073741824 | bytes 4718592 | tf_op jit(solution)/shard_map/partial_sums/pallas_call | solution.py:185
  76.1 2.7 %collective-permute-done.16.refs_2_ = bf16[256,1024]{1,0:T(8,128)(2,1)S(1)} collective-permute-done((bf16[256,1024]{1,0:T(8,128)(2,1)S(1)}, bf16[256,1024]{1,0:T(8,128)(2,1)S(1)}, u32[]{:S(2)}, u32[]{:S(2)}) %collective-permute-start.16) | collective-permute-done | bytes 524320 | tf_op jit(solution)/shard_map/ppermute | solution.py:320
  80.3 2.6 %collective-permute-done.9.refs_1_ = bf16[256,1024]{1,0:T(8,128)(2,1)S(1)} collective-permute-done((bf16[256,1024]{1,0:T(8,128)(2,1)S(1)}, bf16[256,1024]{1,0:T(8,128)(2,1)S(1)}, u32[]{:S(2)}, u32[]{:S(2)}) %collective-permute-start.9) | collective-permute-done | bytes 524320 | tf_op jit(solution)/shard_map/ppermute | solution.py:317
  83.6 4.4 %collective-permute-start.13 = (bf16[256,1024]{1,0:T(8,128)(2,1)S(1)}, bf16[256,1024]{1,0:T(8,128)(2,1)S(1)}, u32[]{:S(2)}, u32[]{:S(2)}) collective-permute-start(bf16[256,1024]{1,0:T(8,128)(2,1)S(1)} %added.9), channel_id=1, source_target_pairs={{0,8},{2,10},{4,12},{6,14},{8,0},{10,2},{12,4},{14,6},{16,24},{18,... | collective-permute-start | bytes 1572872 | tf_op jit(solution)/shard_map/ppermute | solution.py:320
  88.0 3.2 %collective-permute-done.7.refs_1_ = bf16[256,1024]{1,0:T(8,128)(2,1)S(1)} collective-permute-done((bf16[256,1024]{1,0:T(8,128)(2,1)S(1)}, bf16[256,1024]{1,0:T(8,128)(2,1)S(1)}, u32[]{:S(2)}, u32[]{:S(2)}) %collective-permute-start.7) | collective-permute-done | bytes 524320 | tf_op jit(solution)/shard_map/ppermute | solution.py:317
  91.2 4.2 %collective-permute-done.13.refs_2_ = bf16[256,1024]{1,0:T(8,128)(2,1)S(1)} collective-permute-done((bf16[256,1024]{1,0:T(8,128)(2,1)S(1)}, bf16[256,1024]{1,0:T(8,128)(2,1)S(1)}, u32[]{:S(2)}, u32[]{:S(2)}) %collective-permute-start.13) | collective-permute-done | bytes 524320 | tf_op jit(solution)/shard_map/ppermute | solution.py:320
  95.4 2.6 %moments.1 = (f32[256,1024]{1,0:T(8,128)}, f32[256,1024]{1,0:T(8,128)}, bf16[256,1024]{1,0:T(8,128)(2,1)S(1)}) custom-call(s32[11]{0:T(128)S(1)} %stack.51.place_ref, f32[256,1024]{1,0:T(8,128)S(1)} %get-tuple-element.50.refs_0_, bf16[256,1024]{1,0:T(8,128)(2,1)S(1)} %collective-permute-done.7.refs_1_, ...), custom_call_target="tpu_custom_call" | custom-call | flops 5242880 | bytes 7340032 | tf_op jit(solution)/shard_map/moments/pallas_call | solution.py:218
  98.1 1.9 %collective-permute-done.18.m_ref = bf16[256,1024]{1,0:T(8,128)(2,1)S(1)} collective-permute-done((bf16[256,1024]{1,0:T(8,128)(2,1)S(1)}, bf16[256,1024]{1,0:T(8,128)(2,1)S(1)}, u32[]{:S(2)}, u32[]{:S(2)}) %collective-permute-start.18) | collective-permute-done | bytes 524320 | tf_op jit(solution)/shard_map/ppermute | solution.py:332
  100.0 7.5 %update_rows.1 = bf16[2,256,4096]{2,1,0:T(8,128)(2,1)} custom-call(s32[11]{0:T(128)S(1)} %stack.51.place_ref, bf16[256,1024]{1,0:T(8,128)(2,1)S(1)} %get-tuple-element.64.n_ref, bf16[256,1024]{1,0:T(8,128)(2,1)S(1)} %collective-permute-done.18.m_ref, bf16[4096,1024]{1,0:T(8,128)(2,1)S(1)} %bitcast.12), custom_call_target="tpu_custom_call" | custom-call | flops 4294967296 | bytes 13631488 | tf_op jit(solution)/shard_map/update_rows/pallas_call | solution.py:246
  (39 shorter events, 19.1 us)
Async XLA Ops:
  2.4 12.3 %collective-permute-start = (bf16[384,512]{1,0:T(8,128)(2,1)S(1)}, bf16[384,512]{1,0:T(8,128)(2,1)S(1)}, u32[]{:S(2)}, u32[]{:S(2)}) collective-permute-start(bf16[384,512]{1,0:T(8,128)(2,1)S(1)} %get-tuple-element.39), channel_id=1, source_target_pairs={{0,4},{2,6},{4,0},{6,2},{8,12},{10,14},{12,8},{14,10},{16,20},{18,... | collective-permute-start | bytes 1179656 | tf_op jit(solution)/shard_map/ppermute | solution.py:294
  14.7 6.0 %collective-permute-start.2 = (f32[512,512]{1,0:T(8,128)S(1)}, f32[512,512]{1,0:T(8,128)S(1)}, u32[]{:S(2)}, u32[]{:S(2)}) collective-permute-start(f32[512,512]{1,0:T(8,128)S(1)} %get-tuple-element.43), channel_id=1, source_target_pairs={{0,1},{1,0},{2,3},{3,2},{4,5},{5,4},{6,7},{7,6},{8,9},{9,8},{10,11... | collective-permute-start | bytes 3145736 | tf_op jit(solution)/shard_map/ppermute | solution.py:300
  14.8 5.9 %collective-permute-start.1 = (bf16[128,512]{1,0:T(8,128)(2,1)S(1)}, bf16[128,512]{1,0:T(8,128)(2,1)S(1)}, u32[]{:S(2)}, u32[]{:S(2)}) collective-permute-start(bf16[128,512]{1,0:T(8,128)(2,1)S(1)} %get-tuple-element.41), channel_id=1, source_target_pairs={{0,4},{2,6},{4,0},{6,2},{8,12},{10,14},{12,8},{14,10},{16,20},{18,... | collective-permute-start | bytes 393224 | tf_op jit(solution)/shard_map/ppermute | solution.py:295
  21.3 13.6 %collective-permute-start.3 = (bf16[512,512]{1,0:T(8,128)(2,1)S(1)}, bf16[512,512]{1,0:T(8,128)(2,1)S(1)}, u32[]{:S(2)}, u32[]{:S(2)}) collective-permute-start(bf16[512,512]{1,0:T(8,128)(2,1)S(1)} %added.6.refs_1_.refs_2_), channel_id=1, source_target_pairs={{0,4},{2,6},{4,0},{6,2},{8,12},{10,14},{12,8},{14,10},{16,20},{18,... | collective-permute-start | bytes 1572872 | tf_op jit(solution)/shard_map/ppermute | solution.py:303
  22.9 13.6 %collective-permute-start.5 = (bf16[512,512]{1,0:T(8,128)(2,1)S(1)}, bf16[512,512]{1,0:T(8,128)(2,1)S(1)}, u32[]{:S(2)}, u32[]{:S(2)}) collective-permute-start(bf16[512,512]{1,0:T(8,128)(2,1)S(1)} %added.6.refs_1_.refs_2_), channel_id=1, source_target_pairs={{0,1},{1,0},{2,3},{3,2},{4,5},{5,4},{6,7},{7,6},{8,9},{9,8},{10,11... | collective-permute-start | bytes 1572872 | tf_op jit(solution)/shard_map/ppermute | solution.py:304
  34.9 1.9 %collective-permute-start.6 = (bf16[512,512]{1,0:T(8,128)(2,1)S(1)}, bf16[512,512]{1,0:T(8,128)(2,1)S(1)}, u32[]{:S(2)}, u32[]{:S(2)}) collective-permute-start(bf16[512,512]{1,0:T(8,128)(2,1)S(1)} %collective-permute-done.3.refs_3_.refs_4_), channel_id=1, source_target_pairs={{0,1},{1,0},{2,3},{3,2},{4,5},{5,4},{6,7},{7,6},{8,9},{9,8},{10,11... | collective-permute-start | bytes 1572872 | tf_op jit(solution)/shard_map/ppermute | solution.py:308
  34.9 14.7 %collective-permute-start.14 = (bf16[512,512]{1,0:T(8,128)(2,1)S(1)}, bf16[512,512]{1,0:T(8,128)(2,1)S(1)}, u32[]{:S(2)}, u32[]{:S(2)}) collective-permute-start(bf16[512,512]{1,0:T(8,128)(2,1)S(1)} %get-tuple-element.59), channel_id=1, source_target_pairs={{0,4},{2,6},{4,0},{6,2},{8,12},{10,14},{12,8},{14,10},{16,20},{18,... | collective-permute-start | bytes 1572872 | tf_op jit(solution)/shard_map/ppermute | solution.py:310
  39.7 14.3 %collective-permute-start.10 = (bf16[256,1024]{1,0:T(8,128)(2,1)S(1)}, bf16[256,1024]{1,0:T(8,128)(2,1)S(1)}, u32[]{:S(2)}, u32[]{:S(2)}) collective-permute-start(bf16[256,1024]{1,0:T(8,128)(2,1)S(1)} %get-tuple-element.58), channel_id=1, source_target_pairs={{0,2},{2,0},{4,6},{6,4},{8,10},{10,8},{12,14},{14,12},{16,18},{18,... | collective-permute-start | bytes 1572872 | tf_op jit(solution)/shard_map/ppermute | solution.py:317
  41.2 19.6 %collective-permute-start.8 = (bf16[512,512]{1,0:T(8,128)(2,1)S(1)}, bf16[512,512]{1,0:T(8,128)(2,1)S(1)}, u32[]{:S(2)}, u32[]{:S(2)}) collective-permute-start(bf16[512,512]{1,0:T(8,128)(2,1)S(1)} %get-tuple-element.52), channel_id=1, source_target_pairs={{0,4},{2,6},{4,0},{6,2},{8,12},{10,14},{12,8},{14,10},{16,20},{18,... | collective-permute-start | bytes 1572872 | tf_op jit(solution)/shard_map/ppermute | solution.py:310
  52.5 13.2 %collective-permute-start.15 = (bf16[256,1024]{1,0:T(8,128)(2,1)S(1)}, bf16[256,1024]{1,0:T(8,128)(2,1)S(1)}, u32[]{:S(2)}, u32[]{:S(2)}) collective-permute-start(bf16[256,1024]{1,0:T(8,128)(2,1)S(1)} %get-tuple-element.61), channel_id=1, source_target_pairs={{0,2},{2,0},{4,6},{6,4},{8,10},{10,8},{12,14},{14,12},{16,18},{18,... | collective-permute-start | bytes 1572872 | tf_op jit(solution)/shard_map/ppermute | solution.py:317
  54.7 14.8 %collective-permute-start.11 = (bf16[256,1024]{1,0:T(8,128)(2,1)S(1)}, bf16[256,1024]{1,0:T(8,128)(2,1)S(1)}, u32[]{:S(2)}, u32[]{:S(2)}) collective-permute-start(bf16[256,1024]{1,0:T(8,128)(2,1)S(1)} %added.7), channel_id=1, source_target_pairs={{0,8},{2,10},{4,12},{6,14},{8,0},{10,2},{12,4},{14,6},{16,24},{18,... | collective-permute-start | bytes 1572872 | tf_op jit(solution)/shard_map/ppermute | solution.py:320
  56.3 15.4 %collective-permute-start.4 = (bf16[512,512]{1,0:T(8,128)(2,1)S(1)}, bf16[512,512]{1,0:T(8,128)(2,1)S(1)}, u32[]{:S(2)}, u32[]{:S(2)}) collective-permute-start(bf16[512,512]{1,0:T(8,128)(2,1)S(1)} %get-tuple-element.48), channel_id=1, source_target_pairs={{0,4},{2,6},{4,0},{6,2},{8,12},{10,14},{12,8},{14,10},{16,20},{18,... | collective-permute-start | bytes 1572872 | tf_op jit(solution)/shard_map/ppermute | solution.py:310
  66.4 12.5 %collective-permute-start.16 = (bf16[256,1024]{1,0:T(8,128)(2,1)S(1)}, bf16[256,1024]{1,0:T(8,128)(2,1)S(1)}, u32[]{:S(2)}, u32[]{:S(2)}) collective-permute-start(bf16[256,1024]{1,0:T(8,128)(2,1)S(1)} %added.10), channel_id=1, source_target_pairs={{0,8},{2,10},{4,12},{6,14},{8,0},{10,2},{12,4},{14,6},{16,24},{18,... | collective-permute-start | bytes 1572872 | tf_op jit(solution)/shard_map/ppermute | solution.py:320
  68.0 14.9 %collective-permute-start.9 = (bf16[256,1024]{1,0:T(8,128)(2,1)S(1)}, bf16[256,1024]{1,0:T(8,128)(2,1)S(1)}, u32[]{:S(2)}, u32[]{:S(2)}) collective-permute-start(bf16[256,1024]{1,0:T(8,128)(2,1)S(1)} %get-tuple-element.54), channel_id=1, source_target_pairs={{0,2},{2,0},{4,6},{6,4},{8,10},{10,8},{12,14},{14,12},{16,18},{18,... | collective-permute-start | bytes 1572872 | tf_op jit(solution)/shard_map/ppermute | solution.py:317
  69.5 30.5 %slice-start = ((s8[8388608]{0:T(1024)(128)(4,1)}), s8[4194304]{0:T(1024)(128)(4,1)S(1)}, s32[]{:S(2)}) async-start(s8[8388608]{0:T(1024)(128)(4,1)} %bitcast.11), calls=%async_computation | async-start | bytes 8388608
  70.2 12.6 %collective-permute-start.12 = (bf16[256,1024]{1,0:T(8,128)(2,1)S(1)}, bf16[256,1024]{1,0:T(8,128)(2,1)S(1)}, u32[]{:S(2)}, u32[]{:S(2)}) collective-permute-start(bf16[256,1024]{1,0:T(8,128)(2,1)S(1)} %added.8), channel_id=1, source_target_pairs={{0,0},{2,2},{4,4},{6,6},{8,16},{10,18},{12,20},{14,22},{16,8},{18,... | collective-permute-start | bytes 1572872 | tf_op jit(solution)/shard_map/ppermute | solution.py:320
  74.6 20.8 %copy-start = (f32[256,1024]{1,0:T(8,128)S(1)}, f32[256,1024]{1,0:T(8,128)}, u32[]{:S(2)}) copy-start(f32[256,1024]{1,0:T(8,128)} %refs_4_.1) | copy-start | bytes 3145732
  74.6 20.8 %copy-start.1 = (f32[256,1024]{1,0:T(8,128)S(1)}, f32[256,1024]{1,0:T(8,128)}, u32[]{:S(2)}) copy-start(f32[256,1024]{1,0:T(8,128)} %refs_5_.1) | copy-start | bytes 3145732
  74.6 25.4 %slice-start.1 = ((s8[8388608]{0:T(1024)(128)(4,1)}), s8[4194304]{0:T(1024)(128)(4,1)S(1)}, s32[]{:S(2)}) async-start(s8[8388608]{0:T(1024)(128)(4,1)} %bitcast.11), calls=%async_computation.1 | async-start | bytes 8388608
  74.6 16.6 %collective-permute-start.7 = (bf16[256,1024]{1,0:T(8,128)(2,1)S(1)}, bf16[256,1024]{1,0:T(8,128)(2,1)S(1)}, u32[]{:S(2)}, u32[]{:S(2)}) collective-permute-start(bf16[256,1024]{1,0:T(8,128)(2,1)S(1)} %get-tuple-element.51), channel_id=1, source_target_pairs={{0,2},{2,0},{4,6},{6,4},{8,10},{10,8},{12,14},{14,12},{16,18},{18,... | collective-permute-start | bytes 1572872 | tf_op jit(solution)/shard_map/ppermute | solution.py:317
  79.6 11.6 %collective-permute-start.17 = (bf16[256,1024]{1,0:T(8,128)(2,1)S(1)}, bf16[256,1024]{1,0:T(8,128)(2,1)S(1)}, u32[]{:S(2)}, u32[]{:S(2)}) collective-permute-start(bf16[256,1024]{1,0:T(8,128)(2,1)S(1)} %added.11), channel_id=1, source_target_pairs={{0,0},{2,2},{4,4},{6,6},{8,16},{10,18},{12,20},{14,22},{16,8},{18,... | collective-permute-start | bytes 1572872 | tf_op jit(solution)/shard_map/ppermute | solution.py:320
  83.6 11.8 %collective-permute-start.13 = (bf16[256,1024]{1,0:T(8,128)(2,1)S(1)}, bf16[256,1024]{1,0:T(8,128)(2,1)S(1)}, u32[]{:S(2)}, u32[]{:S(2)}) collective-permute-start(bf16[256,1024]{1,0:T(8,128)(2,1)S(1)} %added.9), channel_id=1, source_target_pairs={{0,8},{2,10},{4,12},{6,14},{8,0},{10,2},{12,4},{14,6},{16,24},{18,... | collective-permute-start | bytes 1572872 | tf_op jit(solution)/shard_map/ppermute | solution.py:320
  98.1 1.9 %collective-permute-start.18 = (bf16[256,1024]{1,0:T(8,128)(2,1)S(1)}, bf16[256,1024]{1,0:T(8,128)(2,1)S(1)}, u32[]{:S(2)}, u32[]{:S(2)}) collective-permute-start(bf16[256,1024]{1,0:T(8,128)(2,1)S(1)} %get-tuple-element.64.n_ref), channel_id=1, source_target_pairs={{0,1},{1,0},{2,3},{3,2},{4,5},{5,4},{6,7},{7,6},{8,9},{9,8},{10,11... | collective-permute-start | bytes 1572872 | tf_op jit(solution)/shard_map/ppermute | solution.py:332

commit v3 on v2

--- a/solution.py
+++ b/solution.py
@@ -99,38 +99,55 @@
     )(place, grads)
 
 
-def rank_halves(place, activations, basis, core_at, steps=4):
+def rank_halves(place, activations, basis, core_at, pieces=(1, 3, 4)):
     tokens, depth = activations.shape
     ranks = basis.shape[1] // 2
-    tile = depth // steps
-
-    def kernel(place_ref, a_ref, b_ref, other_ref, own_ref):
+    unit = depth // sum(pieces)
+    ends = [unit * sum(pieces[: k + 1]) for k in range(len(pieces))]
+    spans = [slice(end - unit * n, end) for end, n in zip(ends, pieces)]
+
+    def kernel(place_ref, a_hbm, b_hbm, other_ref, own_ref, a_ref, b_ref, total_ref, sems):
         core = place_ref[core_at]
-        for o_ref, half in ((other_ref, 1 - core), (own_ref, core)):
-            columns = pl.ds(pl.multiple_of(half * ranks, ranks), ranks)
-            part = jnp.dot(a_ref[...], b_ref[:, columns], preferred_element_type=jnp.float32)
-
-            @pl.when(pl.program_id(0) == 0)
-            def _():
-                o_ref[...] = part
-
-            @pl.when(pl.program_id(0) > 0)
-            def _():
-                o_ref[...] += part
-
-    half = shape(tokens, ranks, jnp.float32)
+        copies = []
+        for k, span in enumerate(spans):
+            copies.append(
+                (
+                    pltpu.make_async_copy(a_hbm.at[:, span], a_ref.at[:, span], sems.at[2 * k]),
+                    pltpu.make_async_copy(b_hbm.at[span, :], b_ref.at[span, :], sems.at[2 * k + 1]),
+                )
+            )
+        for pair in copies:
+            for copy in pair:
+                copy.start()
+        for k, (span, pair) in enumerate(zip(spans, copies)):
+            for copy in pair:
+                copy.wait()
+            for o_ref, half in ((total_ref, 1 - core), (own_ref, core)):
+                columns = pl.ds(pl.multiple_of(half * ranks, ranks), ranks)
+                part = jnp.dot(
+                    a_ref[:, span], b_ref[span, columns], preferred_element_type=jnp.float32
+                )
+                if k:
+                    part = o_ref[...] + part
+                if k == len(spans) - 1 and o_ref is total_ref:
+                    other_ref[...] = part.astype(other_ref.dtype)
+                else:
+                    o_ref[...] = part
+
     return call(
         kernel,
         "rank_halves",
-        [half, half],
-        [
-            pl.BlockSpec((tokens, tile), lambda k, p: (0, k)),
-            pl.BlockSpec((tile, 2 * ranks), lambda k, p: (k, 0)),
-        ],
-        16,
+        [shape(tokens, ranks, jnp.bfloat16), shape(tokens, ranks, jnp.float32)],
+        [pl.BlockSpec(memory_space=pl.ANY)] * 2,
+        24,
         4 * tokens * depth * ranks,
         2 * (tokens + 2 * ranks) * depth + 8 * tokens * ranks,
-        grid=(steps,),
+        scratch=[
+            pltpu.VMEM((tokens, depth), activations.dtype),
+            pltpu.VMEM((depth, 2 * ranks), basis.dtype),
+            pltpu.VMEM((tokens, ranks), jnp.float32),
+            pltpu.SemaphoreType.DMA((2 * len(pieces),)),
+        ],
     )(place, activations, basis)
 
 
@@ -195,7 +212,7 @@
     )(place, grads, *got, *rank_own, *rank_got)
 
 
-def moments(place, terms, masked, moment1, moment2, mask_at, core_at, steps=4):
+def moments(place, terms, masked, moment1, moment2, mask_at, core_at, steps=2):
     owned, ranks = moment1.shape
     rows = owned // steps
     count = len(terms)
@@ -228,7 +245,7 @@
     )(place, *terms, masked, moment1, moment2)
 
 
-def update_rows(place, normed, normed_other, basis, core_at, steps=8):
+def update_rows(place, normed, normed_other, basis, core_at, steps=4):
     owned, ranks = normed.shape
     width = basis.shape[0]
     tile = width // steps
@@ -268,7 +285,11 @@
     along_y = [(i, i ^ 2) for i in range(shards)]
     along_x = [(i, i ^ 1) for i in range(shards)]
     outer = [(i, i ^ 4) for i in range(shards)]
-    inner = [(i, i ^ 12 if 4 <= i < shards - 4 else i) for i in range(shards)]
+    inner = [
+        (2 * i + k, 2 * (i ^ 12) + k if 4 <= i < shards - 4 else 2 * i + 1 - k)
+        for i in range(shards)
+        for k in range(2)
+    ]
     cores = [(0, 1), (1, 0)]
 
     order = [
@@ -287,18 +308,15 @@
     x_at, core_at, mid_at = range(2 * planes, 2 * planes + 3)
 
     wide = 2 * owned
-    split = tokens * 3 // 4
     grads, basis_hbm = (pltpu.with_memory_space_constraint(a, pltpu.HBM) for a in (out_grads, basis))
-    early, late = take(place, grads, [(0, 0, split), (0, split, tokens - split)], wide)
-    activations, early, late = lax.optimization_barrier((activations, early, late))
-    early = lax.ppermute(early, "dp", along_y)
-    late = lax.ppermute(late, "dp", along_y)
+    (mine,) = take(place, grads, [(0, 0, tokens)], wide)
+    activations, mine = lax.optimization_barrier((activations, mine))
+    near = lax.ppermute(mine, "dp", along_y)
 
     activations = pltpu.with_memory_space_constraint(activations, pltpu.HBM)
     other, own = rank_halves(place, activations, basis_hbm, core_at)
-    other, own, early = lax.optimization_barrier((other, own, early))
+    other, own, near = lax.optimization_barrier((other, own, near))
     arrived = lax.ppermute(other, "mp", cores)
-    own, late = lax.optimization_barrier((own, late))
     half = added(place, [own, arrived], jnp.bfloat16)
     half_far = lax.ppermute(half, "dp", along_y)
     half_other = lax.ppermute(half, "mp", cores)
@@ -307,7 +325,7 @@
     half_far, *rest = lax.optimization_barrier((half_far, *rest))
     half_far_other = lax.ppermute(half_far, "mp", cores)
     rank_own, rank_got = (half, half_other), (half_far, half_far_other)
-    got = [[early, late]] + [[lax.ppermute(mine, "dp", along_y)] for mine in rest]
+    got = [[near]] + [[lax.ppermute(mine, "dp", along_y)] for mine in rest]
 
     sums = []
     for c in range(planes):
@@ -316,15 +334,16 @@
         )
         sums.append([keep, lax.ppermute(send, "dp", along_x)])
 
-    def hop(terms, pairs, *masked):
-        return lax.ppermute(added(place, terms, jnp.bfloat16, masked, mid_at), "dp", pairs)
+    def hop(terms, axes, pairs, *masked):
+        return lax.ppermute(added(place, terms, jnp.bfloat16, masked, mid_at), axes, pairs)
 
     first, second, third, final = sums
-    out1 = hop(first, outer)
-    out2 = hop(second, outer)
-    in2 = hop([*first, out1], inner)
-    out3 = hop(third, outer, in2)
-    in3 = hop([*second, out2], inner)
+    out1 = hop(first, "dp", outer)
+    out2 = hop(second, "dp", outer)
+    in2 = hop([*first, out1], ("dp", "mp"), inner)
+    out3 = hop(third, "dp", outer, in2)
+    place, _ = lax.optimization_barrier((place, third[1]))
+    in3 = hop([*second, out2], ("dp", "mp"), inner)
 
     new_first, new_second, normed = moments(
         place, [*final, out3], in3, moment1, moment2, mid_at, core_at

time: 108 us -> 105 us (0.972)
  Pallas kernels: 38.4 us -> 35.7 us
  waiting for transfers between devices: 41.9 us -> 44.5 us
  starting transfers between devices: 26.2 us -> 23.9 us
    ppermute x10 -> x9, waiting for transfers between devices: 21.8 us -> 25.3 us  [the longest x3 12.1 us: staged(): got = [[near]] + [[lax.ppermute(mine, 'dp', along_y)] for mine in rest]]
    ppermute x10 -> x9, starting transfers between devices: 18.5 us -> 15 us  [the longest x5 7.18 us: hop(): lax.ppermute(added(place, terms, jnp.bfloat16, masked, mid_at), axes, pairs)]
    ppermute x4, waiting for transfers between devices: 7.79 us -> 4.89 us  [staged(): sums.append([keep, lax.ppermute(send, 'dp', along_x)])]
    ppermute x1, waiting for transfers between devices: 0.01 us -> 1.91 us  [staged(): arrived = lax.ppermute(other, 'mp', cores)]
    pallas_call x1, Pallas kernels: 9.25 us -> 7.61 us  [rank_halves(): call(kernel, 'rank_halves', [shape(tokens, ranks, jnp.bfloat16), shape(to...]
  transfers between devices with their start and end apart: 19 -> 18, of which waited for: 12 -> 13; matrix products, arithmetic and copies ran while one was open for 0% -> 0% of each run, Pallas kernels for 24% -> 23%
where the time goes in v3:
time: 105 us
  waiting for transfers between devices  44.5 us (42%)
  Pallas kernels  35.7 us (34%)
  starting transfers between devices  23.9 us (23%)
    ppermute x3, waiting for transfers between devices, staged(): got = [[near]] + [[lax.ppermute(mine, 'dp', along_y)] for mine in rest]  12.1 us
    pallas_call x4, Pallas kernels, partial_sums(): call(kernel, 'partial_sums', [shape(owned, 2 * ranks, jnp.bfloat16), shap...  11.5 us
    ppermute x1, waiting for transfers between devices, staged(): half_far = lax.ppermute(half, 'dp', along_y)  10.3 us
    ppermute x5, waiting for transfers between devices, hop(): lax.ppermute(added(place, terms, jnp.bfloat16, masked, mid_at), axes, pairs)  8.91 us
    pallas_call x1, Pallas kernels, rank_halves(): call(kernel, 'rank_halves', [shape(tokens, ranks, jnp.bfloat16), shape(to...  7.61 us
    ppermute x5, starting transfers between devices, hop(): lax.ppermute(added(place, terms, jnp.bfloat16, masked, mid_at), axes, pairs)  7.18 us
    ppermute x4, starting transfers between devices, staged(): sums.append([keep, lax.ppermute(send, 'dp', along_x)])  7.08 us
    pallas_call x1, Pallas kernels, update_rows(): call(kernel, 'update_rows', [jax.ShapeDtypeStruct((2, owned, width), jnp....  6.71 us
  transfers between devices with their start and end apart: 18, of which 13 were waited for; matrix products, arithmetic and copies ran while one was open for 0% of the time, Pallas kernels for 23%

profile of v3, /device:TPU:0, one launch (start us, length us, event | category | flops | bytes accessed | tf_op | source)
XLA Modules:
  0.0 105.0 jit_solution(17922606375604686694)
XLA Ops:
  2.4 3.0 %collective-permute-start = (bf16[512,512]{1,0:T(8,128)(2,1)S(1)}, bf16[512,512]{1,0:T(8,128)(2,1)S(1)}, u32[]{:S(2)}, u32[]{:S(2)}) collective-permute-start(bf16[512,512]{1,0:T(8,128)(2,1)S(1)} %take.2), channel_id=1, source_target_pairs={{0,4},{2,6},{4,0},{6,2},{8,12},{10,14},{12,8},{14,10},{16,20},{18,... | collective-permute-start | bytes 1572872 | tf_op jit(solution)/shard_map/ppermute | solution.py:314
  5.4 7.6 %rank_halves.1 = (bf16[512,512]{1,0:T(8,128)(2,1)S(1)}, f32[512,512]{1,0:T(8,128)S(1)}) custom-call(s32[11]{0:T(128)S(1)} %stack.51.place_ref, bf16[512,4096]{1,0:T(8,128)(2,1)} %a_hbm, bf16[4096,1024]{1,0:T(8,128)(2,1)} %b_ref.1), custom_call_target="tpu_custom_call" | custom-call | flops 4294967296 | bytes 14680064 | tf_op jit(solution)/shard_map/rank_halves/pallas_call | solution.py:137
  13.1 4.3 %collective-permute-done.refs_0_ = bf16[512,512]{1,0:T(8,128)(2,1)S(1)} collective-permute-done((bf16[512,512]{1,0:T(8,128)(2,1)S(1)}, bf16[512,512]{1,0:T(8,128)(2,1)S(1)}, u32[]{:S(2)}, u32[]{:S(2)}) %collective-permute-start) | collective-permute-done | bytes 524320 | tf_op jit(solution)/shard_map/ppermute | solution.py:314
  17.4 1.9 %collective-permute-done.1.refs_1_ = bf16[512,512]{1,0:T(8,128)(2,1)S(1)} collective-permute-done((bf16[512,512]{1,0:T(8,128)(2,1)S(1)}, bf16[512,512]{1,0:T(8,128)(2,1)S(1)}, u32[]{:S(2)}, u32[]{:S(2)}) %collective-permute-start.1) | collective-permute-done | bytes 524320 | tf_op jit(solution)/shard_map/ppermute | solution.py:319
  19.9 1.8 %collective-permute-start.2 = (bf16[512,512]{1,0:T(8,128)(2,1)S(1)}, bf16[512,512]{1,0:T(8,128)(2,1)S(1)}, u32[]{:S(2)}, u32[]{:S(2)}) collective-permute-start(bf16[512,512]{1,0:T(8,128)(2,1)S(1)} %added.6.refs_1_), channel_id=1, source_target_pairs={{0,4},{2,6},{4,0},{6,2},{8,12},{10,14},{12,8},{14,10},{16,20},{18,... | collective-permute-start | bytes 1572872 | tf_op jit(solution)/shard_map/ppermute | solution.py:321
  21.7 1.9 %take.3 = (bf16[512,512]{1,0:T(8,128)(2,1)S(1)}, bf16[512,512]{1,0:T(8,128)(2,1)S(1)}, bf16[512,512]{1,0:T(8,128)(2,1)S(1)}) custom-call(s32[11]{0:T(128)S(1)} %stack.51.place_ref, bf16[512,4096]{1,0:T(8,128)(2,1)} %g_ref.11), custom_call_target="tpu_custom_call" | custom-call | bytes 3145728 | tf_op jit(solution)/shard_map/take/pallas_call | solution.py:90
  23.7 10.3 %collective-permute-done.2.refs_3_ = bf16[512,512]{1,0:T(8,128)(2,1)S(1)} collective-permute-done((bf16[512,512]{1,0:T(8,128)(2,1)S(1)}, bf16[512,512]{1,0:T(8,128)(2,1)S(1)}, u32[]{:S(2)}, u32[]{:S(2)}) %collective-permute-start.2) | collective-permute-done | bytes 524320 | tf_op jit(solution)/shard_map/ppermute | solution.py:321
  35.9 2.9 %partial_sums.6 = (bf16[256,1024]{1,0:T(8,128)(2,1)S(1)}, f32[256,1024]{1,0:T(8,128)S(1)}) custom-call(s32[11]{0:T(128)S(1)} %stack.51.place_ref, bf16[512,4096]{1,0:T(8,128)(2,1)} %g_ref.11, bf16[512,512]{1,0:T(8,128)(2,1)S(1)} %collective-permute-done.refs_0_, bf16[512,512]{1,0:T(8,128)(2,1)S(1)} %added.6.refs_1_, ...), custom_call_target="tpu_custom_call" | custom-call | flops 1073741824 | bytes 4718592 | tf_op jit(solution)/shard_map/partial_sums/pallas_call | solution.py:202
  42.0 6.6 %collective-permute-done.13.refs_0_ = bf16[512,512]{1,0:T(8,128)(2,1)S(1)} collective-permute-done((bf16[512,512]{1,0:T(8,128)(2,1)S(1)}, bf16[512,512]{1,0:T(8,128)(2,1)S(1)}, u32[]{:S(2)}, u32[]{:S(2)}) %collective-permute-start.13) | collective-permute-done | bytes 524320 | tf_op jit(solution)/shard_map/ppermute | solution.py:328
  48.7 2.9 %partial_sums.7 = (bf16[256,1024]{1,0:T(8,128)(2,1)S(1)}, f32[256,1024]{1,0:T(8,128)S(1)}) custom-call(s32[11]{0:T(128)S(1)} %stack.51.place_ref, bf16[512,4096]{1,0:T(8,128)(2,1)} %g_ref.11, bf16[512,512]{1,0:T(8,128)(2,1)S(1)} %collective-permute-done.13.refs_0_, bf16[512,512]{1,0:T(8,128)(2,1)S(1)} %added.6.refs_1_, ...), custom_call_target="tpu_custom_call" | custom-call | flops 1073741824 | bytes 4718592 | tf_op jit(solution)/shard_map/partial_sums/pallas_call | solution.py:202
  51.5 1.8 %collective-permute-start.14 = (bf16[256,1024]{1,0:T(8,128)(2,1)S(1)}, bf16[256,1024]{1,0:T(8,128)(2,1)S(1)}, u32[]{:S(2)}, u32[]{:S(2)}) collective-permute-start(bf16[256,1024]{1,0:T(8,128)(2,1)S(1)} %get-tuple-element.53), channel_id=1, source_target_pairs={{0,2},{2,0},{4,6},{6,4},{8,10},{10,8},{12,14},{14,12},{16,18},{18,... | collective-permute-start | bytes 1572872 | tf_op jit(solution)/shard_map/ppermute | solution.py:335
  57.1 2.8 %collective-permute-done.3.refs_0_ = bf16[512,512]{1,0:T(8,128)(2,1)S(1)} collective-permute-done((bf16[512,512]{1,0:T(8,128)(2,1)S(1)}, bf16[512,512]{1,0:T(8,128)(2,1)S(1)}, u32[]{:S(2)}, u32[]{:S(2)}) %collective-permute-start.3) | collective-permute-done | bytes 524320 | tf_op jit(solution)/shard_map/ppermute | solution.py:328
  59.9 2.9 %partial_sums.4 = (bf16[256,1024]{1,0:T(8,128)(2,1)S(1)}, f32[256,1024]{1,0:T(8,128)S(1)}) custom-call(s32[11]{0:T(128)S(1)} %stack.51.place_ref, bf16[512,4096]{1,0:T(8,128)(2,1)} %g_ref.11, bf16[512,512]{1,0:T(8,128)(2,1)S(1)} %collective-permute-done.3.refs_0_, bf16[512,512]{1,0:T(8,128)(2,1)S(1)} %added.6.refs_1_, ...), custom_call_target="tpu_custom_call" | custom-call | flops 1073741824 | bytes 4718592 | tf_op jit(solution)/shard_map/partial_sums/pallas_call | solution.py:202
  65.4 1.9 %collective-permute-start.15 = (bf16[256,1024]{1,0:T(8,128)(2,1)S(1)}, bf16[256,1024]{1,0:T(8,128)(2,1)S(1)}, u32[]{:S(2)}, u32[]{:S(2)}) collective-permute-start(bf16[256,1024]{1,0:T(8,128)(2,1)S(1)} %added.10), channel_id=1, source_target_pairs={{0,8},{2,10},{4,12},{6,14},{8,0},{10,2},{12,4},{14,6},{16,24},{18,... | collective-permute-start | bytes 1572872 | tf_op jit(solution)/shard_map/ppermute | solution.py:338
  68.1 2.7 %collective-permute-done.7.refs_0_ = bf16[512,512]{1,0:T(8,128)(2,1)S(1)} collective-permute-done((bf16[512,512]{1,0:T(8,128)(2,1)S(1)}, bf16[512,512]{1,0:T(8,128)(2,1)S(1)}, u32[]{:S(2)}, u32[]{:S(2)}) %collective-permute-start.7) | collective-permute-done | bytes 524320 | tf_op jit(solution)/shard_map/ppermute | solution.py:328
  70.8 2.9 %partial_sums.5 = (bf16[256,1024]{1,0:T(8,128)(2,1)S(1)}, f32[256,1024]{1,0:T(8,128)S(1)}) custom-call(s32[11]{0:T(128)S(1)} %stack.51.place_ref, bf16[512,4096]{1,0:T(8,128)(2,1)} %g_ref.11, bf16[512,512]{1,0:T(8,128)(2,1)S(1)} %collective-permute-done.7.refs_0_, bf16[512,512]{1,0:T(8,128)(2,1)S(1)} %added.6.refs_1_, ...), custom_call_target="tpu_custom_call" | custom-call | flops 1073741824 | bytes 4718592 | tf_op jit(solution)/shard_map/partial_sums/pallas_call | solution.py:202
  73.7 1.8 %collective-permute-start.8 = (bf16[256,1024]{1,0:T(8,128)(2,1)S(1)}, bf16[256,1024]{1,0:T(8,128)(2,1)S(1)}, u32[]{:S(2)}, u32[]{:S(2)}) collective-permute-start(bf16[256,1024]{1,0:T(8,128)(2,1)S(1)} %get-tuple-element.46), channel_id=1, source_target_pairs={{0,2},{2,0},{4,6},{6,4},{8,10},{10,8},{12,14},{14,12},{16,18},{18,... | collective-permute-start | bytes 1572872 | tf_op jit(solution)/shard_map/ppermute | solution.py:335
  76.0 2.1 %collective-permute-done.15.refs_2_ = bf16[256,1024]{1,0:T(8,128)(2,1)S(1)} collective-permute-done((bf16[256,1024]{1,0:T(8,128)(2,1)S(1)}, bf16[256,1024]{1,0:T(8,128)(2,1)S(1)}, u32[]{:S(2)}, u32[]{:S(2)}) %collective-permute-start.15) | collective-permute-done | bytes 524320 | tf_op jit(solution)/shard_map/ppermute | solution.py:338
  79.7 3.5 %collective-permute-start.12 = (bf16[256,1024]{1,0:T(8,128)(2,1)S(1)}, bf16[256,1024]{1,0:T(8,128)(2,1)S(1)}, u32[]{:S(2)}, u32[]{:S(2)}) collective-permute-start(bf16[256,1024]{1,0:T(8,128)(2,1)S(1)} %added.9), channel_id=1, source_target_pairs={{0,8},{2,10},{4,12},{6,14},{8,0},{10,2},{12,4},{14,6},{16,24},{18,... | collective-permute-start | bytes 1572872 | tf_op jit(solution)/shard_map/ppermute | solution.py:338
  83.2 4.1 %collective-permute-done.8.refs_1_ = bf16[256,1024]{1,0:T(8,128)(2,1)S(1)} collective-permute-done((bf16[256,1024]{1,0:T(8,128)(2,1)S(1)}, bf16[256,1024]{1,0:T(8,128)(2,1)S(1)}, u32[]{:S(2)}, u32[]{:S(2)}) %collective-permute-start.8) | collective-permute-done | bytes 524320 | tf_op jit(solution)/shard_map/ppermute | solution.py:335
  87.3 6.8 %collective-permute-done.12.refs_2_ = bf16[256,1024]{1,0:T(8,128)(2,1)S(1)} collective-permute-done((bf16[256,1024]{1,0:T(8,128)(2,1)S(1)}, bf16[256,1024]{1,0:T(8,128)(2,1)S(1)}, u32[]{:S(2)}, u32[]{:S(2)}) %collective-permute-start.12) | collective-permute-done | bytes 524320 | tf_op jit(solution)/shard_map/ppermute | solution.py:338
  94.1 2.3 %moments.1 = (f32[256,1024]{1,0:T(8,128)}, f32[256,1024]{1,0:T(8,128)}, bf16[256,1024]{1,0:T(8,128)(2,1)S(1)}) custom-call(s32[11]{0:T(128)S(1)} %stack.51.place_ref, f32[256,1024]{1,0:T(8,128)S(1)} %get-tuple-element.45.refs_0_, bf16[256,1024]{1,0:T(8,128)(2,1)S(1)} %collective-permute-done.8.refs_1_, ...), custom_call_target="tpu_custom_call" | custom-call | flops 5242880 | bytes 7340032 | tf_op jit(solution)/shard_map/moments/pallas_call | solution.py:235
  96.4 1.9 %collective-permute-done.17.m_ref = bf16[256,1024]{1,0:T(8,128)(2,1)S(1)} collective-permute-done((bf16[256,1024]{1,0:T(8,128)(2,1)S(1)}, bf16[256,1024]{1,0:T(8,128)(2,1)S(1)}, u32[]{:S(2)}, u32[]{:S(2)}) %collective-permute-start.17) | collective-permute-done | bytes 524320 | tf_op jit(solution)/shard_map/ppermute | solution.py:351
  98.3 6.7 %update_rows.1 = bf16[2,256,4096]{2,1,0:T(8,128)(2,1)} custom-call(s32[11]{0:T(128)S(1)} %stack.51.place_ref, bf16[256,1024]{1,0:T(8,128)(2,1)S(1)} %get-tuple-element.56.n_ref, bf16[256,1024]{1,0:T(8,128)(2,1)S(1)} %collective-permute-done.17.m_ref, bf16[4096,1024]{1,0:T(8,128)(2,1)S(1)} %bitcast.12), custom_call_target="tpu_custom_call" | custom-call | flops 4294967296 | bytes 13631488 | tf_op jit(solution)/shard_map/update_rows/pallas_call | solution.py:263
  (37 shorter events, 16.8 us)
Async XLA Ops:
  2.4 15.0 %collective-permute-start = (bf16[512,512]{1,0:T(8,128)(2,1)S(1)}, bf16[512,512]{1,0:T(8,128)(2,1)S(1)}, u32[]{:S(2)}, u32[]{:S(2)}) collective-permute-start(bf16[512,512]{1,0:T(8,128)(2,1)S(1)} %take.2), channel_id=1, source_target_pairs={{0,4},{2,6},{4,0},{6,2},{8,12},{10,14},{12,8},{14,10},{16,20},{18,... | collective-permute-start | bytes 1572872 | tf_op jit(solution)/shard_map/ppermute | solution.py:314
  17.4 1.9 %collective-permute-start.1 = (bf16[512,512]{1,0:T(8,128)(2,1)S(1)}, bf16[512,512]{1,0:T(8,128)(2,1)S(1)}, u32[]{:S(2)}, u32[]{:S(2)}) collective-permute-start(bf16[512,512]{1,0:T(8,128)(2,1)S(1)} %get-tuple-element.35), channel_id=1, source_target_pairs={{0,1},{1,0},{2,3},{3,2},{4,5},{5,4},{6,7},{7,6},{8,9},{9,8},{10,11... | collective-permute-start | bytes 1572872 | tf_op jit(solution)/shard_map/ppermute | solution.py:319
  19.9 14.0 %collective-permute-start.2 = (bf16[512,512]{1,0:T(8,128)(2,1)S(1)}, bf16[512,512]{1,0:T(8,128)(2,1)S(1)}, u32[]{:S(2)}, u32[]{:S(2)}) collective-permute-start(bf16[512,512]{1,0:T(8,128)(2,1)S(1)} %added.6.refs_1_), channel_id=1, source_target_pairs={{0,4},{2,6},{4,0},{6,2},{8,12},{10,14},{12,8},{14,10},{16,20},{18,... | collective-permute-start | bytes 1572872 | tf_op jit(solution)/shard_map/ppermute | solution.py:321
  21.7 14.0 %collective-permute-start.4 = (bf16[512,512]{1,0:T(8,128)(2,1)S(1)}, bf16[512,512]{1,0:T(8,128)(2,1)S(1)}, u32[]{:S(2)}, u32[]{:S(2)}) collective-permute-start(bf16[512,512]{1,0:T(8,128)(2,1)S(1)} %added.6.refs_1_), channel_id=1, source_target_pairs={{0,1},{1,0},{2,3},{3,2},{4,5},{5,4},{6,7},{7,6},{8,9},{9,8},{10,11... | collective-permute-start | bytes 1572872 | tf_op jit(solution)/shard_map/ppermute | solution.py:322
  33.9 1.9 %collective-permute-start.5 = (bf16[512,512]{1,0:T(8,128)(2,1)S(1)}, bf16[512,512]{1,0:T(8,128)(2,1)S(1)}, u32[]{:S(2)}, u32[]{:S(2)}) collective-permute-start(bf16[512,512]{1,0:T(8,128)(2,1)S(1)} %collective-permute-done.2.refs_3_), channel_id=1, source_target_pairs={{0,1},{1,0},{2,3},{3,2},{4,5},{5,4},{6,7},{7,6},{8,9},{9,8},{10,11... | collective-permute-start | bytes 1572872 | tf_op jit(solution)/shard_map/ppermute | solution.py:326
  34.0 14.7 %collective-permute-start.13 = (bf16[512,512]{1,0:T(8,128)(2,1)S(1)}, bf16[512,512]{1,0:T(8,128)(2,1)S(1)}, u32[]{:S(2)}, u32[]{:S(2)}) collective-permute-start(bf16[512,512]{1,0:T(8,128)(2,1)S(1)} %get-tuple-element.51), channel_id=1, source_target_pairs={{0,4},{2,6},{4,0},{6,2},{8,12},{10,14},{12,8},{14,10},{16,20},{18,... | collective-permute-start | bytes 1572872 | tf_op jit(solution)/shard_map/ppermute | solution.py:328
  38.7 14.6 %collective-permute-start.9 = (bf16[256,1024]{1,0:T(8,128)(2,1)S(1)}, bf16[256,1024]{1,0:T(8,128)(2,1)S(1)}, u32[]{:S(2)}, u32[]{:S(2)}) collective-permute-start(bf16[256,1024]{1,0:T(8,128)(2,1)S(1)} %get-tuple-element.50), channel_id=1, source_target_pairs={{0,2},{2,0},{4,6},{6,4},{8,10},{10,8},{12,14},{14,12},{16,18},{18,... | collective-permute-start | bytes 1572872 | tf_op jit(solution)/shard_map/ppermute | solution.py:335
  40.5 19.4 %collective-permute-start.3 = (bf16[512,512]{1,0:T(8,128)(2,1)S(1)}, bf16[512,512]{1,0:T(8,128)(2,1)S(1)}, u32[]{:S(2)}, u32[]{:S(2)}) collective-permute-start(bf16[512,512]{1,0:T(8,128)(2,1)S(1)} %get-tuple-element.40), channel_id=1, source_target_pairs={{0,4},{2,6},{4,0},{6,2},{8,12},{10,14},{12,8},{14,10},{16,20},{18,... | collective-permute-start | bytes 1572872 | tf_op jit(solution)/shard_map/ppermute | solution.py:328
  51.5 13.2 %collective-permute-start.14 = (bf16[256,1024]{1,0:T(8,128)(2,1)S(1)}, bf16[256,1024]{1,0:T(8,128)(2,1)S(1)}, u32[]{:S(2)}, u32[]{:S(2)}) collective-permute-start(bf16[256,1024]{1,0:T(8,128)(2,1)S(1)} %get-tuple-element.53), channel_id=1, source_target_pairs={{0,2},{2,0},{4,6},{6,4},{8,10},{10,8},{12,14},{14,12},{16,18},{18,... | collective-permute-start | bytes 1572872 | tf_op jit(solution)/shard_map/ppermute | solution.py:335
  54.0 13.3 %collective-permute-start.10 = (bf16[256,1024]{1,0:T(8,128)(2,1)S(1)}, bf16[256,1024]{1,0:T(8,128)(2,1)S(1)}, u32[]{:S(2)}, u32[]{:S(2)}) collective-permute-start(bf16[256,1024]{1,0:T(8,128)(2,1)S(1)} %added.7), channel_id=1, source_target_pairs={{0,8},{2,10},{4,12},{6,14},{8,0},{10,2},{12,4},{14,6},{16,24},{18,... | collective-permute-start | bytes 1572872 | tf_op jit(solution)/shard_map/ppermute | solution.py:338
  55.6 15.2 %collective-permute-start.7 = (bf16[512,512]{1,0:T(8,128)(2,1)S(1)}, bf16[512,512]{1,0:T(8,128)(2,1)S(1)}, u32[]{:S(2)}, u32[]{:S(2)}) collective-permute-start(bf16[512,512]{1,0:T(8,128)(2,1)S(1)} %get-tuple-element.44), channel_id=1, source_target_pairs={{0,4},{2,6},{4,0},{6,2},{8,12},{10,14},{12,8},{14,10},{16,20},{18,... | collective-permute-start | bytes 1572872 | tf_op jit(solution)/shard_map/ppermute | solution.py:328
  62.8 13.2 %collective-permute-start.6 = (bf16[256,1024]{1,0:T(8,128)(2,1)S(1)}, bf16[256,1024]{1,0:T(8,128)(2,1)S(1)}, u32[]{:S(2)}, u32[]{:S(2)}) collective-permute-start(bf16[256,1024]{1,0:T(8,128)(2,1)S(1)} %get-tuple-element.42), channel_id=1, source_target_pairs={{0,2},{2,0},{4,6},{6,4},{8,10},{10,8},{12,14},{14,12},{16,18},{18,... | collective-permute-start | bytes 1572872 | tf_op jit(solution)/shard_map/ppermute | solution.py:335
  65.4 12.7 %collective-permute-start.15 = (bf16[256,1024]{1,0:T(8,128)(2,1)S(1)}, bf16[256,1024]{1,0:T(8,128)(2,1)S(1)}, u32[]{:S(2)}, u32[]{:S(2)}) collective-permute-start(bf16[256,1024]{1,0:T(8,128)(2,1)S(1)} %added.10), channel_id=1, source_target_pairs={{0,8},{2,10},{4,12},{6,14},{8,0},{10,2},{12,4},{14,6},{16,24},{18,... | collective-permute-start | bytes 1572872 | tf_op jit(solution)/shard_map/ppermute | solution.py:338
  67.3 31.0 %slice-start = ((s8[8388608]{0:T(1024)(128)(4,1)}), s8[4194304]{0:T(1024)(128)(4,1)S(1)}, s32[]{:S(2)}) async-start(s8[8388608]{0:T(1024)(128)(4,1)} %bitcast.11), calls=%async_computation | async-start | bytes 8388608
  68.0 10.9 %collective-permute-start.11 = (bf16[256,1024]{1,0:T(8,128)(2,1)S(1)}, bf16[256,1024]{1,0:T(8,128)(2,1)S(1)}, u32[]{:S(2)}, u32[]{:S(2)}) collective-permute-start(bf16[256,1024]{1,0:T(8,128)(2,1)S(1)} %added.8), channel_id=1, source_target_pairs={{0,1},{1,0},{2,3},{3,2},{4,5},{5,4},{6,7},{7,6},{8,16},{9,17},{10,... | collective-permute-start | bytes 1572872 | tf_op jit(solution)/shard_map/ppermute | solution.py:338
  73.6 20.4 %copy-start = (f32[256,1024]{1,0:T(8,128)S(1)}, f32[256,1024]{1,0:T(8,128)}, u32[]{:S(2)}) copy-start(f32[256,1024]{1,0:T(8,128)} %refs_4_.1) | copy-start | bytes 3145732
  73.6 20.4 %copy-start.1 = (f32[256,1024]{1,0:T(8,128)S(1)}, f32[256,1024]{1,0:T(8,128)}, u32[]{:S(2)}) copy-start(f32[256,1024]{1,0:T(8,128)} %refs_5_.1) | copy-start | bytes 3145732
  73.7 24.7 %slice-start.1 = ((s8[8388608]{0:T(1024)(128)(4,1)}), s8[4194304]{0:T(1024)(128)(4,1)S(1)}, s32[]{:S(2)}) async-start(s8[8388608]{0:T(1024)(128)(4,1)} %bitcast.11), calls=%async_computation.1 | async-start | bytes 8388608
  73.7 13.6 %collective-permute-start.8 = (bf16[256,1024]{1,0:T(8,128)(2,1)S(1)}, bf16[256,1024]{1,0:T(8,128)(2,1)S(1)}, u32[]{:S(2)}, u32[]{:S(2)}) collective-permute-start(bf16[256,1024]{1,0:T(8,128)(2,1)S(1)} %get-tuple-element.46), channel_id=1, source_target_pairs={{0,2},{2,0},{4,6},{6,4},{8,10},{10,8},{12,14},{14,12},{16,18},{18,... | collective-permute-start | bytes 1572872 | tf_op jit(solution)/shard_map/ppermute | solution.py:335
  78.9 8.4 %collective-permute-start.16 = (bf16[256,1024]{1,0:T(8,128)(2,1)S(1)}, bf16[256,1024]{1,0:T(8,128)(2,1)S(1)}, u32[]{:S(2)}, u32[]{:S(2)}) collective-permute-start(bf16[256,1024]{1,0:T(8,128)(2,1)S(1)} %added.11), channel_id=1, source_target_pairs={{0,1},{1,0},{2,3},{3,2},{4,5},{5,4},{6,7},{7,6},{8,16},{9,17},{10,... | collective-permute-start | bytes 1572872 | tf_op jit(solution)/shard_map/ppermute | solution.py:338
  79.7 14.4 %collective-permute-start.12 = (bf16[256,1024]{1,0:T(8,128)(2,1)S(1)}, bf16[256,1024]{1,0:T(8,128)(2,1)S(1)}, u32[]{:S(2)}, u32[]{:S(2)}) collective-permute-start(bf16[256,1024]{1,0:T(8,128)(2,1)S(1)} %added.9), channel_id=1, source_target_pairs={{0,8},{2,10},{4,12},{6,14},{8,0},{10,2},{12,4},{14,6},{16,24},{18,... | collective-permute-start | bytes 1572872 | tf_op jit(solution)/shard_map/ppermute | solution.py:338
  96.4 1.9 %collective-permute-start.17 = (bf16[256,1024]{1,0:T(8,128)(2,1)S(1)}, bf16[256,1024]{1,0:T(8,128)(2,1)S(1)}, u32[]{:S(2)}, u32[]{:S(2)}) collective-permute-start(bf16[256,1024]{1,0:T(8,128)(2,1)S(1)} %get-tuple-element.56.n_ref), channel_id=1, source_target_pairs={{0,1},{1,0},{2,3},{3,2},{4,5},{5,4},{6,7},{7,6},{8,9},{9,8},{10,11... | collective-permute-start | bytes 1572872 | tf_op jit(solution)/shard_map/ppermute | solution.py:351

commit v4 on v3

--- a/solution.py
+++ b/solution.py
@@ -51,7 +51,9 @@
     return pl.BlockSpec((rows, columns), lambda *_: (0, 0))
 
 
-def call(kernel, name, outs, specs, mib, flops, moved, out_specs=None, grid=(1,), scratch=()):
+def call(
+    kernel, name, outs, specs, mib, flops, moved, out_specs=None, grid=(1,), scratch=(), aliases=None
+):
     return pl.pallas_call(
         kernel,
         out_shape=outs,
@@ -62,31 +64,41 @@
             out_specs=[whole(*o.shape) for o in outs] if out_specs is None else out_specs,
             scratch_shapes=scratch,
         ),
+        input_output_aliases=aliases or {},
         compiler_params=pltpu.CompilerParams(vmem_limit_bytes=mib * 1024 * 1024),
         cost_estimate=pl.CostEstimate(flops=flops, bytes_accessed=moved, transcendentals=0),
         name=name,
     )
 
 
+def part(rows, columns, at):
+    return pl.BlockSpec((rows, columns), lambda *_: (at, 0))
+
+
 def shape(rows, columns, dtype):
     return jax.ShapeDtypeStruct((rows, columns), dtype)
 
 
-def take(place, grads, pieces, wide):
+def take(place, grads, pieces, owned):
     def kernel(place_ref, g_ref, *refs):
         outs, sems = refs[:-1], refs[-1]
         copies = []
-        for k, ((entry, first, rows), out) in enumerate(zip(pieces, outs)):
-            columns = pl.ds(pl.multiple_of(place_ref[entry] * wide, wide), wide)
-            copies.append(
-                pltpu.make_async_copy(g_ref.at[pl.ds(first, rows), columns], out, sems.at[k])
-            )
+        for k, ((entry, stride, first, rows), out) in enumerate(zip(pieces, outs)):
+            for side in range(2):
+                block = (place_ref[entry] + side * stride) * owned
+                copies.append(
+                    pltpu.make_async_copy(
+                        g_ref.at[pl.ds(first, rows), pl.ds(pl.multiple_of(block, owned), owned)],
+                        out.at[:, pl.ds(side * owned, owned)],
+                        sems.at[2 * k + side],
+                    )
+                )
         for copy in copies:
             copy.start()
         for copy in copies:
             copy.wait()
 
-    outs = [shape(rows, wide, grads.dtype) for _, _, rows in pieces]
+    outs = [shape(rows, 2 * owned, grads.dtype) for _, _, _, rows in pieces]
     return call(
         kernel,
         "take",
@@ -94,8 +106,8 @@
         [pl.BlockSpec(memory_space=pl.ANY)],
         8,
         0,
-        4 * wide * sum(rows for _, _, rows in pieces),
-        scratch=[pltpu.SemaphoreType.DMA((len(pieces),))],
+        8 * owned * sum(rows for _, _, _, rows in pieces),
+        scratch=[pltpu.SemaphoreType.DMA((2 * len(pieces),))],
     )(place, grads)
 
 
@@ -151,42 +163,67 @@
     )(place, activations, basis)
 
 
-def added(place, terms, dtype, masked=(), mask_at=None):
-    rows, columns = terms[0].shape
-    count = len(terms)
-
-    def kernel(place_ref, *refs):
-        total = refs[0][...].astype(jnp.float32)
-        for ref in refs[1:count]:
-            total += ref[...].astype(jnp.float32)
-        for ref in refs[count:-1]:
-            total += jnp.where(place_ref[mask_at] == 1, ref[...].astype(jnp.float32), 0.0)
-        refs[-1][...] = total.astype(dtype)
-
+def added(place, keep, at, parts, terms, masked, mask_at):
+    rows, ranks = keep.shape[0] // parts, keep.shape[1]
     operands = [*terms, *masked]
+    pieces = max([len(term) for term in operands])
+    height = rows // pieces
+    flat = [piece for term in operands for piece in term]
+
+    def kernel(place_ref, keep_ref, *refs):
+        for k in range(pieces):
+            here = slice(k * height, (k + 1) * height)
+            total, first = keep_ref[here, :], 0
+            for number, term in enumerate(operands):
+                own = refs[first : first + len(term)]
+                first += len(term)
+                value = own[k][...] if len(term) == pieces else own[0][here, :]
+                value = value.astype(jnp.float32)
+                if number >= len(terms):
+                    value = jnp.where(place_ref[mask_at] == 1, value, 0.0)
+                total = total + value
+            refs[-1][here, :] = total.astype(jnp.bfloat16)
+
     return call(
         kernel,
         "added",
-        [shape(rows, columns, dtype)],
-        [whole(rows, columns)] * len(operands),
+        [shape(rows, ranks, jnp.bfloat16)],
+        [part(rows, ranks, at)] + [whole(*piece.shape) for piece in flat],
         12,
-        rows * columns * len(operands),
-        4 * rows * columns * len(operands),
-    )(place, *operands)[0]
-
-
-def partial_sums(place, grads, got, rank_own, rank_got, block_at, x_at):
+        rows * ranks * len(operands),
+        4 * rows * ranks * len(operands),
+    )(place, keep, *flat)[0]
+
+
+def rounded(place, own, arrived):
+    def kernel(place_ref, a_ref, b_ref, o_ref):
+        o_ref[...] = (a_ref[...] + b_ref[...].astype(jnp.float32)).astype(jnp.bfloat16)
+
+    rows, columns = own.shape
+    return call(
+        kernel,
+        "rounded",
+        [shape(rows, columns, jnp.bfloat16)],
+        [whole(rows, columns)] * 2,
+        12,
+        rows * columns,
+        10 * rows * columns,
+    )(place, own, arrived)[0]
+
+
+def partial_sums(place, grads, got, rank_own, rank_got, theirs_at, ours_at, side_at, parts):
     tokens, ranks = rank_own[0].shape
     wide = got[0].shape[1]
     owned = wide // 2
     pieces = len(got)
-
-    def kernel(place_ref, g_ref, *refs):
-        got_refs, (t0_ref, t1_ref, u0_ref, u1_ref, send_ref, keep_ref) = refs[:pieces], refs[pieces:]
-        x = place_ref[x_at]
-        theirs = pl.ds(pl.multiple_of((1 - x) * owned, owned), owned)
-        ours = pl.ds(pl.multiple_of(x * owned, owned), owned)
-        mine = jnp.concatenate([g_ref[:, theirs], g_ref[:, ours]], axis=1)
+    rows = owned // parts
+
+    def kernel(place_ref, theirs_ref, ours_ref, *refs):
+        got_refs, (t0_ref, t1_ref, u0_ref, u1_ref, *send_refs, keep_ref) = refs[:pieces], refs[pieces:]
+        mine = jnp.concatenate([theirs_ref[...], ours_ref[...]], axis=1)
+        near = place_ref[side_at]
+        theirs = pl.ds(pl.multiple_of((1 - near) * owned, owned), owned)
+        ours = pl.ds(pl.multiple_of(near * owned, owned), owned)
         far = jnp.concatenate(
             [jnp.concatenate([r[:, theirs], r[:, ours]], axis=1) for r in got_refs], axis=0
         )
@@ -196,20 +233,24 @@
                 mine, t_ref[...], dims, preferred_element_type=jnp.float32
             ) + lax.dot_general(far, u_ref[...], dims, preferred_element_type=jnp.float32)
             columns = slice(side * ranks, (side + 1) * ranks)
-            send_ref[:, columns] = total[:owned].astype(send_ref.dtype)
+            for at, send_ref in enumerate(send_refs):
+                send_ref[:, columns] = total[at * rows : (at + 1) * rows].astype(send_ref.dtype)
             keep_ref[:, columns] = total[owned:]
 
     return call(
         kernel,
         "partial_sums",
-        [shape(owned, 2 * ranks, jnp.bfloat16), shape(owned, 2 * ranks, jnp.float32)],
-        [pl.BlockSpec((tokens, wide), lambda i, p: (0, p[block_at]))]
+        [shape(rows, 2 * ranks, jnp.bfloat16)] * parts + [shape(owned, 2 * ranks, jnp.float32)],
+        [
+            pl.BlockSpec((tokens, owned), lambda i, p: (0, p[theirs_at])),
+            pl.BlockSpec((tokens, owned), lambda i, p: (0, p[ours_at])),
+        ]
         + [whole(*g.shape) for g in got]
         + [whole(tokens, ranks)] * 4,
         20,
         8 * tokens * wide * ranks,
         4 * tokens * (wide + 2 * ranks) + 12 * owned * ranks,
-    )(place, grads, *got, *rank_own, *rank_got)
+    )(place, grads, grads, *got, *rank_own, *rank_got)
 
 
 def moments(place, terms, masked, moment1, moment2, mask_at, core_at, steps=2):
@@ -302,51 +343,83 @@
     blocks = [
         sum(jnp.where(z == p, order[p][c], 0) for p in range(planes)) for c in range(planes)
     ]
-    place = jnp.stack(
-        [b * 2 + 1 - y for b in blocks] + [b * 2 + y for b in blocks] + [x, core, mid]
-    ).astype(jnp.int32)
-    x_at, core_at, mid_at = range(2 * planes, 2 * planes + 3)
-
-    wide = 2 * owned
+    first_y = [c != 1 for c in range(planes)]
+    base = [b * 4 + ((1 - y) * 2 if f else 1 - x) for b, f in zip(blocks, first_y)]
+    ours = [b * 4 + y * 2 + x for b in blocks]
+    theirs = [b * 4 + (y * 2 + 1 - x if f else (1 - y) * 2 + x) for b, f in zip(blocks, first_y)]
+    place = jnp.stack([*base, *ours, *theirs, x, y, core, mid]).astype(jnp.int32)
+    ours_at, theirs_at = planes, 2 * planes
+    x_at, y_at, core_at, mid_at = range(3 * planes, 3 * planes + 4)
+
+    def piece(c, first=0, rows=tokens):
+        return c, 1 if first_y[c] else 2, first, rows
+
+    def raw(c, mine):
+        return lax.ppermute(mine, "dp", along_y if first_y[c] else along_x)
+
     grads, basis_hbm = (pltpu.with_memory_space_constraint(a, pltpu.HBM) for a in (out_grads, basis))
-    (mine,) = take(place, grads, [(0, 0, tokens)], wide)
-    activations, mine = lax.optimization_barrier((activations, mine))
-    near = lax.ppermute(mine, "dp", along_y)
+    early = take(place, grads, [piece(0), piece(1)], owned)
+    activations, *early = lax.optimization_barrier((activations, *early))
+    first, second = (raw(c, mine) for c, mine in enumerate(early))
 
     activations = pltpu.with_memory_space_constraint(activations, pltpu.HBM)
     other, own = rank_halves(place, activations, basis_hbm, core_at)
-    other, own, near = lax.optimization_barrier((other, own, near))
+    other, own, first, second = lax.optimization_barrier((other, own, first, second))
     arrived = lax.ppermute(other, "mp", cores)
-    half = added(place, [own, arrived], jnp.bfloat16)
-    half_far = lax.ppermute(half, "dp", along_y)
+    half = rounded(place, own, arrived)
+    half_y = lax.ppermute(half, "dp", along_y)
+    half_x = lax.ppermute(half, "dp", along_x)
     half_other = lax.ppermute(half, "mp", cores)
     place_later, _ = lax.optimization_barrier((place, half))
-    rest = take(place_later, grads, [(c, 0, tokens) for c in range(1, planes)], wide)
-    half_far, *rest = lax.optimization_barrier((half_far, *rest))
-    half_far_other = lax.ppermute(half_far, "mp", cores)
-    rank_own, rank_got = (half, half_other), (half_far, half_far_other)
-    got = [[near]] + [[lax.ppermute(mine, "dp", along_y)] for mine in rest]
-
-    sums = []
-    for c in range(planes):
-        send, keep = partial_sums(
-            place, grads, got[c], rank_own, rank_got, planes + c, x_at
+    rest = take(place_later, grads, [piece(c) for c in range(2, planes)], owned)
+    half_y, *rest = lax.optimization_barrier((half_y, *rest))
+    got = [[first], [second]] + [
+        [raw(c, mine)] for c, mine in enumerate(rest, 2)
+    ]
+    rank_own = (half, half_other)
+    rank_y = (half_y, lax.ppermute(half_y, "mp", cores))
+    rank_x = (half_x, lax.ppermute(half_x, "mp", cores))
+
+    parts = [2, 1, 1, 1]
+    keeps, arrivals, now = {}, {}, [place]
+
+    def then(result):
+        return result
+
+    def block(c):
+        *sends, keeps[c] = then(
+            partial_sums(
+                now[0],
+                grads,
+                got[c],
+                rank_own,
+                rank_y if first_y[c] else rank_x,
+                theirs_at + c,
+                ours_at + c,
+                x_at if first_y[c] else y_at,
+                parts[c],
+            )
         )
-        sums.append([keep, lax.ppermute(send, "dp", along_x)])
-
-    def hop(terms, axes, pairs, *masked):
-        return lax.ppermute(added(place, terms, jnp.bfloat16, masked, mid_at), axes, pairs)
-
-    first, second, third, final = sums
-    out1 = hop(first, "dp", outer)
-    out2 = hop(second, "dp", outer)
-    in2 = hop([*first, out1], ("dp", "mp"), inner)
-    out3 = hop(third, "dp", outer, in2)
-    place, _ = lax.optimization_barrier((place, third[1]))
-    in3 = hop([*second, out2], ("dp", "mp"), inner)
-
+        second = along_x if first_y[c] else along_y
+        arrivals[c] = [lax.ppermute(send, "dp", second) for send in sends]
+
+    def hop(c, at, of, axes, pairs, terms=(), masked=()):
+        come = arrivals[c] if of == 1 else [arrivals[c][at]]
+        value = then(added(now[0], keeps[c], at, of, [come, *terms], masked, mid_at))
+        return lax.ppermute(value, axes, pairs)
+
+    both = ("dp", "mp")
+    block(0)
+    block(1)
+    out1 = [hop(0, at, parts[0], "dp", outer) for at in range(parts[0])]
+    block(2)
+    in2 = hop(0, 0, 1, both, inner, [out1])
+    out2 = hop(1, 0, 1, "dp", outer)
+    block(3)
+    out3 = hop(2, 0, 1, "dp", outer, masked=[[in2]])
+    in3 = hop(1, 0, 1, both, inner, [[out2]])
     new_first, new_second, normed = moments(
-        place, [*final, out3], in3, moment1, moment2, mid_at, core_at
+        now[0], [keeps[3], *arrivals[3], out3], in3, moment1, moment2, mid_at, core_at
     )
     normed_other = lax.ppermute(normed, "mp", cores)
     update = update_rows(place, normed, normed_other, basis, core_at)

time: 105 us -> 103 us (0.981); the launches traced: 105 us -> 102 us
  waiting for transfers between devices: 44.5 us -> 41.5 us
    ppermute x15 -> x19, waiting for transfers between devices: 40.7 us -> 37.7 us  [the longest x5 14.5 us: block(): arrivals[c] = [lax.ppermute(send, 'dp', second) for send in sends]]
    ppermute x15 -> x19, starting transfers between devices: 23.9 us -> 23.1 us  [the longest x6 8.27 us: hop(): return lax.ppermute(value, axes, pairs)]
    pallas_call x12 -> x13, Pallas kernels: 19 us -> 19.5 us  [the longest x4 11.4 us: partial_sums(): call(kernel, 'partial_sums', [shape(rows, 2 * ranks, jnp.bfloat16)] * par...]
  transfers between devices with their start and end apart: 18 -> 22, of which waited for: 13 -> 13; matrix products, arithmetic and copies ran while one was open for 0% -> 0% of each run, Pallas kernels for 23% -> 24%
where the time goes in v4:
time: 103 us; the launch traced here: 102 us
  waiting for transfers between devices  41.5 us (40%)
  Pallas kernels  36.2 us (35%)
  starting transfers between devices  23.1 us (22%)
    ppermute x5, waiting for transfers between devices, block(): arrivals[c] = [lax.ppermute(send, 'dp', second) for send in sends]  14.5 us
    pallas_call x4, Pallas kernels, partial_sums(): call(kernel, 'partial_sums', [shape(rows, 2 * ranks, jnp.bfloat16)] * par...  11.4 us
    ppermute x1, waiting for transfers between devices, staged(): half_y = lax.ppermute(half, 'dp', along_y)  10.2 us
    ppermute x4, waiting for transfers between devices, raw(): return lax.ppermute(mine, 'dp', along_y if first_y[c] else along_x)  9.53 us
    ppermute x6, starting transfers between devices, hop(): return lax.ppermute(value, axes, pairs)  8.27 us
    pallas_call x1, Pallas kernels, rank_halves(): call(kernel, 'rank_halves', [shape(tokens, ranks, jnp.bfloat16), shape(to...  7.61 us
    pallas_call x1, Pallas kernels, update_rows(): call(kernel, 'update_rows', [jax.ShapeDtypeStruct((2, owned, width), jnp....  6.71 us
    ppermute x4, starting transfers between devices, raw(): return lax.ppermute(mine, 'dp', along_y if first_y[c] else along_x)  6.27 us
  transfers between devices with their start and end apart: 22, of which 13 were waited for; matrix products, arithmetic and copies ran while one was open for 0% of the time, Pallas kernels for 24%

profile of v4, /device:TPU:0, one launch (start us, length us, event | category | flops | bytes accessed | tf_op | source)
XLA Modules:
  0.0 101.8 jit_solution(605659916857471935)
XLA Ops:
  0.8 1.8 %take.2 = (bf16[512,512]{1,0:T(8,128)(2,1)S(1)}, bf16[512,512]{1,0:T(8,128)(2,1)S(1)}) custom-call(s32[16]{0:T(128)S(1)} %stack.71.place_ref, bf16[512,4096]{1,0:T(8,128)(2,1)} %ours_ref.7), custom_call_target="tpu_custom_call" | custom-call | bytes 2097152 | tf_op jit(solution)/shard_map/take/pallas_call | solution.py:102
  2.6 3.0 %collective-permute-start = (bf16[512,512]{1,0:T(8,128)(2,1)S(1)}, bf16[512,512]{1,0:T(8,128)(2,1)S(1)}, u32[]{:S(2)}, u32[]{:S(2)}) collective-permute-start(bf16[512,512]{1,0:T(8,128)(2,1)S(1)} %get-tuple-element.37), channel_id=1, source_target_pairs={{0,4},{2,6},{4,0},{6,2},{8,12},{10,14},{12,8},{14,10},{16,20},{18,... | collective-permute-start | bytes 1572872 | tf_op jit(solution)/shard_map/ppermute | solution.py:358
  7.1 7.6 %rank_halves.1 = (bf16[512,512]{1,0:T(8,128)(2,1)S(1)}, f32[512,512]{1,0:T(8,128)S(1)}) custom-call(s32[16]{0:T(128)S(1)} %stack.71.place_ref, bf16[512,4096]{1,0:T(8,128)(2,1)} %a_hbm, bf16[4096,1024]{1,0:T(8,128)(2,1)} %b_ref.1), custom_call_target="tpu_custom_call" | custom-call | flops 4294967296 | bytes 14680064 | tf_op jit(solution)/shard_map/rank_halves/pallas_call | solution.py:149
  14.8 2.8 %collective-permute-done.refs_0_ = bf16[512,512]{1,0:T(8,128)(2,1)S(1)} collective-permute-done((bf16[512,512]{1,0:T(8,128)(2,1)S(1)}, bf16[512,512]{1,0:T(8,128)(2,1)S(1)}, u32[]{:S(2)}, u32[]{:S(2)}) %collective-permute-start) | collective-permute-done | bytes 524320 | tf_op jit(solution)/shard_map/ppermute | solution.py:358
  19.0 1.9 %collective-permute-done.2.b_ref = bf16[512,512]{1,0:T(8,128)(2,1)S(1)} collective-permute-done((bf16[512,512]{1,0:T(8,128)(2,1)S(1)}, bf16[512,512]{1,0:T(8,128)(2,1)S(1)}, u32[]{:S(2)}, u32[]{:S(2)}) %collective-permute-start.2) | collective-permute-done | bytes 524320 | tf_op jit(solution)/shard_map/ppermute | solution.py:368
  22.0 1.6 %collective-permute-start.16 = (bf16[512,512]{1,0:T(8,128)(2,1)S(1)}, bf16[512,512]{1,0:T(8,128)(2,1)S(1)}, u32[]{:S(2)}, u32[]{:S(2)}) collective-permute-start(bf16[512,512]{1,0:T(8,128)(2,1)S(1)} %rounded.1.refs_1_), channel_id=1, source_target_pairs={{0,2},{2,0},{4,6},{6,4},{8,10},{10,8},{12,14},{14,12},{16,18},{18,... | collective-permute-start | bytes 1572872 | tf_op jit(solution)/shard_map/ppermute | solution.py:371
  23.6 1.8 %take.3 = (bf16[512,512]{1,0:T(8,128)(2,1)S(1)}, bf16[512,512]{1,0:T(8,128)(2,1)S(1)}) custom-call(s32[16]{0:T(128)S(1)} %stack.71.place_ref, bf16[512,4096]{1,0:T(8,128)(2,1)} %ours_ref.7), custom_call_target="tpu_custom_call" | custom-call | bytes 2097152 | tf_op jit(solution)/shard_map/take/pallas_call | solution.py:102
  25.4 10.2 %collective-permute-done.3.refs_3_ = bf16[512,512]{1,0:T(8,128)(2,1)S(1)} collective-permute-done((bf16[512,512]{1,0:T(8,128)(2,1)S(1)}, bf16[512,512]{1,0:T(8,128)(2,1)S(1)}, u32[]{:S(2)}, u32[]{:S(2)}) %collective-permute-start.3) | collective-permute-done | bytes 524320 | tf_op jit(solution)/shard_map/ppermute | solution.py:370
  37.5 2.9 %partial_sums.6 = (bf16[128,1024]{1,0:T(8,128)(2,1)S(1)}, bf16[128,1024]{1,0:T(8,128)(2,1)S(1)}, f32[256,1024]{1,0:T(8,128)S(1)}) custom-call(s32[16]{0:T(128)S(1)} %stack.71.place_ref, bf16[512,4096]{1,0:T(8,128)(2,1)} %ours_ref.7, bf16[512,4096]{1,0:T(8,128)(2,1)} %ours_ref.7, bf16[512,512]{1,0:T(8,128)(2,1)S(1)} %collective-permute-done.refs_0_, ...), custom_call_target="tpu_custom_call" | custom-call | flops 1073741824 | bytes 4718592 | tf_op jit(solution)/shard_map/partial_sums/pallas_call | solution.py:240
  42.5 2.9 %partial_sums.7 = (bf16[256,1024]{1,0:T(8,128)(2,1)S(1)}, f32[256,1024]{1,0:T(8,128)S(1)}) custom-call(s32[16]{0:T(128)S(1)} %stack.71.place_ref, bf16[512,4096]{1,0:T(8,128)(2,1)} %ours_ref.7, bf16[512,4096]{1,0:T(8,128)(2,1)} %ours_ref.7, bf16[512,512]{1,0:T(8,128)(2,1)S(1)} %collective-permute-done.1.refs_0_, bf16[512,512]{1,0:T(8,128)(2,1)S(1)} %rounded.1.refs_1_, ...), custom_call_target="tpu_custom_call" | custom-call | flops 1073741824 | bytes 4718592 | tf_op jit(solution)/shard_map/partial_sums/pallas_call | solution.py:240
  46.0 3.6 %collective-permute-done.10.refs_0_ = bf16[128,1024]{1,0:T(8,128)(2,1)S(1)} collective-permute-done((bf16[128,1024]{1,0:T(8,128)(2,1)S(1)}, bf16[128,1024]{1,0:T(8,128)(2,1)S(1)}, u32[]{:S(2)}, u32[]{:S(2)}) %collective-permute-start.10) | collective-permute-done | bytes 262176 | tf_op jit(solution)/shard_map/ppermute | solution.py:404
  51.8 2.6 %collective-permute-done.11.refs_0_.refs_1_ = bf16[128,1024]{1,0:T(8,128)(2,1)S(1)} collective-permute-done((bf16[128,1024]{1,0:T(8,128)(2,1)S(1)}, bf16[128,1024]{1,0:T(8,128)(2,1)S(1)}, u32[]{:S(2)}, u32[]{:S(2)}) %collective-permute-start.11) | collective-permute-done | bytes 262176 | tf_op jit(solution)/shard_map/ppermute | solution.py:404
  55.0 1.6 %collective-permute-start.13 = (bf16[128,1024]{1,0:T(8,128)(2,1)S(1)}, bf16[128,1024]{1,0:T(8,128)(2,1)S(1)}, u32[]{:S(2)}, u32[]{:S(2)}) collective-permute-start(bf16[128,1024]{1,0:T(8,128)(2,1)S(1)} %added.7), channel_id=1, source_target_pairs={{0,8},{2,10},{4,12},{6,14},{8,0},{10,2},{12,4},{14,6},{16,24},{18,... | collective-permute-start | bytes 786440 | tf_op jit(solution)/shard_map/ppermute | solution.py:409
  57.2 2.9 %partial_sums.5 = (bf16[256,1024]{1,0:T(8,128)(2,1)S(1)}, f32[256,1024]{1,0:T(8,128)S(1)}) custom-call(s32[16]{0:T(128)S(1)} %stack.71.place_ref, bf16[512,4096]{1,0:T(8,128)(2,1)} %ours_ref.7, bf16[512,4096]{1,0:T(8,128)(2,1)} %ours_ref.7, bf16[512,512]{1,0:T(8,128)(2,1)S(1)} %collective-permute-done.8.refs_0_, bf16[512,512]{1,0:T(8,128)(2,1)S(1)} %rounded.1.refs_1_, ...), custom_call_target="tpu_custom_call" | custom-call | flops 1073741824 | bytes 4718592 | tf_op jit(solution)/shard_map/partial_sums/pallas_call | solution.py:240
  64.0 3.2 %collective-permute-start.19 = (bf16[256,1024]{1,0:T(8,128)(2,1)S(1)}, bf16[256,1024]{1,0:T(8,128)(2,1)S(1)}, u32[]{:S(2)}, u32[]{:S(2)}) collective-permute-start(bf16[256,1024]{1,0:T(8,128)(2,1)S(1)} %added.10), channel_id=1, source_target_pairs={{0,8},{2,10},{4,12},{6,14},{8,0},{10,2},{12,4},{14,6},{16,24},{18,... | collective-permute-start | bytes 1572872 | tf_op jit(solution)/shard_map/ppermute | solution.py:409
  67.2 5.3 %collective-permute-done.4.refs_0_ = bf16[512,512]{1,0:T(8,128)(2,1)S(1)} collective-permute-done((bf16[512,512]{1,0:T(8,128)(2,1)S(1)}, bf16[512,512]{1,0:T(8,128)(2,1)S(1)}, u32[]{:S(2)}, u32[]{:S(2)}) %collective-permute-start.4) | collective-permute-done | bytes 524320 | tf_op jit(solution)/shard_map/ppermute | solution.py:358
  72.5 2.9 %partial_sums.4 = (bf16[256,1024]{1,0:T(8,128)(2,1)S(1)}, f32[256,1024]{1,0:T(8,128)S(1)}) custom-call(s32[16]{0:T(128)S(1)} %stack.71.place_ref, bf16[512,4096]{1,0:T(8,128)(2,1)} %ours_ref.7, bf16[512,4096]{1,0:T(8,128)(2,1)} %ours_ref.7, bf16[512,512]{1,0:T(8,128)(2,1)S(1)} %collective-permute-done.4.refs_0_, bf16[512,512]{1,0:T(8,128)(2,1)S(1)} %rounded.1.refs_1_, ...), custom_call_target="tpu_custom_call" | custom-call | flops 1073741824 | bytes 4718592 | tf_op jit(solution)/shard_map/partial_sums/pallas_call | solution.py:240
  75.4 1.7 %collective-permute-start.7 = (bf16[256,1024]{1,0:T(8,128)(2,1)S(1)}, bf16[256,1024]{1,0:T(8,128)(2,1)S(1)}, u32[]{:S(2)}, u32[]{:S(2)}) collective-permute-start(bf16[256,1024]{1,0:T(8,128)(2,1)S(1)} %get-tuple-element.47), channel_id=1, source_target_pairs={{0,2},{2,0},{4,6},{6,4},{8,10},{10,8},{12,14},{14,12},{16,18},{18,... | collective-permute-start | bytes 1572872 | tf_op jit(solution)/shard_map/ppermute | solution.py:404
  77.8 1.6 %collective-permute-start.15 = (bf16[256,1024]{1,0:T(8,128)(2,1)S(1)}, bf16[256,1024]{1,0:T(8,128)(2,1)S(1)}, u32[]{:S(2)}, u32[]{:S(2)}) collective-permute-start(bf16[256,1024]{1,0:T(8,128)(2,1)S(1)} %added.9), channel_id=1, source_target_pairs={{0,8},{2,10},{4,12},{6,14},{8,0},{10,2},{12,4},{14,6},{16,24},{18,... | collective-permute-start | bytes 1572872 | tf_op jit(solution)/shard_map/ppermute | solution.py:409
  80.3 8.3 %collective-permute-done.7.refs_1_ = bf16[256,1024]{1,0:T(8,128)(2,1)S(1)} collective-permute-done((bf16[256,1024]{1,0:T(8,128)(2,1)S(1)}, bf16[256,1024]{1,0:T(8,128)(2,1)S(1)}, u32[]{:S(2)}, u32[]{:S(2)}) %collective-permute-start.7) | collective-permute-done | bytes 524320 | tf_op jit(solution)/shard_map/ppermute | solution.py:404
  88.6 2.3 %collective-permute-done.15.refs_2_ = bf16[256,1024]{1,0:T(8,128)(2,1)S(1)} collective-permute-done((bf16[256,1024]{1,0:T(8,128)(2,1)S(1)}, bf16[256,1024]{1,0:T(8,128)(2,1)S(1)}, u32[]{:S(2)}, u32[]{:S(2)}) %collective-permute-start.15) | collective-permute-done | bytes 524320 | tf_op jit(solution)/shard_map/ppermute | solution.py:409
  90.9 2.3 %moments.1 = (f32[256,1024]{1,0:T(8,128)}, f32[256,1024]{1,0:T(8,128)}, bf16[256,1024]{1,0:T(8,128)(2,1)S(1)}) custom-call(s32[16]{0:T(128)S(1)} %stack.71.place_ref, f32[256,1024]{1,0:T(8,128)S(1)} %get-tuple-element.46.refs_0_, bf16[256,1024]{1,0:T(8,128)(2,1)S(1)} %collective-permute-done.7.refs_1_, ...), custom_call_target="tpu_custom_call" | custom-call | flops 5242880 | bytes 7340032 | tf_op jit(solution)/shard_map/moments/pallas_call | solution.py:276
  93.2 1.9 %collective-permute-done.21.m_ref = bf16[256,1024]{1,0:T(8,128)(2,1)S(1)} collective-permute-done((bf16[256,1024]{1,0:T(8,128)(2,1)S(1)}, bf16[256,1024]{1,0:T(8,128)(2,1)S(1)}, u32[]{:S(2)}, u32[]{:S(2)}) %collective-permute-start.21) | collective-permute-done | bytes 524320 | tf_op jit(solution)/shard_map/ppermute | solution.py:424
  95.1 6.7 %update_rows.1 = bf16[2,256,4096]{2,1,0:T(8,128)(2,1)} custom-call(s32[16]{0:T(128)S(1)} %stack.71.place_ref, bf16[256,1024]{1,0:T(8,128)(2,1)S(1)} %get-tuple-element.60.n_ref, bf16[256,1024]{1,0:T(8,128)(2,1)S(1)} %collective-permute-done.21.m_ref, bf16[4096,1024]{1,0:T(8,128)(2,1)S(1)} %bitcast.17), custom_call_target="tpu_custom_call" | custom-call | flops 4294967296 | bytes 13631488 | tf_op jit(solution)/shard_map/update_rows/pallas_call | solution.py:304
  (46 shorter events, 17.6 us)
Async XLA Ops:
  2.6 15.0 %collective-permute-start = (bf16[512,512]{1,0:T(8,128)(2,1)S(1)}, bf16[512,512]{1,0:T(8,128)(2,1)S(1)}, u32[]{:S(2)}, u32[]{:S(2)}) collective-permute-start(bf16[512,512]{1,0:T(8,128)(2,1)S(1)} %get-tuple-element.37), channel_id=1, source_target_pairs={{0,4},{2,6},{4,0},{6,2},{8,12},{10,14},{12,8},{14,10},{16,20},{18,... | collective-permute-start | bytes 1572872 | tf_op jit(solution)/shard_map/ppermute | solution.py:358
  5.6 13.4 %collective-permute-start.1 = (bf16[512,512]{1,0:T(8,128)(2,1)S(1)}, bf16[512,512]{1,0:T(8,128)(2,1)S(1)}, u32[]{:S(2)}, u32[]{:S(2)}) collective-permute-start(bf16[512,512]{1,0:T(8,128)(2,1)S(1)} %get-tuple-element.38), channel_id=1, source_target_pairs={{0,2},{2,0},{4,6},{6,4},{8,10},{10,8},{12,14},{14,12},{16,18},{18,... | collective-permute-start | bytes 1572872 | tf_op jit(solution)/shard_map/ppermute | solution.py:358
  19.0 1.9 %collective-permute-start.2 = (bf16[512,512]{1,0:T(8,128)(2,1)S(1)}, bf16[512,512]{1,0:T(8,128)(2,1)S(1)}, u32[]{:S(2)}, u32[]{:S(2)}) collective-permute-start(bf16[512,512]{1,0:T(8,128)(2,1)S(1)} %get-tuple-element.40), channel_id=1, source_target_pairs={{0,1},{1,0},{2,3},{3,2},{4,5},{5,4},{6,7},{7,6},{8,9},{9,8},{10,11... | collective-permute-start | bytes 1572872 | tf_op jit(solution)/shard_map/ppermute | solution.py:368
  21.6 14.0 %collective-permute-start.3 = (bf16[512,512]{1,0:T(8,128)(2,1)S(1)}, bf16[512,512]{1,0:T(8,128)(2,1)S(1)}, u32[]{:S(2)}, u32[]{:S(2)}) collective-permute-start(bf16[512,512]{1,0:T(8,128)(2,1)S(1)} %rounded.1.refs_1_), channel_id=1, source_target_pairs={{0,4},{2,6},{4,0},{6,2},{8,12},{10,14},{12,8},{14,10},{16,20},{18,... | collective-permute-start | bytes 1572872 | tf_op jit(solution)/shard_map/ppermute | solution.py:370
  22.0 13.7 %collective-permute-start.16 = (bf16[512,512]{1,0:T(8,128)(2,1)S(1)}, bf16[512,512]{1,0:T(8,128)(2,1)S(1)}, u32[]{:S(2)}, u32[]{:S(2)}) collective-permute-start(bf16[512,512]{1,0:T(8,128)(2,1)S(1)} %rounded.1.refs_1_), channel_id=1, source_target_pairs={{0,2},{2,0},{4,6},{6,4},{8,10},{10,8},{12,14},{14,12},{16,18},{18,... | collective-permute-start | bytes 1572872 | tf_op jit(solution)/shard_map/ppermute | solution.py:371
  23.6 13.7 %collective-permute-start.5 = (bf16[512,512]{1,0:T(8,128)(2,1)S(1)}, bf16[512,512]{1,0:T(8,128)(2,1)S(1)}, u32[]{:S(2)}, u32[]{:S(2)}) collective-permute-start(bf16[512,512]{1,0:T(8,128)(2,1)S(1)} %rounded.1.refs_1_), channel_id=1, source_target_pairs={{0,1},{1,0},{2,3},{3,2},{4,5},{5,4},{6,7},{7,6},{8,9},{9,8},{10,11... | collective-permute-start | bytes 1572872 | tf_op jit(solution)/shard_map/ppermute | solution.py:372
  35.6 1.9 %collective-permute-start.6 = (bf16[512,512]{1,0:T(8,128)(2,1)S(1)}, bf16[512,512]{1,0:T(8,128)(2,1)S(1)}, u32[]{:S(2)}, u32[]{:S(2)}) collective-permute-start(bf16[512,512]{1,0:T(8,128)(2,1)S(1)} %collective-permute-done.3.refs_3_), channel_id=1, source_target_pairs={{0,1},{1,0},{2,3},{3,2},{4,5},{5,4},{6,7},{7,6},{8,9},{9,8},{10,11... | collective-permute-start | bytes 1572872 | tf_op jit(solution)/shard_map/ppermute | solution.py:380
  35.7 6.8 %collective-permute-start.17 = (bf16[512,512]{1,0:T(8,128)(2,1)S(1)}, bf16[512,512]{1,0:T(8,128)(2,1)S(1)}, u32[]{:S(2)}, u32[]{:S(2)}) collective-permute-start(bf16[512,512]{1,0:T(8,128)(2,1)S(1)} %collective-permute-done.16.refs_3_), channel_id=1, source_target_pairs={{0,1},{1,0},{2,3},{3,2},{4,5},{5,4},{6,7},{7,6},{8,9},{9,8},{10,11... | collective-permute-start | bytes 1572872 | tf_op jit(solution)/shard_map/ppermute | solution.py:381
  36.1 21.0 %collective-permute-start.8 = (bf16[512,512]{1,0:T(8,128)(2,1)S(1)}, bf16[512,512]{1,0:T(8,128)(2,1)S(1)}, u32[]{:S(2)}, u32[]{:S(2)}) collective-permute-start(bf16[512,512]{1,0:T(8,128)(2,1)S(1)} %get-tuple-element.48), channel_id=1, source_target_pairs={{0,4},{2,6},{4,0},{6,2},{8,12},{10,14},{12,8},{14,10},{16,20},{18,... | collective-permute-start | bytes 1572872 | tf_op jit(solution)/shard_map/ppermute | solution.py:358
  40.4 9.2 %collective-permute-start.10 = (bf16[128,1024]{1,0:T(8,128)(2,1)S(1)}, bf16[128,1024]{1,0:T(8,128)(2,1)S(1)}, u32[]{:S(2)}, u32[]{:S(2)}) collective-permute-start(bf16[128,1024]{1,0:T(8,128)(2,1)S(1)} %get-tuple-element.53), channel_id=1, source_target_pairs={{0,2},{2,0},{4,6},{6,4},{8,10},{10,8},{12,14},{14,12},{16,18},{18,... | collective-permute-start | bytes 786440 | tf_op jit(solution)/shard_map/ppermute | solution.py:404
  42.0 12.4 %collective-permute-start.11 = (bf16[128,1024]{1,0:T(8,128)(2,1)S(1)}, bf16[128,1024]{1,0:T(8,128)(2,1)S(1)}, u32[]{:S(2)}, u32[]{:S(2)}) collective-permute-start(bf16[128,1024]{1,0:T(8,128)(2,1)S(1)} %get-tuple-element.54), channel_id=1, source_target_pairs={{0,2},{2,0},{4,6},{6,4},{8,10},{10,8},{12,14},{14,12},{16,18},{18,... | collective-permute-start | bytes 786440 | tf_op jit(solution)/shard_map/ppermute | solution.py:404
  45.3 18.0 %collective-permute-start.18 = (bf16[256,1024]{1,0:T(8,128)(2,1)S(1)}, bf16[256,1024]{1,0:T(8,128)(2,1)S(1)}, u32[]{:S(2)}, u32[]{:S(2)}) collective-permute-start(bf16[256,1024]{1,0:T(8,128)(2,1)S(1)} %get-tuple-element.57), channel_id=1, source_target_pairs={{0,4},{2,6},{4,0},{6,2},{8,12},{10,14},{12,8},{14,10},{16,20},{18,... | collective-permute-start | bytes 1572872 | tf_op jit(solution)/shard_map/ppermute | solution.py:404
  50.2 11.4 %collective-permute-start.12 = (bf16[128,1024]{1,0:T(8,128)(2,1)S(1)}, bf16[128,1024]{1,0:T(8,128)(2,1)S(1)}, u32[]{:S(2)}, u32[]{:S(2)}) collective-permute-start(bf16[128,1024]{1,0:T(8,128)(2,1)S(1)} %added.6), channel_id=1, source_target_pairs={{0,8},{2,10},{4,12},{6,14},{8,0},{10,2},{12,4},{14,6},{16,24},{18,... | collective-permute-start | bytes 786440 | tf_op jit(solution)/shard_map/ppermute | solution.py:409
  55.0 7.6 %collective-permute-start.13 = (bf16[128,1024]{1,0:T(8,128)(2,1)S(1)}, bf16[128,1024]{1,0:T(8,128)(2,1)S(1)}, u32[]{:S(2)}, u32[]{:S(2)}) collective-permute-start(bf16[128,1024]{1,0:T(8,128)(2,1)S(1)} %added.7), channel_id=1, source_target_pairs={{0,8},{2,10},{4,12},{6,14},{8,0},{10,2},{12,4},{14,6},{16,24},{18,... | collective-permute-start | bytes 786440 | tf_op jit(solution)/shard_map/ppermute | solution.py:409
  56.6 15.8 %collective-permute-start.4 = (bf16[512,512]{1,0:T(8,128)(2,1)S(1)}, bf16[512,512]{1,0:T(8,128)(2,1)S(1)}, u32[]{:S(2)}, u32[]{:S(2)}) collective-permute-start(bf16[512,512]{1,0:T(8,128)(2,1)S(1)} %get-tuple-element.44), channel_id=1, source_target_pairs={{0,4},{2,6},{4,0},{6,2},{8,12},{10,14},{12,8},{14,10},{16,20},{18,... | collective-permute-start | bytes 1572872 | tf_op jit(solution)/shard_map/ppermute | solution.py:358
  60.0 17.1 %collective-permute-start.9 = (bf16[256,1024]{1,0:T(8,128)(2,1)S(1)}, bf16[256,1024]{1,0:T(8,128)(2,1)S(1)}, u32[]{:S(2)}, u32[]{:S(2)}) collective-permute-start(bf16[256,1024]{1,0:T(8,128)(2,1)S(1)} %get-tuple-element.50), channel_id=1, source_target_pairs={{0,2},{2,0},{4,6},{6,4},{8,10},{10,8},{12,14},{14,12},{16,18},{18,... | collective-permute-start | bytes 1572872 | tf_op jit(solution)/shard_map/ppermute | solution.py:404
  63.3 13.8 %collective-permute-start.14 = (bf16[256,1024]{1,0:T(8,128)(2,1)S(1)}, bf16[256,1024]{1,0:T(8,128)(2,1)S(1)}, u32[]{:S(2)}, u32[]{:S(2)}) collective-permute-start(bf16[256,1024]{1,0:T(8,128)(2,1)S(1)} %added.8), channel_id=1, source_target_pairs={{0,1},{1,0},{2,3},{3,2},{4,5},{5,4},{6,7},{7,6},{8,16},{9,17},{10,... | collective-permute-start | bytes 1572872 | tf_op jit(solution)/shard_map/ppermute | solution.py:409
  63.4 31.7 %slice-start = ((s8[8388608]{0:T(1024)(128)(4,1)}), s8[4194304]{0:T(1024)(128)(4,1)S(1)}, s32[]{:S(2)}) async-start(s8[8388608]{0:T(1024)(128)(4,1)} %bitcast.16), calls=%async_computation | async-start | bytes 8388608
  64.0 31.1 %slice-start.1 = ((s8[8388608]{0:T(1024)(128)(4,1)}), s8[4194304]{0:T(1024)(128)(4,1)S(1)}, s32[]{:S(2)}) async-start(s8[8388608]{0:T(1024)(128)(4,1)} %bitcast.16), calls=%async_computation.1 | async-start | bytes 8388608
  64.0 15.4 %collective-permute-start.19 = (bf16[256,1024]{1,0:T(8,128)(2,1)S(1)}, bf16[256,1024]{1,0:T(8,128)(2,1)S(1)}, u32[]{:S(2)}, u32[]{:S(2)}) collective-permute-start(bf16[256,1024]{1,0:T(8,128)(2,1)S(1)} %added.10), channel_id=1, source_target_pairs={{0,8},{2,10},{4,12},{6,14},{8,0},{10,2},{12,4},{14,6},{16,24},{18,... | collective-permute-start | bytes 1572872 | tf_op jit(solution)/shard_map/ppermute | solution.py:409
  75.4 13.2 %collective-permute-start.7 = (bf16[256,1024]{1,0:T(8,128)(2,1)S(1)}, bf16[256,1024]{1,0:T(8,128)(2,1)S(1)}, u32[]{:S(2)}, u32[]{:S(2)}) collective-permute-start(bf16[256,1024]{1,0:T(8,128)(2,1)S(1)} %get-tuple-element.47), channel_id=1, source_target_pairs={{0,2},{2,0},{4,6},{6,4},{8,10},{10,8},{12,14},{14,12},{16,18},{18,... | collective-permute-start | bytes 1572872 | tf_op jit(solution)/shard_map/ppermute | solution.py:404
  77.8 13.0 %collective-permute-start.15 = (bf16[256,1024]{1,0:T(8,128)(2,1)S(1)}, bf16[256,1024]{1,0:T(8,128)(2,1)S(1)}, u32[]{:S(2)}, u32[]{:S(2)}) collective-permute-start(bf16[256,1024]{1,0:T(8,128)(2,1)S(1)} %added.9), channel_id=1, source_target_pairs={{0,8},{2,10},{4,12},{6,14},{8,0},{10,2},{12,4},{14,6},{16,24},{18,... | collective-permute-start | bytes 1572872 | tf_op jit(solution)/shard_map/ppermute | solution.py:409
  80.2 10.7 %collective-permute-start.20 = (bf16[256,1024]{1,0:T(8,128)(2,1)S(1)}, bf16[256,1024]{1,0:T(8,128)(2,1)S(1)}, u32[]{:S(2)}, u32[]{:S(2)}) collective-permute-start(bf16[256,1024]{1,0:T(8,128)(2,1)S(1)} %added.11), channel_id=1, source_target_pairs={{0,1},{1,0},{2,3},{3,2},{4,5},{5,4},{6,7},{7,6},{8,16},{9,17},{10,... | collective-permute-start | bytes 1572872 | tf_op jit(solution)/shard_map/ppermute | solution.py:409
  93.2 1.9 %collective-permute-start.21 = (bf16[256,1024]{1,0:T(8,128)(2,1)S(1)}, bf16[256,1024]{1,0:T(8,128)(2,1)S(1)}, u32[]{:S(2)}, u32[]{:S(2)}) collective-permute-start(bf16[256,1024]{1,0:T(8,128)(2,1)S(1)} %get-tuple-element.60.n_ref), channel_id=1, source_target_pairs={{0,1},{1,0},{2,3},{3,2},{4,5},{5,4},{6,7},{7,6},{8,9},{9,8},{10,11... | collective-permute-start | bytes 1572872 | tf_op jit(solution)/shard_map/ppermute | solution.py:424
  (2 other events, 31.0 us)

commit v5 on v4

--- a/solution.py
+++ b/solution.py
@@ -364,8 +364,9 @@
 
     activations = pltpu.with_memory_space_constraint(activations, pltpu.HBM)
     other, own = rank_halves(place, activations, basis_hbm, core_at)
-    other, own, first, second = lax.optimization_barrier((other, own, first, second))
+    other, own, first = lax.optimization_barrier((other, own, first))
     arrived = lax.ppermute(other, "mp", cores)
+    arrived, second = lax.optimization_barrier((arrived, second))
     half = rounded(place, own, arrived)
     half_y = lax.ppermute(half, "dp", along_y)
     half_x = lax.ppermute(half, "dp", along_x)

time: 103 us -> 103 us (level)
  starting transfers between devices: 23.1 us -> 25.2 us
  waiting for transfers between devices: 41.5 us -> 39.5 us
    ppermute x1, waiting for transfers between devices: 1.91 us -> 0.45 us  [staged(): arrived = lax.ppermute(other, 'mp', cores)]
    ppermute x1, starting transfers between devices: 0.42 us -> 1.81 us  [staged(): half_y = lax.ppermute(half, 'dp', along_y)]
    ppermute x1, waiting for transfers between devices: 0.08 us -> 1.46 us  [staged(): half_x = lax.ppermute(half, 'dp', along_x)]
    ppermute x6, waiting for transfers between devices: 3.28 us -> 2.02 us  [hop(): return lax.ppermute(value, axes, pairs)]
    ppermute x1, waiting for transfers between devices: 10.2 us -> 8.95 us  [staged(): half_y = lax.ppermute(half, 'dp', along_y)]
    ppermute x4, waiting for transfers between devices: 9.53 us -> 10.7 us  [raw(): return lax.ppermute(mine, 'dp', along_y if first_y[c] else along_x)]
  transfers between devices with their start and end apart: 22 -> 22, of which waited for: 13 -> 11; matrix products, arithmetic and copies ran while one was open for 0% -> 0% of each run, Pallas kernels for 24% -> 24%
where the time goes in v5:
time: 103 us; the launch traced here: 102 us
  waiting for transfers between devices  39.5 us (38%)
  Pallas kernels  36.2 us (35%)
  starting transfers between devices  25.2 us (24%)
    ppermute x5, waiting for transfers between devices, block(): arrivals[c] = [lax.ppermute(send, 'dp', second) for send in sends]  14 us
    pallas_call x4, Pallas kernels, partial_sums(): call(kernel, 'partial_sums', [shape(rows, 2 * ranks, jnp.bfloat16)] * par...  11.5 us
    ppermute x4, waiting for transfers between devices, raw(): return lax.ppermute(mine, 'dp', along_y if first_y[c] else along_x)  10.7 us
    ppermute x1, waiting for transfers between devices, staged(): half_y = lax.ppermute(half, 'dp', along_y)  8.95 us
    ppermute x6, starting transfers between devices, hop(): return lax.ppermute(value, axes, pairs)  8.44 us
    pallas_call x1, Pallas kernels, rank_halves(): call(kernel, 'rank_halves', [shape(tokens, ranks, jnp.bfloat16), shape(to...  7.61 us
    ppermute x4, starting transfers between devices, raw(): return lax.ppermute(mine, 'dp', along_y if first_y[c] else along_x)  6.83 us
    pallas_call x1, Pallas kernels, update_rows(): call(kernel, 'update_rows', [jax.ShapeDtypeStruct((2, owned, width), jnp....  6.71 us
  transfers between devices with their start and end apart: 22, of which 11 were waited for; matrix products, arithmetic and copies ran while one was open for 0% of the time, Pallas kernels for 24%

profile of v5, /device:TPU:0, one launch (start us, length us, event | category | flops | bytes accessed | tf_op | source)
XLA Modules:
  0.0 101.9 jit_solution(7494671590725932828)
XLA Ops:
  0.8 1.8 %take.2 = (bf16[512,512]{1,0:T(8,128)(2,1)S(1)}, bf16[512,512]{1,0:T(8,128)(2,1)S(1)}) custom-call(s32[16]{0:T(128)S(1)} %stack.71.place_ref, bf16[512,4096]{1,0:T(8,128)(2,1)} %ours_ref.7), custom_call_target="tpu_custom_call" | custom-call | bytes 2097152 | tf_op jit(solution)/shard_map/take/pallas_call | solution.py:102
  2.6 3.0 %collective-permute-start = (bf16[512,512]{1,0:T(8,128)(2,1)S(1)}, bf16[512,512]{1,0:T(8,128)(2,1)S(1)}, u32[]{:S(2)}, u32[]{:S(2)}) collective-permute-start(bf16[512,512]{1,0:T(8,128)(2,1)S(1)} %get-tuple-element.38), channel_id=1, source_target_pairs={{0,4},{2,6},{4,0},{6,2},{8,12},{10,14},{12,8},{14,10},{16,20},{18,... | collective-permute-start | bytes 1572872 | tf_op jit(solution)/shard_map/ppermute | solution.py:358
  7.1 7.6 %rank_halves.1 = (bf16[512,512]{1,0:T(8,128)(2,1)S(1)}, f32[512,512]{1,0:T(8,128)S(1)}) custom-call(s32[16]{0:T(128)S(1)} %stack.71.place_ref, bf16[512,4096]{1,0:T(8,128)(2,1)} %a_hbm, bf16[4096,1024]{1,0:T(8,128)(2,1)} %b_ref.1), custom_call_target="tpu_custom_call" | custom-call | flops 4294967296 | bytes 14680064 | tf_op jit(solution)/shard_map/rank_halves/pallas_call | solution.py:149
  14.8 2.8 %collective-permute-done.refs_0_ = bf16[512,512]{1,0:T(8,128)(2,1)S(1)} collective-permute-done((bf16[512,512]{1,0:T(8,128)(2,1)S(1)}, bf16[512,512]{1,0:T(8,128)(2,1)S(1)}, u32[]{:S(2)}, u32[]{:S(2)}) %collective-permute-start) | collective-permute-done | bytes 524320 | tf_op jit(solution)/shard_map/ppermute | solution.py:358
  20.1 1.8 %collective-permute-start.3 = (bf16[512,512]{1,0:T(8,128)(2,1)S(1)}, bf16[512,512]{1,0:T(8,128)(2,1)S(1)}, u32[]{:S(2)}, u32[]{:S(2)}) collective-permute-start(bf16[512,512]{1,0:T(8,128)(2,1)S(1)} %rounded.1.refs_1_), channel_id=1, source_target_pairs={{0,4},{2,6},{4,0},{6,2},{8,12},{10,14},{12,8},{14,10},{16,20},{18,... | collective-permute-start | bytes 1572872 | tf_op jit(solution)/shard_map/ppermute | solution.py:371
  23.4 1.8 %take.3 = (bf16[512,512]{1,0:T(8,128)(2,1)S(1)}, bf16[512,512]{1,0:T(8,128)(2,1)S(1)}) custom-call(s32[16]{0:T(128)S(1)} %stack.71.place_ref, bf16[512,4096]{1,0:T(8,128)(2,1)} %ours_ref.7), custom_call_target="tpu_custom_call" | custom-call | bytes 2097152 | tf_op jit(solution)/shard_map/take/pallas_call | solution.py:102
  25.2 8.9 %collective-permute-done.3.refs_3_ = bf16[512,512]{1,0:T(8,128)(2,1)S(1)} collective-permute-done((bf16[512,512]{1,0:T(8,128)(2,1)S(1)}, bf16[512,512]{1,0:T(8,128)(2,1)S(1)}, u32[]{:S(2)}, u32[]{:S(2)}) %collective-permute-start.3) | collective-permute-done | bytes 524320 | tf_op jit(solution)/shard_map/ppermute | solution.py:371
  36.4 2.9 %partial_sums.6 = (bf16[128,1024]{1,0:T(8,128)(2,1)S(1)}, bf16[128,1024]{1,0:T(8,128)(2,1)S(1)}, f32[256,1024]{1,0:T(8,128)S(1)}) custom-call(s32[16]{0:T(128)S(1)} %stack.71.place_ref, bf16[512,4096]{1,0:T(8,128)(2,1)} %ours_ref.7, bf16[512,4096]{1,0:T(8,128)(2,1)} %ours_ref.7, bf16[512,512]{1,0:T(8,128)(2,1)S(1)} %collective-permute-done.refs_0_, ...), custom_call_target="tpu_custom_call" | custom-call | flops 1073741824 | bytes 4718592 | tf_op jit(solution)/shard_map/partial_sums/pallas_call | solution.py:240
  39.3 1.5 %collective-permute-start.10 = (bf16[128,1024]{1,0:T(8,128)(2,1)S(1)}, bf16[128,1024]{1,0:T(8,128)(2,1)S(1)}, u32[]{:S(2)}, u32[]{:S(2)}) collective-permute-start(bf16[128,1024]{1,0:T(8,128)(2,1)S(1)} %get-tuple-element.55), channel_id=1, source_target_pairs={{0,2},{2,0},{4,6},{6,4},{8,10},{10,8},{12,14},{14,12},{16,18},{18,... | collective-permute-start | bytes 786440 | tf_op jit(solution)/shard_map/ppermute | solution.py:405
  41.4 2.9 %partial_sums.7 = (bf16[256,1024]{1,0:T(8,128)(2,1)S(1)}, f32[256,1024]{1,0:T(8,128)S(1)}) custom-call(s32[16]{0:T(128)S(1)} %stack.71.place_ref, bf16[512,4096]{1,0:T(8,128)(2,1)} %ours_ref.7, bf16[512,4096]{1,0:T(8,128)(2,1)} %ours_ref.7, bf16[512,512]{1,0:T(8,128)(2,1)S(1)} %collective-permute-done.2.refs_0_, bf16[512,512]{1,0:T(8,128)(2,1)S(1)} %rounded.1.refs_1_, ...), custom_call_target="tpu_custom_call" | custom-call | flops 1073741824 | bytes 4718592 | tf_op jit(solution)/shard_map/partial_sums/pallas_call | solution.py:240
  45.7 2.9 %collective-permute-done.10.refs_0_ = bf16[128,1024]{1,0:T(8,128)(2,1)S(1)} collective-permute-done((bf16[128,1024]{1,0:T(8,128)(2,1)S(1)}, bf16[128,1024]{1,0:T(8,128)(2,1)S(1)}, u32[]{:S(2)}, u32[]{:S(2)}) %collective-permute-start.10) | collective-permute-done | bytes 262176 | tf_op jit(solution)/shard_map/ppermute | solution.py:405
  49.1 1.6 %collective-permute-start.12 = (bf16[128,1024]{1,0:T(8,128)(2,1)S(1)}, bf16[128,1024]{1,0:T(8,128)(2,1)S(1)}, u32[]{:S(2)}, u32[]{:S(2)}) collective-permute-start(bf16[128,1024]{1,0:T(8,128)(2,1)S(1)} %added.6), channel_id=1, source_target_pairs={{0,8},{2,10},{4,12},{6,14},{8,0},{10,2},{12,4},{14,6},{16,24},{18,... | collective-permute-start | bytes 786440 | tf_op jit(solution)/shard_map/ppermute | solution.py:410
  50.7 2.2 %collective-permute-done.11.refs_0_.refs_1_ = bf16[128,1024]{1,0:T(8,128)(2,1)S(1)} collective-permute-done((bf16[128,1024]{1,0:T(8,128)(2,1)S(1)}, bf16[128,1024]{1,0:T(8,128)(2,1)S(1)}, u32[]{:S(2)}, u32[]{:S(2)}) %collective-permute-start.11) | collective-permute-done | bytes 262176 | tf_op jit(solution)/shard_map/ppermute | solution.py:405
  53.6 1.9 %collective-permute-start.13 = (bf16[128,1024]{1,0:T(8,128)(2,1)S(1)}, bf16[128,1024]{1,0:T(8,128)(2,1)S(1)}, u32[]{:S(2)}, u32[]{:S(2)}) collective-permute-start(bf16[128,1024]{1,0:T(8,128)(2,1)S(1)} %added.7), channel_id=1, source_target_pairs={{0,8},{2,10},{4,12},{6,14},{8,0},{10,2},{12,4},{14,6},{16,24},{18,... | collective-permute-start | bytes 786440 | tf_op jit(solution)/shard_map/ppermute | solution.py:410
  56.9 2.9 %partial_sums.5 = (bf16[256,1024]{1,0:T(8,128)(2,1)S(1)}, f32[256,1024]{1,0:T(8,128)S(1)}) custom-call(s32[16]{0:T(128)S(1)} %stack.71.place_ref, bf16[512,4096]{1,0:T(8,128)(2,1)} %ours_ref.7, bf16[512,4096]{1,0:T(8,128)(2,1)} %ours_ref.7, bf16[512,512]{1,0:T(8,128)(2,1)S(1)} %collective-permute-done.8.refs_0_, bf16[512,512]{1,0:T(8,128)(2,1)S(1)} %rounded.1.refs_1_, ...), custom_call_target="tpu_custom_call" | custom-call | flops 1073741824 | bytes 4718592 | tf_op jit(solution)/shard_map/partial_sums/pallas_call | solution.py:240
  62.8 3.2 %collective-permute-start.19 = (bf16[256,1024]{1,0:T(8,128)(2,1)S(1)}, bf16[256,1024]{1,0:T(8,128)(2,1)S(1)}, u32[]{:S(2)}, u32[]{:S(2)}) collective-permute-start(bf16[256,1024]{1,0:T(8,128)(2,1)S(1)} %added.10), channel_id=1, source_target_pairs={{0,8},{2,10},{4,12},{6,14},{8,0},{10,2},{12,4},{14,6},{16,24},{18,... | collective-permute-start | bytes 1572872 | tf_op jit(solution)/shard_map/ppermute | solution.py:410
  66.0 6.4 %collective-permute-done.4.refs_0_ = bf16[512,512]{1,0:T(8,128)(2,1)S(1)} collective-permute-done((bf16[512,512]{1,0:T(8,128)(2,1)S(1)}, bf16[512,512]{1,0:T(8,128)(2,1)S(1)}, u32[]{:S(2)}, u32[]{:S(2)}) %collective-permute-start.4) | collective-permute-done | bytes 524320 | tf_op jit(solution)/shard_map/ppermute | solution.py:358
  72.4 2.9 %partial_sums.4 = (bf16[256,1024]{1,0:T(8,128)(2,1)S(1)}, f32[256,1024]{1,0:T(8,128)S(1)}) custom-call(s32[16]{0:T(128)S(1)} %stack.71.place_ref, bf16[512,4096]{1,0:T(8,128)(2,1)} %ours_ref.7, bf16[512,4096]{1,0:T(8,128)(2,1)} %ours_ref.7, bf16[512,512]{1,0:T(8,128)(2,1)S(1)} %collective-permute-done.4.refs_0_, bf16[512,512]{1,0:T(8,128)(2,1)S(1)} %rounded.1.refs_1_, ...), custom_call_target="tpu_custom_call" | custom-call | flops 1073741824 | bytes 4718592 | tf_op jit(solution)/shard_map/partial_sums/pallas_call | solution.py:240
  77.6 1.6 %collective-permute-start.15 = (bf16[256,1024]{1,0:T(8,128)(2,1)S(1)}, bf16[256,1024]{1,0:T(8,128)(2,1)S(1)}, u32[]{:S(2)}, u32[]{:S(2)}) collective-permute-start(bf16[256,1024]{1,0:T(8,128)(2,1)S(1)} %added.9), channel_id=1, source_target_pairs={{0,8},{2,10},{4,12},{6,14},{8,0},{10,2},{12,4},{14,6},{16,24},{18,... | collective-permute-start | bytes 1572872 | tf_op jit(solution)/shard_map/ppermute | solution.py:410
  80.0 8.9 %collective-permute-done.7.refs_1_ = bf16[256,1024]{1,0:T(8,128)(2,1)S(1)} collective-permute-done((bf16[256,1024]{1,0:T(8,128)(2,1)S(1)}, bf16[256,1024]{1,0:T(8,128)(2,1)S(1)}, u32[]{:S(2)}, u32[]{:S(2)}) %collective-permute-start.7) | collective-permute-done | bytes 524320 | tf_op jit(solution)/shard_map/ppermute | solution.py:405
  88.9 2.0 %collective-permute-done.15.refs_2_ = bf16[256,1024]{1,0:T(8,128)(2,1)S(1)} collective-permute-done((bf16[256,1024]{1,0:T(8,128)(2,1)S(1)}, bf16[256,1024]{1,0:T(8,128)(2,1)S(1)}, u32[]{:S(2)}, u32[]{:S(2)}) %collective-permute-start.15) | collective-permute-done | bytes 524320 | tf_op jit(solution)/shard_map/ppermute | solution.py:410
  91.0 2.3 %moments.1 = (f32[256,1024]{1,0:T(8,128)}, f32[256,1024]{1,0:T(8,128)}, bf16[256,1024]{1,0:T(8,128)(2,1)S(1)}) custom-call(s32[16]{0:T(128)S(1)} %stack.71.place_ref, f32[256,1024]{1,0:T(8,128)S(1)} %get-tuple-element.48.refs_0_, bf16[256,1024]{1,0:T(8,128)(2,1)S(1)} %collective-permute-done.7.refs_1_, ...), custom_call_target="tpu_custom_call" | custom-call | flops 5242880 | bytes 7340032 | tf_op jit(solution)/shard_map/moments/pallas_call | solution.py:276
  93.3 1.9 %collective-permute-done.21.m_ref = bf16[256,1024]{1,0:T(8,128)(2,1)S(1)} collective-permute-done((bf16[256,1024]{1,0:T(8,128)(2,1)S(1)}, bf16[256,1024]{1,0:T(8,128)(2,1)S(1)}, u32[]{:S(2)}, u32[]{:S(2)}) %collective-permute-start.21) | collective-permute-done | bytes 524320 | tf_op jit(solution)/shard_map/ppermute | solution.py:425
  95.2 6.7 %update_rows.1 = bf16[2,256,4096]{2,1,0:T(8,128)(2,1)} custom-call(s32[16]{0:T(128)S(1)} %stack.71.place_ref, bf16[256,1024]{1,0:T(8,128)(2,1)S(1)} %get-tuple-element.62.n_ref, bf16[256,1024]{1,0:T(8,128)(2,1)S(1)} %collective-permute-done.21.m_ref, bf16[4096,1024]{1,0:T(8,128)(2,1)S(1)} %bitcast.17), custom_call_target="tpu_custom_call" | custom-call | flops 4294967296 | bytes 13631488 | tf_op jit(solution)/shard_map/update_rows/pallas_call | solution.py:304
  (46 shorter events, 18.6 us)
Async XLA Ops:
  2.6 15.0 %collective-permute-start = (bf16[512,512]{1,0:T(8,128)(2,1)S(1)}, bf16[512,512]{1,0:T(8,128)(2,1)S(1)}, u32[]{:S(2)}, u32[]{:S(2)}) collective-permute-start(bf16[512,512]{1,0:T(8,128)(2,1)S(1)} %get-tuple-element.38), channel_id=1, source_target_pairs={{0,4},{2,6},{4,0},{6,2},{8,12},{10,14},{12,8},{14,10},{16,20},{18,... | collective-permute-start | bytes 1572872 | tf_op jit(solution)/shard_map/ppermute | solution.py:358
  5.6 13.4 %collective-permute-start.2 = (bf16[512,512]{1,0:T(8,128)(2,1)S(1)}, bf16[512,512]{1,0:T(8,128)(2,1)S(1)}, u32[]{:S(2)}, u32[]{:S(2)}) collective-permute-start(bf16[512,512]{1,0:T(8,128)(2,1)S(1)} %get-tuple-element.41), channel_id=1, source_target_pairs={{0,2},{2,0},{4,6},{6,4},{8,10},{10,8},{12,14},{14,12},{16,18},{18,... | collective-permute-start | bytes 1572872 | tf_op jit(solution)/shard_map/ppermute | solution.py:358
  17.6 1.9 %collective-permute-start.1 = (bf16[512,512]{1,0:T(8,128)(2,1)S(1)}, bf16[512,512]{1,0:T(8,128)(2,1)S(1)}, u32[]{:S(2)}, u32[]{:S(2)}) collective-permute-start(bf16[512,512]{1,0:T(8,128)(2,1)S(1)} %get-tuple-element.40), channel_id=1, source_target_pairs={{0,1},{1,0},{2,3},{3,2},{4,5},{5,4},{6,7},{7,6},{8,9},{9,8},{10,11... | collective-permute-start | bytes 1572872 | tf_op jit(solution)/shard_map/ppermute | solution.py:368
  20.1 14.0 %collective-permute-start.3 = (bf16[512,512]{1,0:T(8,128)(2,1)S(1)}, bf16[512,512]{1,0:T(8,128)(2,1)S(1)}, u32[]{:S(2)}, u32[]{:S(2)}) collective-permute-start(bf16[512,512]{1,0:T(8,128)(2,1)S(1)} %rounded.1.refs_1_), channel_id=1, source_target_pairs={{0,4},{2,6},{4,0},{6,2},{8,12},{10,14},{12,8},{14,10},{16,20},{18,... | collective-permute-start | bytes 1572872 | tf_op jit(solution)/shard_map/ppermute | solution.py:371
  21.9 13.7 %collective-permute-start.16 = (bf16[512,512]{1,0:T(8,128)(2,1)S(1)}, bf16[512,512]{1,0:T(8,128)(2,1)S(1)}, u32[]{:S(2)}, u32[]{:S(2)}) collective-permute-start(bf16[512,512]{1,0:T(8,128)(2,1)S(1)} %rounded.1.refs_1_), channel_id=1, source_target_pairs={{0,2},{2,0},{4,6},{6,4},{8,10},{10,8},{12,14},{14,12},{16,18},{18,... | collective-permute-start | bytes 1572872 | tf_op jit(solution)/shard_map/ppermute | solution.py:372
  23.4 13.0 %collective-permute-start.5 = (bf16[512,512]{1,0:T(8,128)(2,1)S(1)}, bf16[512,512]{1,0:T(8,128)(2,1)S(1)}, u32[]{:S(2)}, u32[]{:S(2)}) collective-permute-start(bf16[512,512]{1,0:T(8,128)(2,1)S(1)} %rounded.1.refs_1_), channel_id=1, source_target_pairs={{0,1},{1,0},{2,3},{3,2},{4,5},{5,4},{6,7},{7,6},{8,9},{9,8},{10,11... | collective-permute-start | bytes 1572872 | tf_op jit(solution)/shard_map/ppermute | solution.py:373
  34.1 2.3 %collective-permute-start.6 = (bf16[512,512]{1,0:T(8,128)(2,1)S(1)}, bf16[512,512]{1,0:T(8,128)(2,1)S(1)}, u32[]{:S(2)}, u32[]{:S(2)}) collective-permute-start(bf16[512,512]{1,0:T(8,128)(2,1)S(1)} %collective-permute-done.3.refs_3_), channel_id=1, source_target_pairs={{0,1},{1,0},{2,3},{3,2},{4,5},{5,4},{6,7},{7,6},{8,9},{9,8},{10,11... | collective-permute-start | bytes 1572872 | tf_op jit(solution)/shard_map/ppermute | solution.py:381
  35.6 5.8 %collective-permute-start.17 = (bf16[512,512]{1,0:T(8,128)(2,1)S(1)}, bf16[512,512]{1,0:T(8,128)(2,1)S(1)}, u32[]{:S(2)}, u32[]{:S(2)}) collective-permute-start(bf16[512,512]{1,0:T(8,128)(2,1)S(1)} %collective-permute-done.16.refs_3_), channel_id=1, source_target_pairs={{0,1},{1,0},{2,3},{3,2},{4,5},{5,4},{6,7},{7,6},{8,9},{9,8},{10,11... | collective-permute-start | bytes 1572872 | tf_op jit(solution)/shard_map/ppermute | solution.py:382
  35.6 21.3 %collective-permute-start.8 = (bf16[512,512]{1,0:T(8,128)(2,1)S(1)}, bf16[512,512]{1,0:T(8,128)(2,1)S(1)}, u32[]{:S(2)}, u32[]{:S(2)}) collective-permute-start(bf16[512,512]{1,0:T(8,128)(2,1)S(1)} %get-tuple-element.50), channel_id=1, source_target_pairs={{0,4},{2,6},{4,0},{6,2},{8,12},{10,14},{12,8},{14,10},{16,20},{18,... | collective-permute-start | bytes 1572872 | tf_op jit(solution)/shard_map/ppermute | solution.py:358
  39.3 9.3 %collective-permute-start.10 = (bf16[128,1024]{1,0:T(8,128)(2,1)S(1)}, bf16[128,1024]{1,0:T(8,128)(2,1)S(1)}, u32[]{:S(2)}, u32[]{:S(2)}) collective-permute-start(bf16[128,1024]{1,0:T(8,128)(2,1)S(1)} %get-tuple-element.55), channel_id=1, source_target_pairs={{0,2},{2,0},{4,6},{6,4},{8,10},{10,8},{12,14},{14,12},{16,18},{18,... | collective-permute-start | bytes 786440 | tf_op jit(solution)/shard_map/ppermute | solution.py:405
  40.8 12.1 %collective-permute-start.11 = (bf16[128,1024]{1,0:T(8,128)(2,1)S(1)}, bf16[128,1024]{1,0:T(8,128)(2,1)S(1)}, u32[]{:S(2)}, u32[]{:S(2)}) collective-permute-start(bf16[128,1024]{1,0:T(8,128)(2,1)S(1)} %get-tuple-element.56), channel_id=1, source_target_pairs={{0,2},{2,0},{4,6},{6,4},{8,10},{10,8},{12,14},{14,12},{16,18},{18,... | collective-permute-start | bytes 786440 | tf_op jit(solution)/shard_map/ppermute | solution.py:405
  44.2 17.9 %collective-permute-start.18 = (bf16[256,1024]{1,0:T(8,128)(2,1)S(1)}, bf16[256,1024]{1,0:T(8,128)(2,1)S(1)}, u32[]{:S(2)}, u32[]{:S(2)}) collective-permute-start(bf16[256,1024]{1,0:T(8,128)(2,1)S(1)} %get-tuple-element.59), channel_id=1, source_target_pairs={{0,4},{2,6},{4,0},{6,2},{8,12},{10,14},{12,8},{14,10},{16,20},{18,... | collective-permute-start | bytes 1572872 | tf_op jit(solution)/shard_map/ppermute | solution.py:405
  49.1 12.2 %collective-permute-start.12 = (bf16[128,1024]{1,0:T(8,128)(2,1)S(1)}, bf16[128,1024]{1,0:T(8,128)(2,1)S(1)}, u32[]{:S(2)}, u32[]{:S(2)}) collective-permute-start(bf16[128,1024]{1,0:T(8,128)(2,1)S(1)} %added.6), channel_id=1, source_target_pairs={{0,8},{2,10},{4,12},{6,14},{8,0},{10,2},{12,4},{14,6},{16,24},{18,... | collective-permute-start | bytes 786440 | tf_op jit(solution)/shard_map/ppermute | solution.py:410
  53.6 7.8 %collective-permute-start.13 = (bf16[128,1024]{1,0:T(8,128)(2,1)S(1)}, bf16[128,1024]{1,0:T(8,128)(2,1)S(1)}, u32[]{:S(2)}, u32[]{:S(2)}) collective-permute-start(bf16[128,1024]{1,0:T(8,128)(2,1)S(1)} %added.7), channel_id=1, source_target_pairs={{0,8},{2,10},{4,12},{6,14},{8,0},{10,2},{12,4},{14,6},{16,24},{18,... | collective-permute-start | bytes 786440 | tf_op jit(solution)/shard_map/ppermute | solution.py:410
  55.4 17.0 %collective-permute-start.4 = (bf16[512,512]{1,0:T(8,128)(2,1)S(1)}, bf16[512,512]{1,0:T(8,128)(2,1)S(1)}, u32[]{:S(2)}, u32[]{:S(2)}) collective-permute-start(bf16[512,512]{1,0:T(8,128)(2,1)S(1)} %get-tuple-element.46), channel_id=1, source_target_pairs={{0,4},{2,6},{4,0},{6,2},{8,12},{10,14},{12,8},{14,10},{16,20},{18,... | collective-permute-start | bytes 1572872 | tf_op jit(solution)/shard_map/ppermute | solution.py:358
  59.8 17.1 %collective-permute-start.9 = (bf16[256,1024]{1,0:T(8,128)(2,1)S(1)}, bf16[256,1024]{1,0:T(8,128)(2,1)S(1)}, u32[]{:S(2)}, u32[]{:S(2)}) collective-permute-start(bf16[256,1024]{1,0:T(8,128)(2,1)S(1)} %get-tuple-element.52), channel_id=1, source_target_pairs={{0,2},{2,0},{4,6},{6,4},{8,10},{10,8},{12,14},{14,12},{16,18},{18,... | collective-permute-start | bytes 1572872 | tf_op jit(solution)/shard_map/ppermute | solution.py:405
  62.0 14.8 %collective-permute-start.14 = (bf16[256,1024]{1,0:T(8,128)(2,1)S(1)}, bf16[256,1024]{1,0:T(8,128)(2,1)S(1)}, u32[]{:S(2)}, u32[]{:S(2)}) collective-permute-start(bf16[256,1024]{1,0:T(8,128)(2,1)S(1)} %added.8), channel_id=1, source_target_pairs={{0,1},{1,0},{2,3},{3,2},{4,5},{5,4},{6,7},{7,6},{8,16},{9,17},{10,... | collective-permute-start | bytes 1572872 | tf_op jit(solution)/shard_map/ppermute | solution.py:410
  62.1 33.1 %slice-start = ((s8[8388608]{0:T(1024)(128)(4,1)}), s8[4194304]{0:T(1024)(128)(4,1)S(1)}, s32[]{:S(2)}) async-start(s8[8388608]{0:T(1024)(128)(4,1)} %bitcast.16), calls=%async_computation | async-start | bytes 8388608
  62.8 32.4 %slice-start.1 = ((s8[8388608]{0:T(1024)(128)(4,1)}), s8[4194304]{0:T(1024)(128)(4,1)S(1)}, s32[]{:S(2)}) async-start(s8[8388608]{0:T(1024)(128)(4,1)} %bitcast.16), calls=%async_computation.1 | async-start | bytes 8388608
  62.8 16.4 %collective-permute-start.19 = (bf16[256,1024]{1,0:T(8,128)(2,1)S(1)}, bf16[256,1024]{1,0:T(8,128)(2,1)S(1)}, u32[]{:S(2)}, u32[]{:S(2)}) collective-permute-start(bf16[256,1024]{1,0:T(8,128)(2,1)S(1)} %added.10), channel_id=1, source_target_pairs={{0,8},{2,10},{4,12},{6,14},{8,0},{10,2},{12,4},{14,6},{16,24},{18,... | collective-permute-start | bytes 1572872 | tf_op jit(solution)/shard_map/ppermute | solution.py:410
  75.3 13.6 %collective-permute-start.7 = (bf16[256,1024]{1,0:T(8,128)(2,1)S(1)}, bf16[256,1024]{1,0:T(8,128)(2,1)S(1)}, u32[]{:S(2)}, u32[]{:S(2)}) collective-permute-start(bf16[256,1024]{1,0:T(8,128)(2,1)S(1)} %get-tuple-element.49), channel_id=1, source_target_pairs={{0,2},{2,0},{4,6},{6,4},{8,10},{10,8},{12,14},{14,12},{16,18},{18,... | collective-permute-start | bytes 1572872 | tf_op jit(solution)/shard_map/ppermute | solution.py:405
  77.6 13.3 %collective-permute-start.15 = (bf16[256,1024]{1,0:T(8,128)(2,1)S(1)}, bf16[256,1024]{1,0:T(8,128)(2,1)S(1)}, u32[]{:S(2)}, u32[]{:S(2)}) collective-permute-start(bf16[256,1024]{1,0:T(8,128)(2,1)S(1)} %added.9), channel_id=1, source_target_pairs={{0,8},{2,10},{4,12},{6,14},{8,0},{10,2},{12,4},{14,6},{16,24},{18,... | collective-permute-start | bytes 1572872 | tf_op jit(solution)/shard_map/ppermute | solution.py:410
  79.9 11.0 %collective-permute-start.20 = (bf16[256,1024]{1,0:T(8,128)(2,1)S(1)}, bf16[256,1024]{1,0:T(8,128)(2,1)S(1)}, u32[]{:S(2)}, u32[]{:S(2)}) collective-permute-start(bf16[256,1024]{1,0:T(8,128)(2,1)S(1)} %added.11), channel_id=1, source_target_pairs={{0,1},{1,0},{2,3},{3,2},{4,5},{5,4},{6,7},{7,6},{8,16},{9,17},{10,... | collective-permute-start | bytes 1572872 | tf_op jit(solution)/shard_map/ppermute | solution.py:410
  93.3 1.9 %collective-permute-start.21 = (bf16[256,1024]{1,0:T(8,128)(2,1)S(1)}, bf16[256,1024]{1,0:T(8,128)(2,1)S(1)}, u32[]{:S(2)}, u32[]{:S(2)}) collective-permute-start(bf16[256,1024]{1,0:T(8,128)(2,1)S(1)} %get-tuple-element.62.n_ref), channel_id=1, source_target_pairs={{0,1},{1,0},{2,3},{3,2},{4,5},{5,4},{6,7},{7,6},{8,9},{9,8},{10,11... | collective-permute-start | bytes 1572872 | tf_op jit(solution)/shard_map/ppermute | solution.py:425
  (2 other events, 31.3 us)

commit v6 on v5

--- a/solution.py
+++ b/solution.py
@@ -385,6 +385,7 @@
     keeps, arrivals, now = {}, {}, [place]
 
     def then(result):
+        now[0], _ = lax.optimization_barrier((now[0], result))
         return result
 
     def block(c):
@@ -412,12 +413,14 @@
     both = ("dp", "mp")
     block(0)
     block(1)
-    out1 = [hop(0, at, parts[0], "dp", outer) for at in range(parts[0])]
+    out1 = [hop(0, 0, parts[0], "dp", outer)]
+    out1.append(hop(0, 1, parts[0], "dp", outer))
     block(2)
-    in2 = hop(0, 0, 1, both, inner, [out1])
+    in2 = [hop(0, 0, parts[0], both, inner, [[out1[0]]])]
+    in2.append(hop(0, 1, parts[0], both, inner, [[out1[1]]]))
     out2 = hop(1, 0, 1, "dp", outer)
     block(3)
-    out3 = hop(2, 0, 1, "dp", outer, masked=[[in2]])
+    out3 = hop(2, 0, 1, "dp", outer, masked=[in2])
     in3 = hop(1, 0, 1, both, inner, [[out2]])
     new_first, new_second, normed = moments(
         now[0], [keeps[3], *arrivals[3], out3], in3, moment1, moment2, mid_at, core_at

time: 103 us -> 103 us (level)
  starting transfers between devices: 25.2 us -> 23.3 us
  waiting for transfers between devices: 39.5 us -> 40.8 us
    ppermute x6 -> x7, starting transfers between devices: 8.44 us -> 6.56 us  [hop(): return lax.ppermute(value, axes, pairs)]
    ppermute x4, waiting for transfers between devices: 10.7 us -> 12 us  [raw(): return lax.ppermute(mine, 'dp', along_y if first_y[c] else along_x)]
    pallas_call x6 -> x7, Pallas kernels: 3.92 us -> 4.47 us  [added(): call(kernel, 'added', [shape(rows, ranks, jnp.bfloat16)], [part(rows, ran...]
  transfers between devices with their start and end apart: 22 -> 23, of which waited for: 11 -> 11; matrix products, arithmetic and copies ran while one was open for 0% -> 0% of each run, Pallas kernels for 24% -> 25%
where the time goes in v6:
time: 103 us; the launch traced here: 102 us
  waiting for transfers between devices  40.8 us (40%)
  Pallas kernels  36.8 us (36%)
  starting transfers between devices  23.3 us (23%)
    ppermute x5, waiting for transfers between devices, block(): arrivals[c] = [lax.ppermute(send, 'dp', second) for send in sends]  14 us
    ppermute x4, waiting for transfers between devices, raw(): return lax.ppermute(mine, 'dp', along_y if first_y[c] else along_x)  12 us
    pallas_call x4, Pallas kernels, partial_sums(): call(kernel, 'partial_sums', [shape(rows, 2 * ranks, jnp.bfloat16)] * par...  11.5 us
    ppermute x1, waiting for transfers between devices, staged(): half_y = lax.ppermute(half, 'dp', along_y)  8.95 us
    pallas_call x1, Pallas kernels, rank_halves(): call(kernel, 'rank_halves', [shape(tokens, ranks, jnp.bfloat16), shape(to...  7.61 us
    ppermute x4, starting transfers between devices, raw(): return lax.ppermute(mine, 'dp', along_y if first_y[c] else along_x)  6.83 us
    pallas_call x1, Pallas kernels, update_rows(): call(kernel, 'update_rows', [jax.ShapeDtypeStruct((2, owned, width), jnp....  6.71 us
    ppermute x5, starting transfers between devices, block(): arrivals[c] = [lax.ppermute(send, 'dp', second) for send in sends]  6.6 us
  transfers between devices with their start and end apart: 23, of which 11 were waited for; matrix products, arithmetic and copies ran while one was open for 0% of the time, Pallas kernels for 25%

profile of v6, /device:TPU:0, one launch (start us, length us, event | category | flops | bytes accessed | tf_op | source)
XLA Modules:
  0.0 101.9 jit_solution(18416689800176861314)
XLA Ops:
  0.8 1.8 %take.2 = (bf16[512,512]{1,0:T(8,128)(2,1)S(1)}, bf16[512,512]{1,0:T(8,128)(2,1)S(1)}) custom-call(s32[16]{0:T(128)S(1)} %stack.71.place_ref, bf16[512,4096]{1,0:T(8,128)(2,1)} %ours_ref.7), custom_call_target="tpu_custom_call" | custom-call | bytes 2097152 | tf_op jit(solution)/shard_map/take/pallas_call | solution.py:102
  2.6 3.0 %collective-permute-start = (bf16[512,512]{1,0:T(8,128)(2,1)S(1)}, bf16[512,512]{1,0:T(8,128)(2,1)S(1)}, u32[]{:S(2)}, u32[]{:S(2)}) collective-permute-start(bf16[512,512]{1,0:T(8,128)(2,1)S(1)} %get-tuple-element.49), channel_id=1, source_target_pairs={{0,4},{2,6},{4,0},{6,2},{8,12},{10,14},{12,8},{14,10},{16,20},{18,... | collective-permute-start | bytes 1572872 | tf_op jit(solution)/shard_map/ppermute | solution.py:358
  7.1 7.6 %rank_halves.1 = (bf16[512,512]{1,0:T(8,128)(2,1)S(1)}, f32[512,512]{1,0:T(8,128)S(1)}) custom-call(s32[16]{0:T(128)S(1)} %stack.71.place_ref, bf16[512,4096]{1,0:T(8,128)(2,1)} %a_hbm, bf16[4096,1024]{1,0:T(8,128)(2,1)} %b_ref.1), custom_call_target="tpu_custom_call" | custom-call | flops 4294967296 | bytes 14680064 | tf_op jit(solution)/shard_map/rank_halves/pallas_call | solution.py:149
  14.8 2.8 %collective-permute-done.refs_0_ = bf16[512,512]{1,0:T(8,128)(2,1)S(1)} collective-permute-done((bf16[512,512]{1,0:T(8,128)(2,1)S(1)}, bf16[512,512]{1,0:T(8,128)(2,1)S(1)}, u32[]{:S(2)}, u32[]{:S(2)}) %collective-permute-start) | collective-permute-done | bytes 524320 | tf_op jit(solution)/shard_map/ppermute | solution.py:358
  20.1 1.8 %collective-permute-start.4 = (bf16[512,512]{1,0:T(8,128)(2,1)S(1)}, bf16[512,512]{1,0:T(8,128)(2,1)S(1)}, u32[]{:S(2)}, u32[]{:S(2)}) collective-permute-start(bf16[512,512]{1,0:T(8,128)(2,1)S(1)} %rounded.1.refs_1_), channel_id=1, source_target_pairs={{0,4},{2,6},{4,0},{6,2},{8,12},{10,14},{12,8},{14,10},{16,20},{18,... | collective-permute-start | bytes 1572872 | tf_op jit(solution)/shard_map/ppermute | solution.py:371
  23.4 1.8 %take.3 = (bf16[512,512]{1,0:T(8,128)(2,1)S(1)}, bf16[512,512]{1,0:T(8,128)(2,1)S(1)}) custom-call(s32[16]{0:T(128)S(1)} %stack.71.place_ref, bf16[512,4096]{1,0:T(8,128)(2,1)} %ours_ref.7), custom_call_target="tpu_custom_call" | custom-call | bytes 2097152 | tf_op jit(solution)/shard_map/take/pallas_call | solution.py:102
  25.2 8.9 %collective-permute-done.4.refs_3_ = bf16[512,512]{1,0:T(8,128)(2,1)S(1)} collective-permute-done((bf16[512,512]{1,0:T(8,128)(2,1)S(1)}, bf16[512,512]{1,0:T(8,128)(2,1)S(1)}, u32[]{:S(2)}, u32[]{:S(2)}) %collective-permute-start.4) | collective-permute-done | bytes 524320 | tf_op jit(solution)/shard_map/ppermute | solution.py:371
  36.4 2.9 %partial_sums.4 = (bf16[128,1024]{1,0:T(8,128)(2,1)S(1)}, bf16[128,1024]{1,0:T(8,128)(2,1)S(1)}, f32[256,1024]{1,0:T(8,128)S(1)}) custom-call(s32[16]{0:T(128)S(1)} %stack.71.place_ref, bf16[512,4096]{1,0:T(8,128)(2,1)} %ours_ref.7, bf16[512,4096]{1,0:T(8,128)(2,1)} %ours_ref.7, bf16[512,512]{1,0:T(8,128)(2,1)S(1)} %collective-permute-done.refs_0_, ...), custom_call_target="tpu_custom_call" | custom-call | flops 1073741824 | bytes 4718592 | tf_op jit(solution)/shard_map/partial_sums/pallas_call | solution.py:240
  39.3 1.5 %collective-permute-start.8 = (bf16[128,1024]{1,0:T(8,128)(2,1)S(1)}, bf16[128,1024]{1,0:T(8,128)(2,1)S(1)}, u32[]{:S(2)}, u32[]{:S(2)}) collective-permute-start(bf16[128,1024]{1,0:T(8,128)(2,1)S(1)} %get-tuple-element.59), channel_id=1, source_target_pairs={{0,2},{2,0},{4,6},{6,4},{8,10},{10,8},{12,14},{14,12},{16,18},{18,... | collective-permute-start | bytes 786440 | tf_op jit(solution)/shard_map/ppermute | solution.py:406
  41.4 2.9 %partial_sums.5 = (bf16[256,1024]{1,0:T(8,128)(2,1)S(1)}, f32[256,1024]{1,0:T(8,128)S(1)}) custom-call(s32[16]{0:T(128)S(1)} %stack.71.place_ref, bf16[512,4096]{1,0:T(8,128)(2,1)} %ours_ref.7, bf16[512,4096]{1,0:T(8,128)(2,1)} %ours_ref.7, bf16[512,512]{1,0:T(8,128)(2,1)S(1)} %collective-permute-done.2.refs_0_, bf16[512,512]{1,0:T(8,128)(2,1)S(1)} %rounded.1.refs_1_, ...), custom_call_target="tpu_custom_call" | custom-call | flops 1073741824 | bytes 4718592 | tf_op jit(solution)/shard_map/partial_sums/pallas_call | solution.py:240
  45.7 2.9 %collective-permute-done.8.refs_0_ = bf16[128,1024]{1,0:T(8,128)(2,1)S(1)} collective-permute-done((bf16[128,1024]{1,0:T(8,128)(2,1)S(1)}, bf16[128,1024]{1,0:T(8,128)(2,1)S(1)}, u32[]{:S(2)}, u32[]{:S(2)}) %collective-permute-start.8) | collective-permute-done | bytes 262176 | tf_op jit(solution)/shard_map/ppermute | solution.py:406
  49.1 1.6 %collective-permute-start.11 = (bf16[128,1024]{1,0:T(8,128)(2,1)S(1)}, bf16[128,1024]{1,0:T(8,128)(2,1)S(1)}, u32[]{:S(2)}, u32[]{:S(2)}) collective-permute-start(bf16[128,1024]{1,0:T(8,128)(2,1)S(1)} %added.7), channel_id=1, source_target_pairs={{0,8},{2,10},{4,12},{6,14},{8,0},{10,2},{12,4},{14,6},{16,24},{18,... | collective-permute-start | bytes 786440 | tf_op jit(solution)/shard_map/ppermute | solution.py:411
  50.7 2.2 %collective-permute-done.9.refs_0_ = bf16[128,1024]{1,0:T(8,128)(2,1)S(1)} collective-permute-done((bf16[128,1024]{1,0:T(8,128)(2,1)S(1)}, bf16[128,1024]{1,0:T(8,128)(2,1)S(1)}, u32[]{:S(2)}, u32[]{:S(2)}) %collective-permute-start.9) | collective-permute-done | bytes 262176 | tf_op jit(solution)/shard_map/ppermute | solution.py:406
  53.6 1.9 %collective-permute-start.12 = (bf16[128,1024]{1,0:T(8,128)(2,1)S(1)}, bf16[128,1024]{1,0:T(8,128)(2,1)S(1)}, u32[]{:S(2)}, u32[]{:S(2)}) collective-permute-start(bf16[128,1024]{1,0:T(8,128)(2,1)S(1)} %added.8), channel_id=1, source_target_pairs={{0,8},{2,10},{4,12},{6,14},{8,0},{10,2},{12,4},{14,6},{16,24},{18,... | collective-permute-start | bytes 786440 | tf_op jit(solution)/shard_map/ppermute | solution.py:411
  56.9 2.9 %partial_sums.6 = (bf16[256,1024]{1,0:T(8,128)(2,1)S(1)}, f32[256,1024]{1,0:T(8,128)S(1)}) custom-call(s32[16]{0:T(128)S(1)} %stack.71.place_ref, bf16[512,4096]{1,0:T(8,128)(2,1)} %ours_ref.7, bf16[512,4096]{1,0:T(8,128)(2,1)} %ours_ref.7, bf16[512,512]{1,0:T(8,128)(2,1)S(1)} %collective-permute-done.10.refs_0_, bf16[512,512]{1,0:T(8,128)(2,1)S(1)} %rounded.1.refs_1_, ...), custom_call_target="tpu_custom_call" | custom-call | flops 1073741824 | bytes 4718592 | tf_op jit(solution)/shard_map/partial_sums/pallas_call | solution.py:240
  64.7 7.8 %collective-permute-done.14.refs_0_ = bf16[512,512]{1,0:T(8,128)(2,1)S(1)} collective-permute-done((bf16[512,512]{1,0:T(8,128)(2,1)S(1)}, bf16[512,512]{1,0:T(8,128)(2,1)S(1)}, u32[]{:S(2)}, u32[]{:S(2)}) %collective-permute-start.14) | collective-permute-done | bytes 524320 | tf_op jit(solution)/shard_map/ppermute | solution.py:358
  72.4 2.9 %partial_sums.7 = (bf16[256,1024]{1,0:T(8,128)(2,1)S(1)}, f32[256,1024]{1,0:T(8,128)S(1)}) custom-call(s32[16]{0:T(128)S(1)} %stack.71.place_ref, bf16[512,4096]{1,0:T(8,128)(2,1)} %ours_ref.7, bf16[512,4096]{1,0:T(8,128)(2,1)} %ours_ref.7, bf16[512,512]{1,0:T(8,128)(2,1)S(1)} %collective-permute-done.14.refs_0_, bf16[512,512]{1,0:T(8,128)(2,1)S(1)} %rounded.1.refs_1_, ...), custom_call_target="tpu_custom_call" | custom-call | flops 1073741824 | bytes 4718592 | tf_op jit(solution)/shard_map/partial_sums/pallas_call | solution.py:240
  75.3 1.5 %collective-permute-start.19 = (bf16[256,1024]{1,0:T(8,128)(2,1)S(1)}, bf16[256,1024]{1,0:T(8,128)(2,1)S(1)}, u32[]{:S(2)}, u32[]{:S(2)}) collective-permute-start(bf16[256,1024]{1,0:T(8,128)(2,1)S(1)} %get-tuple-element.77), channel_id=1, source_target_pairs={{0,2},{2,0},{4,6},{6,4},{8,10},{10,8},{12,14},{14,12},{16,18},{18,... | collective-permute-start | bytes 1572872 | tf_op jit(solution)/shard_map/ppermute | solution.py:406
  77.6 1.6 %collective-permute-start.20 = (bf16[256,1024]{1,0:T(8,128)(2,1)S(1)}, bf16[256,1024]{1,0:T(8,128)(2,1)S(1)}, u32[]{:S(2)}, u32[]{:S(2)}) collective-permute-start(bf16[256,1024]{1,0:T(8,128)(2,1)S(1)} %added.12), channel_id=1, source_target_pairs={{0,8},{2,10},{4,12},{6,14},{8,0},{10,2},{12,4},{14,6},{16,24},{18,... | collective-permute-start | bytes 1572872 | tf_op jit(solution)/shard_map/ppermute | solution.py:411
  80.0 8.9 %collective-permute-done.19.refs_1_ = bf16[256,1024]{1,0:T(8,128)(2,1)S(1)} collective-permute-done((bf16[256,1024]{1,0:T(8,128)(2,1)S(1)}, bf16[256,1024]{1,0:T(8,128)(2,1)S(1)}, u32[]{:S(2)}, u32[]{:S(2)}) %collective-permute-start.19) | collective-permute-done | bytes 524320 | tf_op jit(solution)/shard_map/ppermute | solution.py:406
  88.9 2.0 %collective-permute-done.20.refs_2_ = bf16[256,1024]{1,0:T(8,128)(2,1)S(1)} collective-permute-done((bf16[256,1024]{1,0:T(8,128)(2,1)S(1)}, bf16[256,1024]{1,0:T(8,128)(2,1)S(1)}, u32[]{:S(2)}, u32[]{:S(2)}) %collective-permute-start.20) | collective-permute-done | bytes 524320 | tf_op jit(solution)/shard_map/ppermute | solution.py:411
  91.0 2.3 %moments.1 = (f32[256,1024]{1,0:T(8,128)}, f32[256,1024]{1,0:T(8,128)}, bf16[256,1024]{1,0:T(8,128)(2,1)S(1)}) custom-call(s32[16]{0:T(128)S(1)} %stack.71.place_ref, f32[256,1024]{1,0:T(8,128)S(1)} %get-tuple-element.78.refs_0_, bf16[256,1024]{1,0:T(8,128)(2,1)S(1)} %collective-permute-done.19.refs_1_, ...), custom_call_target="tpu_custom_call" | custom-call | flops 5242880 | bytes 7340032 | tf_op jit(solution)/shard_map/moments/pallas_call | solution.py:276
  93.3 1.9 %collective-permute-done.22.m_ref = bf16[256,1024]{1,0:T(8,128)(2,1)S(1)} collective-permute-done((bf16[256,1024]{1,0:T(8,128)(2,1)S(1)}, bf16[256,1024]{1,0:T(8,128)(2,1)S(1)}, u32[]{:S(2)}, u32[]{:S(2)}) %collective-permute-start.22) | collective-permute-done | bytes 524320 | tf_op jit(solution)/shard_map/ppermute | solution.py:428
  95.2 6.7 %update_rows.1 = bf16[2,256,4096]{2,1,0:T(8,128)(2,1)} custom-call(s32[16]{0:T(128)S(1)} %stack.71.place_ref, bf16[256,1024]{1,0:T(8,128)(2,1)S(1)} %get-tuple-element.84.n_ref, bf16[256,1024]{1,0:T(8,128)(2,1)S(1)} %collective-permute-done.22.m_ref, bf16[4096,1024]{1,0:T(8,128)(2,1)S(1)} %bitcast.17), custom_call_target="tpu_custom_call" | custom-call | flops 4294967296 | bytes 13631488 | tf_op jit(solution)/shard_map/update_rows/pallas_call | solution.py:304
  (49 shorter events, 18.9 us)
Async XLA Ops:
  2.6 15.0 %collective-permute-start = (bf16[512,512]{1,0:T(8,128)(2,1)S(1)}, bf16[512,512]{1,0:T(8,128)(2,1)S(1)}, u32[]{:S(2)}, u32[]{:S(2)}) collective-permute-start(bf16[512,512]{1,0:T(8,128)(2,1)S(1)} %get-tuple-element.49), channel_id=1, source_target_pairs={{0,4},{2,6},{4,0},{6,2},{8,12},{10,14},{12,8},{14,10},{16,20},{18,... | collective-permute-start | bytes 1572872 | tf_op jit(solution)/shard_map/ppermute | solution.py:358
  5.6 13.4 %collective-permute-start.2 = (bf16[512,512]{1,0:T(8,128)(2,1)S(1)}, bf16[512,512]{1,0:T(8,128)(2,1)S(1)}, u32[]{:S(2)}, u32[]{:S(2)}) collective-permute-start(bf16[512,512]{1,0:T(8,128)(2,1)S(1)} %get-tuple-element.53), channel_id=1, source_target_pairs={{0,2},{2,0},{4,6},{6,4},{8,10},{10,8},{12,14},{14,12},{16,18},{18,... | collective-permute-start | bytes 1572872 | tf_op jit(solution)/shard_map/ppermute | solution.py:358
  17.6 1.9 %collective-permute-start.1 = (bf16[512,512]{1,0:T(8,128)(2,1)S(1)}, bf16[512,512]{1,0:T(8,128)(2,1)S(1)}, u32[]{:S(2)}, u32[]{:S(2)}) collective-permute-start(bf16[512,512]{1,0:T(8,128)(2,1)S(1)} %get-tuple-element.52), channel_id=1, source_target_pairs={{0,1},{1,0},{2,3},{3,2},{4,5},{5,4},{6,7},{7,6},{8,9},{9,8},{10,11... | collective-permute-start | bytes 1572872 | tf_op jit(solution)/shard_map/ppermute | solution.py:368
  20.1 14.0 %collective-permute-start.4 = (bf16[512,512]{1,0:T(8,128)(2,1)S(1)}, bf16[512,512]{1,0:T(8,128)(2,1)S(1)}, u32[]{:S(2)}, u32[]{:S(2)}) collective-permute-start(bf16[512,512]{1,0:T(8,128)(2,1)S(1)} %rounded.1.refs_1_), channel_id=1, source_target_pairs={{0,4},{2,6},{4,0},{6,2},{8,12},{10,14},{12,8},{14,10},{16,20},{18,... | collective-permute-start | bytes 1572872 | tf_op jit(solution)/shard_map/ppermute | solution.py:371
  21.9 13.7 %collective-permute-start.6 = (bf16[512,512]{1,0:T(8,128)(2,1)S(1)}, bf16[512,512]{1,0:T(8,128)(2,1)S(1)}, u32[]{:S(2)}, u32[]{:S(2)}) collective-permute-start(bf16[512,512]{1,0:T(8,128)(2,1)S(1)} %rounded.1.refs_1_), channel_id=1, source_target_pairs={{0,2},{2,0},{4,6},{6,4},{8,10},{10,8},{12,14},{14,12},{16,18},{18,... | collective-permute-start | bytes 1572872 | tf_op jit(solution)/shard_map/ppermute | solution.py:372
  23.4 13.0 %collective-permute-start.3 = (bf16[512,512]{1,0:T(8,128)(2,1)S(1)}, bf16[512,512]{1,0:T(8,128)(2,1)S(1)}, u32[]{:S(2)}, u32[]{:S(2)}) collective-permute-start(bf16[512,512]{1,0:T(8,128)(2,1)S(1)} %rounded.1.refs_1_), channel_id=1, source_target_pairs={{0,1},{1,0},{2,3},{3,2},{4,5},{5,4},{6,7},{7,6},{8,9},{9,8},{10,11... | collective-permute-start | bytes 1572872 | tf_op jit(solution)/shard_map/ppermute | solution.py:373
  34.1 2.3 %collective-permute-start.5 = (bf16[512,512]{1,0:T(8,128)(2,1)S(1)}, bf16[512,512]{1,0:T(8,128)(2,1)S(1)}, u32[]{:S(2)}, u32[]{:S(2)}) collective-permute-start(bf16[512,512]{1,0:T(8,128)(2,1)S(1)} %collective-permute-done.4.refs_3_), channel_id=1, source_target_pairs={{0,1},{1,0},{2,3},{3,2},{4,5},{5,4},{6,7},{7,6},{8,9},{9,8},{10,11... | collective-permute-start | bytes 1572872 | tf_op jit(solution)/shard_map/ppermute | solution.py:381
  35.6 5.8 %collective-permute-start.7 = (bf16[512,512]{1,0:T(8,128)(2,1)S(1)}, bf16[512,512]{1,0:T(8,128)(2,1)S(1)}, u32[]{:S(2)}, u32[]{:S(2)}) collective-permute-start(bf16[512,512]{1,0:T(8,128)(2,1)S(1)} %collective-permute-done.6.refs_3_), channel_id=1, source_target_pairs={{0,1},{1,0},{2,3},{3,2},{4,5},{5,4},{6,7},{7,6},{8,9},{9,8},{10,11... | collective-permute-start | bytes 1572872 | tf_op jit(solution)/shard_map/ppermute | solution.py:382
  35.6 21.3 %collective-permute-start.10 = (bf16[512,512]{1,0:T(8,128)(2,1)S(1)}, bf16[512,512]{1,0:T(8,128)(2,1)S(1)}, u32[]{:S(2)}, u32[]{:S(2)}) collective-permute-start(bf16[512,512]{1,0:T(8,128)(2,1)S(1)} %get-tuple-element.69), channel_id=1, source_target_pairs={{0,4},{2,6},{4,0},{6,2},{8,12},{10,14},{12,8},{14,10},{16,20},{18,... | collective-permute-start | bytes 1572872 | tf_op jit(solution)/shard_map/ppermute | solution.py:358
  39.3 9.3 %collective-permute-start.8 = (bf16[128,1024]{1,0:T(8,128)(2,1)S(1)}, bf16[128,1024]{1,0:T(8,128)(2,1)S(1)}, u32[]{:S(2)}, u32[]{:S(2)}) collective-permute-start(bf16[128,1024]{1,0:T(8,128)(2,1)S(1)} %get-tuple-element.59), channel_id=1, source_target_pairs={{0,2},{2,0},{4,6},{6,4},{8,10},{10,8},{12,14},{14,12},{16,18},{18,... | collective-permute-start | bytes 786440 | tf_op jit(solution)/shard_map/ppermute | solution.py:406
  40.8 12.1 %collective-permute-start.9 = (bf16[128,1024]{1,0:T(8,128)(2,1)S(1)}, bf16[128,1024]{1,0:T(8,128)(2,1)S(1)}, u32[]{:S(2)}, u32[]{:S(2)}) collective-permute-start(bf16[128,1024]{1,0:T(8,128)(2,1)S(1)} %get-tuple-element.60), channel_id=1, source_target_pairs={{0,2},{2,0},{4,6},{6,4},{8,10},{10,8},{12,14},{14,12},{16,18},{18,... | collective-permute-start | bytes 786440 | tf_op jit(solution)/shard_map/ppermute | solution.py:406
  44.2 18.4 %collective-permute-start.13 = (bf16[256,1024]{1,0:T(8,128)(2,1)S(1)}, bf16[256,1024]{1,0:T(8,128)(2,1)S(1)}, u32[]{:S(2)}, u32[]{:S(2)}) collective-permute-start(bf16[256,1024]{1,0:T(8,128)(2,1)S(1)} %get-tuple-element.64), channel_id=1, source_target_pairs={{0,4},{2,6},{4,0},{6,2},{8,12},{10,14},{12,8},{14,10},{16,20},{18,... | collective-permute-start | bytes 1572872 | tf_op jit(solution)/shard_map/ppermute | solution.py:406
  49.1 12.2 %collective-permute-start.11 = (bf16[128,1024]{1,0:T(8,128)(2,1)S(1)}, bf16[128,1024]{1,0:T(8,128)(2,1)S(1)}, u32[]{:S(2)}, u32[]{:S(2)}) collective-permute-start(bf16[128,1024]{1,0:T(8,128)(2,1)S(1)} %added.7), channel_id=1, source_target_pairs={{0,8},{2,10},{4,12},{6,14},{8,0},{10,2},{12,4},{14,6},{16,24},{18,... | collective-permute-start | bytes 786440 | tf_op jit(solution)/shard_map/ppermute | solution.py:411
  53.6 8.4 %collective-permute-start.12 = (bf16[128,1024]{1,0:T(8,128)(2,1)S(1)}, bf16[128,1024]{1,0:T(8,128)(2,1)S(1)}, u32[]{:S(2)}, u32[]{:S(2)}) collective-permute-start(bf16[128,1024]{1,0:T(8,128)(2,1)S(1)} %added.8), channel_id=1, source_target_pairs={{0,8},{2,10},{4,12},{6,14},{8,0},{10,2},{12,4},{14,6},{16,24},{18,... | collective-permute-start | bytes 786440 | tf_op jit(solution)/shard_map/ppermute | solution.py:411
  55.4 17.0 %collective-permute-start.14 = (bf16[512,512]{1,0:T(8,128)(2,1)S(1)}, bf16[512,512]{1,0:T(8,128)(2,1)S(1)}, u32[]{:S(2)}, u32[]{:S(2)}) collective-permute-start(bf16[512,512]{1,0:T(8,128)(2,1)S(1)} %get-tuple-element.76), channel_id=1, source_target_pairs={{0,4},{2,6},{4,0},{6,2},{8,12},{10,14},{12,8},{14,10},{16,20},{18,... | collective-permute-start | bytes 1572872 | tf_op jit(solution)/shard_map/ppermute | solution.py:358
  59.8 17.1 %collective-permute-start.15 = (bf16[256,1024]{1,0:T(8,128)(2,1)S(1)}, bf16[256,1024]{1,0:T(8,128)(2,1)S(1)}, u32[]{:S(2)}, u32[]{:S(2)}) collective-permute-start(bf16[256,1024]{1,0:T(8,128)(2,1)S(1)} %get-tuple-element.70), channel_id=1, source_target_pairs={{0,2},{2,0},{4,6},{6,4},{8,10},{10,8},{12,14},{14,12},{16,18},{18,... | collective-permute-start | bytes 1572872 | tf_op jit(solution)/shard_map/ppermute | solution.py:406
  62.6 32.6 %slice-start = ((s8[8388608]{0:T(1024)(128)(4,1)}), s8[4194304]{0:T(1024)(128)(4,1)S(1)}, s32[]{:S(2)}) async-start(s8[8388608]{0:T(1024)(128)(4,1)} %bitcast.16), calls=%async_computation | async-start | bytes 8388608
  63.3 16.0 %collective-permute-start.18 = (bf16[256,1024]{1,0:T(8,128)(2,1)S(1)}, bf16[256,1024]{1,0:T(8,128)(2,1)S(1)}, u32[]{:S(2)}, u32[]{:S(2)}) collective-permute-start(bf16[256,1024]{1,0:T(8,128)(2,1)S(1)} %added.11), channel_id=1, source_target_pairs={{0,8},{2,10},{4,12},{6,14},{8,0},{10,2},{12,4},{14,6},{16,24},{18,... | collective-permute-start | bytes 1572872 | tf_op jit(solution)/shard_map/ppermute | solution.py:411
  64.1 12.7 %collective-permute-start.17 = (bf16[128,1024]{1,0:T(8,128)(2,1)S(1)}, bf16[128,1024]{1,0:T(8,128)(2,1)S(1)}, u32[]{:S(2)}, u32[]{:S(2)}) collective-permute-start(bf16[128,1024]{1,0:T(8,128)(2,1)S(1)} %added.10), channel_id=1, source_target_pairs={{0,1},{1,0},{2,3},{3,2},{4,5},{5,4},{6,7},{7,6},{8,16},{9,17},{10,... | collective-permute-start | bytes 786440 | tf_op jit(solution)/shard_map/ppermute | solution.py:411
  64.1 12.7 %collective-permute-start.16 = (bf16[128,1024]{1,0:T(8,128)(2,1)S(1)}, bf16[128,1024]{1,0:T(8,128)(2,1)S(1)}, u32[]{:S(2)}, u32[]{:S(2)}) collective-permute-start(bf16[128,1024]{1,0:T(8,128)(2,1)S(1)} %added.9), channel_id=1, source_target_pairs={{0,1},{1,0},{2,3},{3,2},{4,5},{5,4},{6,7},{7,6},{8,16},{9,17},{10,... | collective-permute-start | bytes 786440 | tf_op jit(solution)/shard_map/ppermute | solution.py:411
  75.3 13.6 %collective-permute-start.19 = (bf16[256,1024]{1,0:T(8,128)(2,1)S(1)}, bf16[256,1024]{1,0:T(8,128)(2,1)S(1)}, u32[]{:S(2)}, u32[]{:S(2)}) collective-permute-start(bf16[256,1024]{1,0:T(8,128)(2,1)S(1)} %get-tuple-element.77), channel_id=1, source_target_pairs={{0,2},{2,0},{4,6},{6,4},{8,10},{10,8},{12,14},{14,12},{16,18},{18,... | collective-permute-start | bytes 1572872 | tf_op jit(solution)/shard_map/ppermute | solution.py:406
  77.6 13.3 %collective-permute-start.20 = (bf16[256,1024]{1,0:T(8,128)(2,1)S(1)}, bf16[256,1024]{1,0:T(8,128)(2,1)S(1)}, u32[]{:S(2)}, u32[]{:S(2)}) collective-permute-start(bf16[256,1024]{1,0:T(8,128)(2,1)S(1)} %added.12), channel_id=1, source_target_pairs={{0,8},{2,10},{4,12},{6,14},{8,0},{10,2},{12,4},{14,6},{16,24},{18,... | collective-permute-start | bytes 1572872 | tf_op jit(solution)/shard_map/ppermute | solution.py:411
  80.0 11.0 %collective-permute-start.21 = (bf16[256,1024]{1,0:T(8,128)(2,1)S(1)}, bf16[256,1024]{1,0:T(8,128)(2,1)S(1)}, u32[]{:S(2)}, u32[]{:S(2)}) collective-permute-start(bf16[256,1024]{1,0:T(8,128)(2,1)S(1)} %added.13), channel_id=1, source_target_pairs={{0,1},{1,0},{2,3},{3,2},{4,5},{5,4},{6,7},{7,6},{8,16},{9,17},{10,... | collective-permute-start | bytes 1572872 | tf_op jit(solution)/shard_map/ppermute | solution.py:411
  93.3 1.9 %collective-permute-start.22 = (bf16[256,1024]{1,0:T(8,128)(2,1)S(1)}, bf16[256,1024]{1,0:T(8,128)(2,1)S(1)}, u32[]{:S(2)}, u32[]{:S(2)}) collective-permute-start(bf16[256,1024]{1,0:T(8,128)(2,1)S(1)} %get-tuple-element.84.n_ref), channel_id=1, source_target_pairs={{0,1},{1,0},{2,3},{3,2},{4,5},{5,4},{6,7},{7,6},{8,9},{9,8},{10,11... | collective-permute-start | bytes 1572872 | tf_op jit(solution)/shard_map/ppermute | solution.py:428
  (3 other events, 63.3 us)
